TPU v7x, 32 devices: a whole 2x2x4 slice. The times are simulated.
32 devices in a mesh: group: 2 (over x), pos: 16 (over z, y, core).
Axes of the slice: x: 2, y: 2, z: 4, core: 2. Of those that a mesh axis runs over, the one named last changes fastest.
Arguments:
- acts: bfloat16 [4, 1024, 1536], P('group', 'pos'), parts along dimension 0, may hold values from -12 to 12
- skips: bfloat16 [4, 2048, 1280], P('group', 'pos'), parts along dimension 0, may hold values from -6 to 6
- norm_gain: float32 [1536], replicated, may hold values from 0.6 to 1.6
- w_query: bfloat16 [1536, 256], replicated, may hold values from -4 to 4
- w_key: bfloat16 [1536, 256], replicated, may hold values from -4 to 4
- w_value: bfloat16 [1536, 768], replicated, may hold values from -0.15625 to 0.15625
- w_out: bfloat16 [768, 1536], replicated, may hold values from -0.21875 to 0.21875
- w_lift: bfloat16 [1536, 1536], P('pos'), may hold values from -0.15625 to 0.15625
- w_skip: bfloat16 [1280, 1536], P('pos'), may hold values from -0.15625 to 0.15625
- depth_kernel: float32 [3, 1536], replicated, may hold values from -3 to 3
- w_point: bfloat16 [1536, 1536], P(None, 'pos'), may hold values from -0.15625 to 0.15625
Outputs:
- decoded: bfloat16 [4, 2048, 1536], P('group', 'pos'), parts along dimension 0
There are 2 independent parts, one for each index of `group`. A program takes and returns all parts, laid end to end along the dimension named above; an argument that names none is the same for every part. Nothing has to cross between parts.
All inputs are finite; a program needn't handle non-finite values.
Results may differ from a plain program's by a relative error of at most 0.014.
Values may be sent and summed in bfloat16 or wider, within the bound.
No kernel may reach another device: no remote copies, remote signals or barrier semaphores. Data moves between devices by JAX's collectives and lax.ppermute only.
A program may use at most 128 MiB of HBM per device.

v0:
```python
import jax
import jax.numpy as jnp
from jax import lax
from jax.sharding import PartitionSpec as P

HEADS = 4
HK = 64
HV = 192


def extended(cells, sides, width):
    for axis, dim in sides:
        count = lax.axis_size(axis)
        ends = count - 1
        head = lax.slice_in_dim(cells, 0, width, axis=dim)
        tail = lax.slice_in_dim(cells, cells.shape[dim] - width, cells.shape[dim], axis=dim)
        cells = jnp.concatenate(
            [
                lax.ppermute(tail, axis, [(i, (i + 1) % count) for i in range(ends)]),
                cells,
                lax.ppermute(head, axis, [((i + 1) % count, i) for i in range(ends)]),
            ],
            axis=dim,
        )
    return cells


def on_device(
    acts, skips, norm_gain, w_query, w_key, w_value, w_out, w_lift, w_skip, depth_kernel, w_point
):
    lift_full, skip_full, point_full = (
        lax.all_gather(w_lift, "pos", axis=0, tiled=True),
        lax.all_gather(w_skip, "pos", axis=0, tiled=True),
        lax.all_gather(w_point, "pos", axis=1, tiled=True),
    )
    seq_count, bin_rows, width = acts.shape
    actsf = acts.astype(jnp.float32)
    centre = actsf - jnp.mean(actsf, axis=-1, keepdims=True)
    normed = (
        centre * lax.rsqrt(jnp.mean(centre * centre, axis=-1, keepdims=True) + 1e-05) * norm_gain
    ).astype(jnp.bfloat16)
    flat = normed.reshape(seq_count * bin_rows, width)
    queries = (
        (jnp.dot(flat, w_query, preferred_element_type=jnp.float32) * HK ** (-0.5))
        .astype(jnp.bfloat16)
        .reshape(seq_count, bin_rows, HEADS, HK)
    )
    keys_here = (
        jnp.dot(flat, w_key, preferred_element_type=jnp.float32)
        .astype(jnp.bfloat16)
        .reshape(seq_count, bin_rows, HEADS * HK)
    )
    values_here = (
        jnp.dot(flat, w_value, preferred_element_type=jnp.float32)
        .astype(jnp.bfloat16)
        .reshape(seq_count, bin_rows, HEADS * HV)
    )
    running = jnp.full((seq_count, HEADS, bin_rows), -1e30, jnp.float32)
    key_piece = lax.all_gather(keys_here, "pos", axis=1, tiled=True)
    value_piece = lax.all_gather(values_here, "pos", axis=1, tiled=True)
    count = key_piece.shape[1]
    keyed = key_piece.reshape(seq_count, count, HEADS, HK)
    valued = value_piece.reshape(seq_count, count, HEADS, HV)
    scores = jnp.einsum("sqhd,skhd->shqk", queries, keyed, preferred_element_type=jnp.float32)
    newest = jnp.maximum(running, jnp.max(scores, axis=-1))
    weights = jnp.exp(scores - newest[..., None])
    totals = jnp.sum(weights, axis=-1)
    summed = jnp.einsum(
        "shqk,skhv->shqv", weights.astype(jnp.bfloat16), valued, preferred_element_type=jnp.float32
    )
    running, totals, summed = (newest, totals, summed)
    mixed = (
        (summed / totals[..., None])
        .transpose(0, 2, 1, 3)
        .reshape(seq_count * bin_rows, HEADS * HV)
        .astype(jnp.bfloat16)
    )
    attended = (
        actsf.reshape(seq_count * bin_rows, width)
        + jnp.dot(mixed, w_out, preferred_element_type=jnp.float32)
    ).astype(jnp.bfloat16)
    activated = jax.nn.gelu(attended.astype(jnp.float32)).astype(jnp.bfloat16)
    lifted = jnp.dot(activated, lift_full, preferred_element_type=jnp.float32)
    lifted = lifted.astype(jnp.bfloat16).reshape(seq_count, bin_rows, width)
    raised = jnp.repeat(lifted, 2, axis=1).reshape(seq_count * 2 * bin_rows, width)
    skip_act = (
        jax.nn.gelu(skips.astype(jnp.float32))
        .astype(jnp.bfloat16)
        .reshape(seq_count * 2 * bin_rows, skips.shape[2])
    )
    skip_term = jnp.dot(skip_act, skip_full, preferred_element_type=jnp.float32)
    merged = (
        (raised.astype(jnp.float32) + skip_term)
        .astype(jnp.bfloat16)
        .reshape(seq_count, 2 * bin_rows, width)
    )
    padded = extended(merged, (("pos", 1),), 1)
    paddedf = padded.astype(jnp.float32)
    spread = (
        depth_kernel[0] * paddedf[:, :-2]
        + depth_kernel[1] * paddedf[:, 1:-1]
        + depth_kernel[2] * paddedf[:, 2:]
    ).astype(jnp.bfloat16)
    spread = spread.reshape(seq_count * 2 * bin_rows, width)
    decoded = jnp.dot(spread, point_full, preferred_element_type=jnp.float32)
    return decoded.astype(jnp.bfloat16).reshape(seq_count, 2 * bin_rows, width)


def solution(mesh):
    return jax.shard_map(
        on_device,
        mesh=mesh,
        in_specs=(
            P("group", "pos", None),
            P("group", "pos", None),
            P(),
            P(),
            P(),
            P(),
            P(),
            P("pos", None),
            P("pos", None),
            P(),
            P(None, "pos"),
        ),
        out_specs=P("group", "pos", None),
        check_vma=False,
    )
```

profile of v0, /device:TPU:0, one launch (start us, length us, event | category | flops | bytes accessed | tf_op | source)
XLA Modules:
  0.0 268.4 jit_solution(8063212985456525454)
XLA Ops:
  6.5 0.0 copy-start
  6.5 0.0 copy-start.3
  6.5 0.0 all-gather.6.cloned.1.call-start
  6.5 1.3 convert_reduce_fusion
  7.8 1.3 multiply_reduce_fusion
  9.1 1.3 multiply_convert_fusion
  10.4 0.0 copy-done.3
  10.4 0.9 convolution_convert_fusion.3
  11.3 0.0 all-gather.6.cloned.1.call-update
  11.3 0.0 copy-start.4
  11.3 0.0 all-gather.8.cloned.1.call-start
  11.4 2.9 %convolution_convert_fusion.2 = bf16[128,768]{1,0:T(8,128)(2,1)} fusion(bf16[128,1536]{1,0:T(8,128)(2,1)S(1)} %bitcast.36, bf16[1536,768]{1,0:T(8,128)(2,1)} %param.16), kind=kOutput, calls=%fused_computation.30 | convolution fusion | flops 302088192 | bytes 2949120 | tf_op jit(solution)/shard_map/dot_general | solution.py:54
  14.3 0.0 all-gather.8.cloned.1.call-update
  14.3 0.0 all-gather.10.cloned.1.call-start
  14.3 0.7 all-gather.10.cloned.1.call-update
  15.0 0.0 all-gather.12.cloned.1.call-start
  15.1 0.5 all-gather.12.cloned.1.call-update
  15.6 0.0 all-gather.14.cloned.1.call-start
  15.6 0.5 all-gather.14.cloned.1.call-update
  16.2 0.0 copy-done.4
  16.2 0.9 fusion.16
  17.1 1.0 reshape.61
  18.1 2.4 fusion.13
  20.4 31.7 %all-gather.6.cloned.1.call-done = bf16[2,1024,256]{2,1,0:T(8,128)(2,1)} async-done(((bf16[2,64,256]{2,1,0:T(8,128)(2,1)}), bf16[2,1024,256]{2,1,0:T(8,128)(2,1)}) %all-gather.6.cloned.1.call-update) | async-done | bytes 1048592 | tf_op jit(solution)/shard_map/all_gather | solution.py:59
  52.1 1.5 copy.15
  53.6 0.5 fusion.38
  54.1 0.0 copy-start.1
  54.1 1.3 copy-done.1
  55.5 0.5 fusion.3
  56.0 42.6 %all-gather.8.cloned.1.call-done = bf16[2,1024,768]{2,1,0:T(8,128)(2,1)} async-done(((bf16[2,64,768]{2,1,0:T(8,128)(2,1)}), bf16[2,1024,768]{2,1,0:T(8,128)(2,1)}) %all-gather.8.cloned.1.call-update) | async-done | bytes 3145744 | tf_op jit(solution)/shard_map/all_gather | solution.py:60
  98.6 4.6 %copy.17 = bf16[2,1024,768]{1,2,0:T(8,128)(2,1)} copy(bf16[2,1024,768]{2,1,0:T(8,128)(2,1)} %all-gather.8.cloned.1.call-done) | data formatting | bytes 6291456 | tf_op jit(solution)/shard_map/all_gather | solution.py:60
  103.2 0.0 copy-start.2
  103.2 3.7 %fusion.15 = bf16[2,64,4,192]{3,1,2,0:T(8,128)(2,1)S(1)} fusion(bf16[2,1024,4,192]{1,3,2,0:T(8,128)(2,1)} %bitcast.40, f32[2,4,64,1024]{3,2,1,0:T(8,128)} %copy-done.1, f32[2,4,64]{2,1,0:T(4,128)S(1)} %broadcast_maximum_fusion, f32[2,64,4]{1,2,0:T(4,128)S(1)} %bitcast.48), kind=kOutput, calls=%fused_computation.28 | convolution fusion | flops 202571776 | bytes 5443584 | tf_op jit(solution)/shard_map/shqk,skhv->shqv/dot_general | solution.py:68
  106.9 0.2 copy.18
  107.2 0.2 convert_element_type.71
  107.4 45.7 %all-gather.10.cloned.1.call-done = bf16[1536,1536]{1,0:T(8,128)(2,1)} async-done(((bf16[96,1536]{1,0:T(8,128)(2,1)}), bf16[1536,1536]{1,0:T(8,128)(2,1)}) %all-gather.10.cloned.1.call-update) | async-done | bytes 4718608 | tf_op jit(solution)/shard_map/all_gather | solution.py:32
  153.1 0.0 copy-done
  153.1 0.0 copy-done.2
  153.1 3.7 %convolution_convert_fusion.1 = bf16[128,1536]{1,0:T(8,128)(2,1)S(1)} fusion(bf16[1536,1536]{1,0:T(8,128)(2,1)} %all-gather.10.cloned.1.call-done, bf16[128,768]{1,0:T(8,128)(2,1)S(1)} %convert_element_type.71, bf16[768,1536]{1,0:T(8,128)(2,1)S(1)} %copy-done, bf16[128,1536]{1,0:T(8,128)(2,1)S(1)} %bitcast.39), kind=kOutput, calls=%fused_computation.6 | convolution fusion | flops 908722176 | bytes 8060928 | tf_op jit(solution)/shard_map/dot_general | solution.py:83
  156.8 1.6 broadcast_in_dim.5
  158.3 0.0 copy-start.5
  158.3 3.2 %convert_element_type.78 = f32[256,1536]{1,0:T(8,128)} reshape(f32[2,64,2,1536]{3,2,1,0:T(2,128)} %broadcast_in_dim.5) | data formatting | bytes 3145728 | tf_op jit(solution)/shard_map/convert_element_type | solution.py:93
  161.5 41.0 %all-gather.12.cloned.1.call-done = bf16[1280,1536]{1,0:T(8,128)(2,1)} async-done(((bf16[80,1536]{1,0:T(8,128)(2,1)}), bf16[1280,1536]{1,0:T(8,128)(2,1)}) %all-gather.12.cloned.1.call-update) | async-done | bytes 3932176 | tf_op jit(solution)/shard_map/all_gather | solution.py:33
  202.6 0.0 copy-done.5
  202.6 0.0 copy-start.6
  202.6 3.8 %fusion = bf16[256,1536]{1,0:T(8,128)(2,1)S(1)} fusion(f32[256,1536]{1,0:T(8,128)} %convert_element_type.78, bf16[256,1280]{1,0:T(8,128)(2,1)S(1)} %bitcast.45, bf16[1280,1536]{1,0:T(8,128)(2,1)} %all-gather.12.cloned.1.call-done), kind=kOutput, calls=%fused_computation.1 | convolution fusion | flops 1007419392 | bytes 6946816 | tf_op jit(solution)/shard_map/dot_general | solution.py:91
  206.4 2.2 collective-permute-start
  208.6 1.3 collective-permute-start.1
  209.9 0.0 copy-done.6
  209.9 0.1 slice_reduce_fusion.2
  209.9 0.0 collective-permute-done
  210.0 1.7 collective-permute-done.1
  211.7 0.2 maximum_convert_fusion
  211.9 0.5 fusion.6
  212.4 44.8 %all-gather.14.cloned.1.call-done = bf16[1536,1536]{0,1:T(8,128)(2,1)} async-done(((bf16[1536,96]{0,1:T(8,128)(2,1)}), bf16[1536,1536]{0,1:T(8,128)(2,1)}) %all-gather.14.cloned.1.call-update) | async-done | bytes 4718608 | tf_op jit(solution)/shard_map/all_gather | solution.py:34
  257.2 4.6 %convolution_convert_fusion = bf16[256,1536]{1,0:T(8,128)(2,1)} fusion(bf16[256,1536]{1,0:T(8,128)(2,1)S(1)} %bitcast.44, bf16[1536,1536]{0,1:T(8,128)(2,1)} %all-gather.14.cloned.1.call-done), kind=kOutput, calls=%fused_computation.2 | convolution fusion | flops 1208352768 | bytes 6291456 | tf_op jit(solution)/shard_map/dot_general | solution.py:105
  (4 shorter events, 0.0 us)
Async XLA Ops:
  6.5 146.6 %copy-start = (bf16[768,1536]{1,0:T(8,128)(2,1)S(1)}, bf16[768,1536]{1,0:T(8,128)(2,1)}, u32[]{:S(2)}) copy-start(bf16[768,1536]{1,0:T(8,128)(2,1)} %param.17) | copy-start | bytes 7077892
  6.5 3.8 %copy-start.3 = (bf16[1536,256]{1,0:T(8,128)(2,1)S(1)}, bf16[1536,256]{1,0:T(8,128)(2,1)}, u32[]{:S(2)}) copy-start(bf16[1536,256]{1,0:T(8,128)(2,1)} %param.15) | copy-start | bytes 2359300
  6.5 45.6 %all-gather.6.cloned.1.call-start = ((), (), s32[]{:S(2)}) async-start(), calls=%async_computation | async-start | bytes 1114112 | tf_op jit(solution)/shard_map/all_gather | solution.py:59
  11.3 4.9 %copy-start.4 = (bf16[1536,256]{1,0:T(8,128)(2,1)S(1)}, bf16[1536,256]{1,0:T(8,128)(2,1)}, u32[]{:S(2)}) copy-start(bf16[1536,256]{1,0:T(8,128)(2,1)} %param.14) | copy-start | bytes 2359300
  11.3 87.3 %all-gather.8.cloned.1.call-start = ((), (), s32[]{:S(2)}) async-start(), calls=%async_computation.1 | async-start | bytes 3342336 | tf_op jit(solution)/shard_map/all_gather | solution.py:60
  14.3 138.8 %all-gather.10.cloned.1.call-start = ((), (), s32[]{:S(2)}) async-start(), calls=%async_computation.2 | async-start | bytes 5013504 | tf_op jit(solution)/shard_map/all_gather | solution.py:32
  15.0 187.6 %all-gather.12.cloned.1.call-start = ((), (), s32[]{:S(2)}) async-start(), calls=%async_computation.3 | async-start | bytes 4177920 | tf_op jit(solution)/shard_map/all_gather | solution.py:33
  15.6 241.7 %all-gather.14.cloned.1.call-start = ((), (), s32[]{:S(2)}) async-start(), calls=%async_computation.4 | async-start | bytes 5013504 | tf_op jit(solution)/shard_map/all_gather | solution.py:34
  54.1 1.4 copy-start.1
  103.2 49.9 %copy-start.2 = (bf16[2,64,1536]{2,1,0:T(8,128)(2,1)S(1)}, bf16[2,64,1536]{2,1,0:T(8,128)(2,1)}, u32[]{:S(2)}) copy-start(bf16[2,64,1536]{2,1,0:T(8,128)(2,1)} %param.11) | copy-start | bytes 1179652
  158.3 44.3 %copy-start.5 = (bf16[2,128,1280]{2,1,0:T(8,128)(2,1)S(1)}, bf16[2,128,1280]{2,1,0:T(8,128)(2,1)}, u32[]{:S(2)}) copy-start(bf16[2,128,1280]{2,1,0:T(8,128)(2,1)} %fusion.13) | copy-start | bytes 1966084
  202.6 7.3 %copy-start.6 = (f32[3,1536]{1,0:T(4,128)S(1)}, f32[3,1536]{1,0:T(4,128)}, u32[]{:S(2)}) copy-start(f32[3,1536]{1,0:T(4,128)} %param.20) | copy-start | bytes 55300
  206.4 3.5 %collective-permute-start = (bf16[2,1,1536]{2,1,0:T(2,128)(2,1)S(1)}, bf16[2,1,1536]{2,1,0:T(2,128)(2,1)S(1)}, u32[]{:S(2)}, u32[]{:S(2)}) collective-permute-start(bf16[2,1,1536]{2,1,0:T(2,128)(2,1)S(1)} %get-tuple-element.8), channel_id=1, source_target_pairs={{0,1},{1,2},{2,3},{3,4},{4,5},{5,6},{6,7},{7,8},{8,9},{9,10},{10,1... | collective-permute-start | bytes 18440 | tf_op jit(solution)/shard_map/ppermute | solution.py:19
  208.6 3.1 %collective-permute-start.1 = (bf16[2,1,1536]{2,1,0:T(2,128)(2,1)S(1)}, bf16[2,1,1536]{2,1,0:T(2,128)(2,1)S(1)}, u32[]{:S(2)}, u32[]{:S(2)}) collective-permute-start(bf16[2,1,1536]{2,1,0:T(2,128)(2,1)S(1)} %get-tuple-element.9), channel_id=1, source_target_pairs={{1,0},{2,1},{3,2},{4,3},{5,4},{6,5},{7,6},{8,7},{9,8},{10,9},{11,1... | collective-permute-start | bytes 18440 | tf_op jit(solution)/shard_map/ppermute | solution.py:21
Sparse Core Ops, SparseCore 0:
  11.4 40.6 all-gather.5
  54.4 44.1 all-gather.7
  100.9 52.1 all-gather.9
  155.2 47.3 all-gather.11
  204.7 52.4 all-gather.13
where the time goes:
time: 269 us; the launch traced here: 268 us
  waiting for transfers between devices  209 us (78%)
  matrix products  21 us (8%)
  local copies, waits for them, and re-layouts  13.7 us (5%)
  between operations  13.3 us (5%)
  other arithmetic  7.44 us (3%)
  starting transfers between devices  3.61 us (1%)
    all_gather x1, waiting for transfers between devices, on_device(): lax.all_gather(w_lift, 'pos', axis=0, tiled=True)  45.7 us
    all_gather x1, waiting for transfers between devices, on_device(): lax.all_gather(w_point, 'pos', axis=1, tiled=True)  44.8 us
    all_gather x1, waiting for transfers between devices, on_device(): value_piece = lax.all_gather(values_here, 'pos', axis=1, tiled=True)  42.6 us
    all_gather x1, waiting for transfers between devices, on_device(): lax.all_gather(w_skip, 'pos', axis=0, tiled=True)  41 us
    all_gather x1, waiting for transfers between devices, on_device(): key_piece = lax.all_gather(keys_here, 'pos', axis=1, tiled=True)  31.7 us
  transfers between devices with their start and end apart: 7, of which 6 were waited for; matrix products, arithmetic and copies ran while one was open for 12% of the time, Pallas kernels for 0%

commit v1 on v0

--- a/solution.py
+++ b/solution.py
@@ -1,11 +1,347 @@
+import functools
+
 import jax
 import jax.numpy as jnp
 from jax import lax
+from jax.experimental import pallas as pl
+from jax.experimental.pallas import tpu as pltpu
 from jax.sharding import PartitionSpec as P
 
 HEADS = 4
 HK = 64
 HV = 192
+F32 = jnp.float32
+BF16 = jnp.bfloat16
+ANY = pl.BlockSpec(memory_space=pl.ANY)
+VMEM = pl.BlockSpec(memory_space=pltpu.VMEM)
+SMEM = pl.BlockSpec(memory_space=pltpu.SMEM)
+LIMIT = pltpu.CompilerParams(vmem_limit_bytes=40 * 1024 * 1024)
+
+POS = 16
+C_SWAP = [(i, i ^ 1) for i in range(POS)]
+Y_SWAP = [(i, i ^ 2) for i in range(POS)]
+CY_SWAP = [(i, i ^ 3) for i in range(POS)]
+Z_RING = [(i, (i + 4) % POS) for i in range(POS)]
+CHIP_UP = [(i, i + 2) for i in range(POS - 2)]
+CHIP_DOWN = [(i + 2, i) for i in range(POS - 2)]
+X_SWAP = [(0, 1), (1, 0)]
+
+
+def over_pos(pairs):
+    return lambda v: lax.ppermute(v, "pos", pairs)
+
+
+c_swap, y_swap, cy_swap = over_pos(C_SWAP), over_pos(Y_SWAP), over_pos(CY_SWAP)
+z_ring = over_pos(Z_RING)
+
+
+def x_swap(v):
+    return lax.ppermute(v, "group", X_SWAP)
+
+
+def project_kernel(idx, acts, gain, wq, wk, wv, *outs):
+    a = acts[...].astype(F32)
+    centre = a - jnp.mean(a, axis=-1, keepdims=True)
+    normed = (
+        centre * lax.rsqrt(jnp.mean(centre * centre, axis=-1, keepdims=True) + 1e-05) * gain[...]
+    ).astype(BF16)
+    q = (jnp.dot(normed, wq[...], preferred_element_type=F32) * HK ** (-0.5))
+    k = jnp.dot(normed, wk[...], preferred_element_type=F32)
+    v = jnp.dot(normed, wv[...], preferred_element_type=F32)
+    zeros = jnp.zeros((a.shape[0], HK), F32)
+    packs = []
+    for h in range(HEADS):
+        packs.append(
+            jnp.concatenate(
+                [
+                    v[:, HV * h : HV * (h + 1)],
+                    k[:, HK * h : HK * (h + 1)],
+                    zeros,
+                    q[:, HK * h : HK * (h + 1)],
+                ],
+                axis=1,
+            ).astype(BF16)
+        )
+    mine = 2 * idx[1] + idx[3]
+    for h in range(HEADS):
+        for s in range(HEADS):
+
+            @pl.when((mine ^ s) == h)
+            def _():
+                outs[s][...] = packs[h]
+
+
+def project(idx, acts, gain, wq, wk, wv):
+    rows = acts.shape[0]
+    return pl.pallas_call(
+        project_kernel,
+        out_shape=[jax.ShapeDtypeStruct((rows, 384), BF16)] * HEADS,
+        in_specs=[SMEM] + [VMEM] * 5,
+        out_specs=[VMEM] * HEADS,
+        compiler_params=LIMIT,
+        name="project",
+    )(idx, acts, gain, wq, wk, wv)
+
+
+def attend_kernel(*refs):
+    packs, kvs, outs = refs[:4], refs[4:8], refs[8:]
+    for s in range(2):
+        rows = pl.ds(64 * s, 64)
+        query = jnp.concatenate([p[rows, 256:384] for p in packs], axis=0)
+        query = jnp.concatenate([jnp.zeros_like(query), query], axis=1)
+        kv = jnp.concatenate([r[pl.ds(256 * s, 256), :] for r in kvs], axis=0)
+        scores = lax.dot_general(
+            query, kv, (((1,), (1,)), ((), ())), preferred_element_type=F32
+        )
+        weights = jnp.exp(scores - jnp.max(scores, axis=-1, keepdims=True))
+        total = jnp.sum(weights, axis=-1, keepdims=True)
+        mixed = (
+            jnp.dot(weights.astype(BF16), kv, preferred_element_type=F32) / total
+        ).astype(BF16)
+        for j in range(4):
+            outs[j][rows, :] = mixed[64 * j : 64 * (j + 1), :]
+
+
+def attend(packs, kvs):
+    return pl.pallas_call(
+        attend_kernel,
+        out_shape=[jax.ShapeDtypeStruct((128, 256), BF16)] * 4,
+        in_specs=[VMEM] * 8,
+        out_specs=[VMEM] * 4,
+        compiler_params=LIMIT,
+        name="attend",
+    )(*packs, *kvs)
+
+
+def output_kernel(idx, acts, wo, *refs):
+    mixed, out = refs[:4], refs[4]
+    mine = 2 * idx[1] + idx[3]
+    total = acts[...].astype(F32)
+    summed = None
+    for s in range(4):
+        rows = pl.ds(pl.multiple_of((mine ^ s) * HV, HV), HV)
+        term = jnp.dot(mixed[s][:, :HV], wo[rows, :], preferred_element_type=F32)
+        summed = term if summed is None else summed + term
+    attended = (total + summed).astype(BF16).astype(F32)
+    out[...] = jax.nn.gelu(attended).astype(BF16)
+
+
+def output(idx, acts, wo, mixed):
+    return pl.pallas_call(
+        output_kernel,
+        out_shape=jax.ShapeDtypeStruct(acts.shape, BF16),
+        in_specs=[SMEM] + [VMEM] * 6,
+        out_specs=VMEM,
+        compiler_params=LIMIT,
+        name="output",
+    )(idx, acts, wo, *mixed)
+
+
+def start_all(copies, sems):
+    started = []
+    for n, (src, dst) in enumerate(copies):
+        copy = pltpu.make_async_copy(src, dst, sems.at[n])
+        copy.start()
+        started.append(copy)
+    return started
+
+
+def place(ref, blocks, columns, dst, height, pos, col):
+    return [
+        (
+            ref.at[pl.ds(row, height), columns],
+            dst.at[pl.ds(pl.multiple_of(p * height, height), height), col],
+        )
+        for row, p in zip(blocks, pos)
+    ]
+
+
+ALL = slice(None)
+
+
+def quarter(x):
+    return pl.ds(pl.multiple_of(x * 384, 384), 384)
+
+
+def merge_kernel(idx, act_own, act_oth, skip_own, skip_oth, *refs):
+    pieces, (merged, first, last), (wl, ws, act, skip, sems) = refs[:14], refs[14:17], refs[17:]
+    x, y, z, c = idx[0], idx[1], idx[2], idx[3]
+    copies = []
+
+    def add(ref, zz, yy, col):
+        pos = [4 * zz + 2 * yy + c, 4 * zz + 2 * yy + 1 - c]
+        copies.extend(place(ref, (0, 176), ALL, wl, 96, pos, col))
+        copies.extend(place(ref, (96, 272), ALL, ws, 80, pos, col))
+
+    own, yown = pieces[:2]
+    add(own, z, y, ALL)
+    add(yown, z, 1 - y, ALL)
+    for k in range(1, 4):
+        zz = lax.rem(z + 4 - k, 4)
+        a, b, xa, xb = pieces[2 + 4 * (k - 1) : 2 + 4 * k]
+        add(a, zz, y, quarter(x))
+        add(b, zz, 1 - y, quarter(x))
+        add(xa, zz, y, quarter(1 - x))
+        add(xb, zz, 1 - y, quarter(1 - x))
+    started = start_all(copies, sems)
+    for s in range(2):
+        for src_a, src_s, cc in ((act_own, skip_own, c), (act_oth, skip_oth, 1 - c)):
+            act[pl.ds(pl.multiple_of(128 * s + 64 * cc, 64), 64), :] = src_a[
+                pl.ds(64 * s, 64), :
+            ]
+            skip[pl.ds(pl.multiple_of(256 * s + 128 * cc, 128), 128), :] = src_s[
+                pl.ds(128 * s, 128), :
+            ]
+    twice = (
+        lax.broadcasted_iota(jnp.int32, (256, 128), 0) // 2
+        == lax.broadcasted_iota(jnp.int32, (256, 128), 1)
+    ).astype(BF16)
+    for copy in started:
+        copy.wait()
+    lifted = jnp.dot(act[...], wl[...], preferred_element_type=F32).astype(BF16)
+    for s in range(2):
+        term = jnp.dot(
+            skip[pl.ds(256 * s, 256), :], ws[...], preferred_element_type=F32
+        )
+        raised = jnp.dot(twice, lifted[128 * s : 128 * (s + 1)], preferred_element_type=F32)
+        total = (raised + term).astype(BF16)
+        merged[s, :, :] = total
+        first[s : s + 1, :] = total[0:1, :]
+        last[s : s + 1, :] = total[255:256, :]
+
+
+def merge(idx, act_own, act_oth, skip_own, skip_oth, pieces):
+    return pl.pallas_call(
+        merge_kernel,
+        out_shape=[
+            jax.ShapeDtypeStruct((2, 256, 768), BF16),
+            jax.ShapeDtypeStruct((2, 768), BF16),
+            jax.ShapeDtypeStruct((2, 768), BF16),
+        ],
+        in_specs=[SMEM] + [VMEM] * 4 + [ANY] * len(pieces),
+        out_specs=[VMEM] * 3,
+        scratch_shapes=[
+            pltpu.VMEM((1536, 768), BF16),
+            pltpu.VMEM((1280, 768), BF16),
+            pltpu.VMEM((256, 1536), BF16),
+            pltpu.VMEM((512, 1280), BF16),
+            pltpu.SemaphoreType.DMA((56,)),
+        ],
+        compiler_params=LIMIT,
+        name="merge",
+    )(idx, act_own, act_oth, skip_own, skip_oth, *pieces)
+
+
+def point_kernel(idx, depth, merged, before, after, *refs):
+    pieces, (own, oth), (wp, spread, sems) = refs[:9], refs[9:11], refs[11:]
+    x, y, z, c = idx[0], idx[1], idx[2], idx[3]
+    copies = []
+
+    def add(ref, zz, yy, col, row=0):
+        pos = [4 * zz + 2 * yy + c, 4 * zz + 2 * yy + 1 - c]
+        copies.extend(place(ref, (row, row + 96), ALL, wp, 96, pos, col))
+
+    add(pieces[0], z, y, ALL)
+    add(pieces[1], z, 1 - y, quarter(x))
+    add(pieces[2], z, 1 - y, quarter(1 - x))
+    for k in range(1, 4):
+        zz = lax.rem(z + 4 - k, 4)
+        for ref, col in ((pieces[2 * k + 1], quarter(x)), (pieces[2 * k + 2], quarter(1 - x))):
+            add(ref, zz, y, col)
+            add(ref, zz, 1 - y, col, 192)
+    started = start_all(copies, sems)
+    taps = depth[:, pl.ds(pl.multiple_of(c * 768, 768), 768)]
+    row = lax.broadcasted_iota(jnp.int32, (256, 768), 0)
+    for s in range(2):
+        here = merged[s, :, :].astype(F32)
+        up = jnp.where(row == 0, before[s : s + 1, :].astype(F32), pltpu.roll(here, 1, 0))
+        down = jnp.where(row == 255, after[s : s + 1, :].astype(F32), pltpu.roll(here, 255, 0))
+        spread[pl.ds(256 * s, 256), :] = (
+            taps[0:1] * up + taps[1:2] * here + taps[2:3] * down
+        ).astype(BF16)
+    for copy in started:
+        copy.wait()
+    for s in range(2):
+        for out, cc in ((oth, 1 - c), (own, c)):
+            part = spread[pl.ds(pl.multiple_of(256 * s + 128 * cc, 128), 128), :]
+            out[s, :, :] = lax.dot_general(
+                part, wp[...], (((1,), (1,)), ((), ())), preferred_element_type=F32
+            ).astype(out.dtype)
+
+
+def point(idx, depth, merged, before, after, pieces):
+    return pl.pallas_call(
+        point_kernel,
+        out_shape=[
+            jax.ShapeDtypeStruct((2, 128, 1536), F32),
+            jax.ShapeDtypeStruct((2, 128, 1536), BF16),
+        ],
+        in_specs=[SMEM] + [VMEM] * 4 + [ANY] * len(pieces),
+        out_specs=[VMEM] * 2,
+        scratch_shapes=[
+            pltpu.VMEM((1536, 768), BF16),
+            pltpu.VMEM((512, 768), BF16),
+            pltpu.SemaphoreType.DMA((30,)),
+        ],
+        compiler_params=LIMIT,
+        name="point",
+    )(idx, depth, merged, before, after, *pieces)
+
+
+def columns(v, i, width):
+    return lax.dynamic_slice_in_dim(v, i * width, width, axis=1)
+
+
+def on_device(
+    acts, skips, norm_gain, w_query, w_key, w_value, w_out, w_lift, w_skip, depth_kernel, w_point
+):
+    pos = lax.axis_index("pos")
+    x, c, y, z = lax.axis_index("group"), pos % 2, pos // 2 % 2, pos // 4
+    idx = jnp.stack([x, y, z, c]).astype(jnp.int32)
+    flat = acts.reshape(128, 1536)
+
+    def chip_half(shard):
+        return jnp.concatenate(
+            [columns(shard, c, 768), c_swap(columns(shard, 1 - c, 768))], axis=0
+        )
+
+    half_a = chip_half(jnp.concatenate([w_lift, w_skip], axis=0))
+    half_b = chip_half(w_point.T)
+    pieces_a = [half_a, y_swap(half_a)]
+    a = columns(half_a, x, 384)
+    for _ in range(3):
+        a = z_ring(a)
+        b = y_swap(a)
+        pieces_a += [a, b, x_swap(a), x_swap(b)]
+    mine_b = columns(half_b, x, 384)
+    y_mine_b = y_swap(mine_b)
+    pieces_b = [half_b, y_mine_b, y_swap(columns(half_b, 1 - x, 384))]
+    b = jnp.concatenate([mine_b, y_mine_b], axis=0)
+    for _ in range(3):
+        b = z_ring(b)
+        pieces_b += [b, x_swap(b)]
+
+    packs = project(idx, flat, norm_gain.reshape(1, -1), w_query, w_key, w_value)
+    swaps = [lambda v: v, c_swap, y_swap, cy_swap]
+    packs = [swap(p) for swap, p in zip(swaps, packs)]
+    kv = jnp.concatenate(
+        [p[:, :256].reshape(2, 64, 256) for p in packs], axis=1
+    ).reshape(512, 256)
+    kvs = [kv]
+    for _ in range(3):
+        kv = z_ring(kv)
+        kvs.append(kv)
+    mixed = attend(packs, kvs)
+    mixed = [swap(m) for swap, m in zip(swaps, mixed)]
+    activated = output(idx, flat, w_out, mixed)
+    skip_act = jax.nn.gelu(skips.astype(F32)).astype(BF16).reshape(256, 1280)
+    merged, first, last = merge(
+        idx, activated, c_swap(activated), skip_act, c_swap(skip_act), pieces_a
+    )
+    before = lax.ppermute(last, "pos", CHIP_UP)
+    after = lax.ppermute(first, "pos", CHIP_DOWN)
+    own, oth = point(idx, depth_kernel, merged, before, after, pieces_b)
+    return (own + c_swap(oth).astype(F32)).astype(BF16)
 
 
 def extended(cells, sides, width):
@@ -25,7 +361,7 @@
     return cells
 
 
-def on_device(
+def on_device_plain(
     acts, skips, norm_gain, w_query, w_key, w_value, w_out, w_lift, w_skip, depth_kernel, w_point
 ):
     lift_full, skip_full, point_full = (
@@ -107,8 +443,9 @@
 
 
 def solution(mesh):
+    planned = dict(mesh.shape) == {"group": 2, "pos": POS}
     return jax.shard_map(
-        on_device,
+        on_device if planned else on_device_plain,
         mesh=mesh,
         in_specs=(
             P("group", "pos", None),

time: 269 us -> 121 us (0.45)
  waiting for transfers between devices: 209 us -> 58.3 us
  starting transfers between devices: 3.61 us -> 39.5 us
  matrix products: 21 us -> 0 us
  Pallas kernels: 0 us -> 15.1 us
  between operations: 13.3 us -> 0.27 us
  local copies, waits for them, and re-layouts: 13.7 us -> 5.79 us
  other arithmetic: 7.44 us -> 1.81 us
    all_gather x5 -> x0, waiting for transfers between devices: 206 us -> none  [the longest x1 45.7 us: on_device(): lax.all_gather(w_lift, 'pos', axis=0, tiled=True)]
    ppermute x2 -> x37, waiting for transfers between devices: 1.69 us -> 58.3 us  [the longest x26 37.8 us: over_pos(): return lambda v: lax.ppermute(v, 'pos', pairs)]
    ppermute x2 -> x37, starting transfers between devices: 3.45 us -> 39.5 us  [the longest x26 22.7 us: over_pos(): return lambda v: lax.ppermute(v, 'pos', pairs)]
    dot_general x8 -> x0, matrix products: 21 us -> none  [the longest x1 4.63 us: on_device(): decoded = jnp.dot(spread, point_full, preferred_element_type=jnp.float32)]
    pallas_call x0 -> x5, Pallas kernels: none -> 15.1 us  [the longest x1 5.51 us: merge(): pl.pallas_call(merge_kernel, out_shape=[jax.ShapeDtypeStruct((2, 256, 768...]
    all_gather x2 -> x0, local copies, waits for them, and re-layouts: 6.13 us -> none  [the longest x1 4.65 us: on_device(): value_piece = lax.all_gather(values_here, 'pos', axis=1, tiled=True)]
    convert_element_type x3 -> x0, local copies, waits for them, and re-layouts: 3.65 us -> none  [the longest x1 3.21 us: on_device(): raised.astype(jnp.float32) + skip_term]
    unnamed x14 -> x23, local copies, waits for them, and re-layouts: 1.38 us -> 4.98 us
  transfers between devices with their start and end apart: 7 -> 37, of which waited for: 6 -> 21; matrix products, arithmetic and copies ran while one was open for 12% -> 1% of each run, Pallas kernels for 0% -> 7%
where the time goes in v1:
time: 121 us
  waiting for transfers between devices  58.3 us (48%)
  starting transfers between devices  39.5 us (33%)
  Pallas kernels  15.1 us (12%)
  local copies, waits for them, and re-layouts  5.79 us (5%)
  other arithmetic  1.81 us (1%)
    ppermute x26, waiting for transfers between devices, over_pos(): return lambda v: lax.ppermute(v, 'pos', pairs)  37.8 us
    ppermute x26, starting transfers between devices, over_pos(): return lambda v: lax.ppermute(v, 'pos', pairs)  22.7 us
    ppermute x9, waiting for transfers between devices, x_swap(): return lax.ppermute(v, 'group', X_SWAP)  20.4 us
    ppermute x9, starting transfers between devices, x_swap(): return lax.ppermute(v, 'group', X_SWAP)  11.4 us
    pallas_call x1, Pallas kernels, merge(): pl.pallas_call(merge_kernel, out_shape=[jax.ShapeDtypeStruct((2, 256, 768...  5.51 us
    pallas_call x1, Pallas kernels, point(): pl.pallas_call(point_kernel, out_shape=[jax.ShapeDtypeStruct((2, 128, 153...  5.37 us
    unnamed x23, local copies, waits for them, and re-layouts  4.98 us
    ppermute x1, starting transfers between devices, on_device(): before = lax.ppermute(last, 'pos', CHIP_UP)  3.95 us
  transfers between devices with their start and end apart: 37, of which 21 were waited for; matrix products, arithmetic and copies ran while one was open for 1% of the time, Pallas kernels for 7%

profile of v1, /device:TPU:0, one launch (start us, length us, event | category | flops | bytes accessed | tf_op | source)
XLA Modules:
  0.0 120.7 jit_solution(4474238482879283331)
XLA Ops:
  0.0 0.7 reshape.25.gain
  0.7 0.1 pad_add_fusion.idx
  0.8 1.7 %copy-done = bf16[1536,768]{1,0:T(8,128)(2,1)S(1)} copy-done((bf16[1536,768]{1,0:T(8,128)(2,1)S(1)}, bf16[1536,768]{1,0:T(8,128)(2,1)}, u32[]{:S(2)}) %copy-start) | copy-done | bytes 2359320
  2.4 1.0 copy-done.2
  3.4 1.1 copy-done.4
  4.6 1.1 copy-done.5
  5.7 1.7 %project.1 = (bf16[128,384]{1,0:T(8,128)(2,1)S(1)}, bf16[128,384]{1,0:T(8,128)(2,1)S(1)}, bf16[128,384]{1,0:T(8,128)(2,1)S(1)}, bf16[128,384]{1,0:T(8,128)(2,1)S(1)}) custom-call(s32[4]{0:T(128)S(1)} %pad_add_fusion.idx, bf16[128,1536]{1,0:T(8,128)(2,1)S(1)} %bitcast.17, f32[1,1536]{1,0:T(1,128)S(1)} %reshape.25.gain, bf16[1536,256]{1,0:T(8,128)(2,1)S(1)} %copy-done.4, ...), custom_call_target="tpu_custom_call" | custom-call | tf_op jit(solution)/shard_map/project/pallas_call | solution.py:76
  7.4 0.5 collective-permute-start
  7.9 2.6 %collective-permute-start.1 = (bf16[128,384]{1,0:T(8,128)(2,1)S(1)}, bf16[128,384]{1,0:T(8,128)(2,1)S(1)}, u32[]{:S(2)}, u32[]{:S(2)}) collective-permute-start(bf16[128,384]{1,0:T(8,128)(2,1)S(1)} %get-tuple-element.20), channel_id=1, source_target_pairs={{0,2},{1,3},{2,0},{3,1},{4,6},{5,7},{6,4},{7,5},{8,10},{9,11},{10,... | collective-permute-start | bytes 294920 | tf_op jit(solution)/shard_map/ppermute | solution.py:31
  10.6 0.2 collective-permute-start.27
  10.9 0.4 collective-permute-start.11
  11.4 2.8 %collective-permute-done.1.refs_2_ = bf16[128,384]{1,0:T(8,128)(2,1)S(1)} collective-permute-done((bf16[128,384]{1,0:T(8,128)(2,1)S(1)}, bf16[128,384]{1,0:T(8,128)(2,1)S(1)}, u32[]{:S(2)}, u32[]{:S(2)}) %collective-permute-start.1) | collective-permute-done | bytes 98336 | tf_op jit(solution)/shard_map/ppermute | solution.py:31
  14.1 1.6 %collective-permute-done.2.refs_3_ = bf16[128,384]{1,0:T(8,128)(2,1)S(1)} collective-permute-done((bf16[128,384]{1,0:T(8,128)(2,1)S(1)}, bf16[128,384]{1,0:T(8,128)(2,1)S(1)}, u32[]{:S(2)}, u32[]{:S(2)}) %collective-permute-start.2) | collective-permute-done | bytes 98336 | tf_op jit(solution)/shard_map/ppermute | solution.py:31
  15.8 1.7 %collective-permute-start.3 = (bf16[512,256]{1,0:T(8,128)(2,1)S(1)}, bf16[512,256]{1,0:T(8,128)(2,1)S(1)}, u32[]{:S(2)}, u32[]{:S(2)}) collective-permute-start(bf16[512,256]{1,0:T(8,128)(2,1)S(1)} %bitcast.19), channel_id=1, source_target_pairs={{0,4},{1,5},{2,6},{3,7},{4,8},{5,9},{6,10},{7,11},{8,12},{9,13},{1... | collective-permute-start | bytes 786440 | tf_op jit(solution)/shard_map/ppermute | solution.py:31
  17.5 1.6 %collective-permute-start.28 = (bf16[192,384]{1,0:T(8,128)(2,1)S(1)}, bf16[192,384]{1,0:T(8,128)(2,1)S(1)}, u32[]{:S(2)}, u32[]{:S(2)}) collective-permute-start(bf16[192,384]{1,0:T(8,128)(2,1)S(1)} %get-tuple-element.34), channel_id=1, source_target_pairs={{0,2},{1,3},{2,0},{3,1},{4,6},{5,7},{6,4},{7,5},{8,10},{9,11},{10,... | collective-permute-start | bytes 442376 | tf_op jit(solution)/shard_map/ppermute | solution.py:31
  19.1 0.4 fusion.5
  19.5 0.1 collective-permute-start.10
  19.7 1.6 %collective-permute-start.13 = (bf16[352,384]{1,0:T(8,128)(2,1)S(1)}, bf16[352,384]{1,0:T(8,128)(2,1)S(1)}, u32[]{:S(2)}, u32[]{:S(2)}) collective-permute-start(bf16[352,384]{1,0:T(8,128)(2,1)S(1)} %fusion.6), channel_id=1, source_target_pairs={{0,4},{1,5},{2,6},{3,7},{4,8},{5,9},{6,10},{7,11},{8,12},{9,13},{1... | collective-permute-start | bytes 811016 | tf_op jit(solution)/shard_map/ppermute | solution.py:31
  21.3 2.0 %collective-permute-done.28.refs_1_ = bf16[192,384]{1,0:T(8,128)(2,1)S(1)} collective-permute-done((bf16[192,384]{1,0:T(8,128)(2,1)S(1)}, bf16[192,384]{1,0:T(8,128)(2,1)S(1)}, u32[]{:S(2)}, u32[]{:S(2)}) %collective-permute-start.28) | collective-permute-done | bytes 147488 | tf_op jit(solution)/shard_map/ppermute | solution.py:31
  23.3 1.6 %collective-permute-start.30 = (bf16[384,384]{1,0:T(8,128)(2,1)S(1)}, bf16[384,384]{1,0:T(8,128)(2,1)S(1)}, u32[]{:S(2)}, u32[]{:S(2)}) collective-permute-start(bf16[384,384]{1,0:T(8,128)(2,1)S(1)} %pad_maximum_fusion.2), channel_id=1, source_target_pairs={{0,4},{1,5},{2,6},{3,7},{4,8},{5,9},{6,10},{7,11},{8,12},{9,13},{1... | collective-permute-start | bytes 884744 | tf_op jit(solution)/shard_map/ppermute | solution.py:31
  25.0 1.8 %collective-permute-done.3.refs_5_ = bf16[512,256]{1,0:T(8,128)(2,1)S(1)} collective-permute-done((bf16[512,256]{1,0:T(8,128)(2,1)S(1)}, bf16[512,256]{1,0:T(8,128)(2,1)S(1)}, u32[]{:S(2)}, u32[]{:S(2)}) %collective-permute-start.3) | collective-permute-done | bytes 262176 | tf_op jit(solution)/shard_map/ppermute | solution.py:31
  26.8 1.6 %collective-permute-start.12 = (bf16[352,768]{1,0:T(8,128)(2,1)S(1)}, bf16[352,768]{1,0:T(8,128)(2,1)S(1)}, u32[]{:S(2)}, u32[]{:S(2)}) collective-permute-start(bf16[352,768]{1,0:T(8,128)(2,1)S(1)} %pad_maximum_fusion.refs_0_), channel_id=1, source_target_pairs={{0,2},{1,3},{2,0},{3,1},{4,6},{5,7},{6,4},{7,5},{8,10},{9,11},{10,... | collective-permute-start | bytes 1622024 | tf_op jit(solution)/shard_map/ppermute | solution.py:31
  28.4 4.1 %collective-permute-done.13.refs_2_ = bf16[352,384]{1,0:T(8,128)(2,1)S(1)} collective-permute-done((bf16[352,384]{1,0:T(8,128)(2,1)S(1)}, bf16[352,384]{1,0:T(8,128)(2,1)S(1)}, u32[]{:S(2)}, u32[]{:S(2)}) %collective-permute-start.13) | collective-permute-done | bytes 270368 | tf_op jit(solution)/shard_map/ppermute | solution.py:31
  32.5 6.3 %collective-permute-done.30.refs_3_ = bf16[384,384]{1,0:T(8,128)(2,1)S(1)} collective-permute-done((bf16[384,384]{1,0:T(8,128)(2,1)S(1)}, bf16[384,384]{1,0:T(8,128)(2,1)S(1)}, u32[]{:S(2)}, u32[]{:S(2)}) %collective-permute-start.30) | collective-permute-done | bytes 294944 | tf_op jit(solution)/shard_map/ppermute | solution.py:31
  38.8 1.6 %collective-permute-start.14 = (bf16[352,384]{1,0:T(8,128)(2,1)S(1)}, bf16[352,384]{1,0:T(8,128)(2,1)S(1)}, u32[]{:S(2)}, u32[]{:S(2)}) collective-permute-start(bf16[352,384]{1,0:T(8,128)(2,1)S(1)} %collective-permute-done.13.refs_2_), channel_id=1, source_target_pairs={{0,2},{1,3},{2,0},{3,1},{4,6},{5,7},{6,4},{7,5},{8,10},{9,11},{10,... | collective-permute-start | bytes 811016 | tf_op jit(solution)/shard_map/ppermute | solution.py:31
  40.4 4.0 %collective-permute-done.4.refs_6_ = bf16[512,256]{1,0:T(8,128)(2,1)S(1)} collective-permute-done((bf16[512,256]{1,0:T(8,128)(2,1)S(1)}, bf16[512,256]{1,0:T(8,128)(2,1)S(1)}, u32[]{:S(2)}, u32[]{:S(2)}) %collective-permute-start.4) | collective-permute-done | bytes 262176 | tf_op jit(solution)/shard_map/ppermute | solution.py:31
  44.5 1.5 %collective-permute-start.15 = (bf16[352,384]{1,0:T(8,128)(2,1)S(1)}, bf16[352,384]{1,0:T(8,128)(2,1)S(1)}, u32[]{:S(2)}, u32[]{:S(2)}) collective-permute-start(bf16[352,384]{1,0:T(8,128)(2,1)S(1)} %collective-permute-done.13.refs_2_), channel_id=1, source_target_pairs={{0,16},{16,0},{1,17},{17,1},{2,18},{18,2},{3,19},{19,3},{4,20},{20... | collective-permute-start | bytes 811016 | tf_op jit(solution)/shard_map/ppermute | solution.py:39
  46.0 4.2 %collective-permute-done.17.refs_6_ = bf16[352,384]{1,0:T(8,128)(2,1)S(1)} collective-permute-done((bf16[352,384]{1,0:T(8,128)(2,1)S(1)}, bf16[352,384]{1,0:T(8,128)(2,1)S(1)}, u32[]{:S(2)}, u32[]{:S(2)}) %collective-permute-start.17) | collective-permute-done | bytes 270368 | tf_op jit(solution)/shard_map/ppermute | solution.py:31
  50.3 5.6 %collective-permute-done.5.refs_7_ = bf16[512,256]{1,0:T(8,128)(2,1)S(1)} collective-permute-done((bf16[512,256]{1,0:T(8,128)(2,1)S(1)}, bf16[512,256]{1,0:T(8,128)(2,1)S(1)}, u32[]{:S(2)}, u32[]{:S(2)}) %collective-permute-start.5) | collective-permute-done | bytes 262176 | tf_op jit(solution)/shard_map/ppermute | solution.py:31
  55.9 1.3 %attend.1 = (bf16[128,256]{1,0:T(8,128)(2,1)S(1)}, bf16[128,256]{1,0:T(8,128)(2,1)S(1)}, bf16[128,256]{1,0:T(8,128)(2,1)S(1)}, bf16[128,256]{1,0:T(8,128)(2,1)S(1)}) custom-call(bf16[128,384]{1,0:T(8,128)(2,1)S(1)} %get-tuple-element.18.refs_0_, bf16[128,384]{1,0:T(8,128)(2,1)S(1)} %collective-permute-done.refs_1_, ...), custom_call_target="tpu_custom_call" | custom-call | tf_op jit(solution)/shard_map/attend/pallas_call | solution.py:106
  57.1 0.1 collective-permute-start.6
  57.2 1.6 %collective-permute-start.7 = (bf16[128,256]{1,0:T(8,128)(2,1)S(1)}, bf16[128,256]{1,0:T(8,128)(2,1)S(1)}, u32[]{:S(2)}, u32[]{:S(2)}) collective-permute-start(bf16[128,256]{1,0:T(8,128)(2,1)S(1)} %get-tuple-element.24), channel_id=1, source_target_pairs={{0,2},{1,3},{2,0},{3,1},{4,6},{5,7},{6,4},{7,5},{8,10},{9,11},{10,... | collective-permute-start | bytes 196616 | tf_op jit(solution)/shard_map/ppermute | solution.py:31
  58.9 0.2 collective-permute-start.8
  59.1 1.6 %collective-permute-start.18 = (bf16[352,384]{1,0:T(8,128)(2,1)S(1)}, bf16[352,384]{1,0:T(8,128)(2,1)S(1)}, u32[]{:S(2)}, u32[]{:S(2)}) collective-permute-start(bf16[352,384]{1,0:T(8,128)(2,1)S(1)} %collective-permute-done.17.refs_6_), channel_id=1, source_target_pairs={{0,2},{1,3},{2,0},{3,1},{4,6},{5,7},{6,4},{7,5},{8,10},{9,11},{10,... | collective-permute-start | bytes 811016 | tf_op jit(solution)/shard_map/ppermute | solution.py:31
  60.7 1.1 collective-permute-done.7.refs_2_
  61.7 1.5 %collective-permute-start.16 = (bf16[352,384]{1,0:T(8,128)(2,1)S(1)}, bf16[352,384]{1,0:T(8,128)(2,1)S(1)}, u32[]{:S(2)}, u32[]{:S(2)}) collective-permute-start(bf16[352,384]{1,0:T(8,128)(2,1)S(1)} %collective-permute-done.14.refs_3_), channel_id=1, source_target_pairs={{0,16},{16,0},{1,17},{17,1},{2,18},{18,2},{3,19},{19,3},{4,20},{20... | collective-permute-start | bytes 811016 | tf_op jit(solution)/shard_map/ppermute | solution.py:39
  63.3 1.1 collective-permute-start.19
  64.4 1.3 %output.1.act_own = bf16[128,1536]{1,0:T(8,128)(2,1)S(1)} custom-call(s32[4]{0:T(128)S(1)} %pad_add_fusion.idx, bf16[128,1536]{1,0:T(8,128)(2,1)S(1)} %bitcast.18, bf16[768,1536]{1,0:T(8,128)(2,1)S(1)} %copy-done.1, bf16[128,256]{1,0:T(8,128)(2,1)S(1)} %get-tuple-element.22.refs_0_, bf16[128,256]{1,0:T(8,128)(2,1)S(1)} %collective-permute-done.6.refs_1_, ...), custom_call_target="tpu_custom_call" | custom-call | tf_op jit(solution)/shard_map/output/pallas_call | solution.py:130
  65.8 0.6 collective-permute-start.9
  66.4 1.1 collective-permute-done.21.refs_10_
  67.5 1.5 %collective-permute-start.22 = (bf16[352,384]{1,0:T(8,128)(2,1)S(1)}, bf16[352,384]{1,0:T(8,128)(2,1)S(1)}, u32[]{:S(2)}, u32[]{:S(2)}) collective-permute-start(bf16[352,384]{1,0:T(8,128)(2,1)S(1)} %collective-permute-done.21.refs_10_), channel_id=1, source_target_pairs={{0,2},{1,3},{2,0},{3,1},{4,6},{5,7},{6,4},{7,5},{8,10},{9,11},{10,... | collective-permute-start | bytes 811016 | tf_op jit(solution)/shard_map/ppermute | solution.py:31
  69.0 0.1 collective-permute-done.18.refs_7_
  69.1 1.4 %collective-permute-start.34 = (bf16[384,384]{1,0:T(8,128)(2,1)S(1)}, bf16[384,384]{1,0:T(8,128)(2,1)S(1)}, u32[]{:S(2)}, u32[]{:S(2)}) collective-permute-start(bf16[384,384]{1,0:T(8,128)(2,1)S(1)} %collective-permute-done.32.refs_5_), channel_id=1, source_target_pairs={{0,4},{1,5},{2,6},{3,7},{4,8},{5,9},{6,10},{7,11},{8,12},{9,13},{1... | collective-permute-start | bytes 884744 | tf_op jit(solution)/shard_map/ppermute | solution.py:31
  70.4 0.7 collective-permute-done.16.refs_5_
  71.1 1.5 %collective-permute-start.20 = (bf16[352,384]{1,0:T(8,128)(2,1)S(1)}, bf16[352,384]{1,0:T(8,128)(2,1)S(1)}, u32[]{:S(2)}, u32[]{:S(2)}) collective-permute-start(bf16[352,384]{1,0:T(8,128)(2,1)S(1)} %collective-permute-done.18.refs_7_), channel_id=1, source_target_pairs={{0,16},{16,0},{1,17},{17,1},{2,18},{18,2},{3,19},{19,3},{4,20},{20... | collective-permute-start | bytes 811016 | tf_op jit(solution)/shard_map/ppermute | solution.py:39
  72.7 4.3 %collective-permute-done.19.refs_8_ = bf16[352,384]{1,0:T(8,128)(2,1)S(1)} collective-permute-done((bf16[352,384]{1,0:T(8,128)(2,1)S(1)}, bf16[352,384]{1,0:T(8,128)(2,1)S(1)}, u32[]{:S(2)}, u32[]{:S(2)}) %collective-permute-start.19) | collective-permute-done | bytes 270368 | tf_op jit(solution)/shard_map/ppermute | solution.py:39
  76.9 1.5 %collective-permute-start.23 = (bf16[352,384]{1,0:T(8,128)(2,1)S(1)}, bf16[352,384]{1,0:T(8,128)(2,1)S(1)}, u32[]{:S(2)}, u32[]{:S(2)}) collective-permute-start(bf16[352,384]{1,0:T(8,128)(2,1)S(1)} %collective-permute-done.21.refs_10_), channel_id=1, source_target_pairs={{0,16},{16,0},{1,17},{17,1},{2,18},{18,2},{3,19},{19,3},{4,20},{20... | collective-permute-start | bytes 811016 | tf_op jit(solution)/shard_map/ppermute | solution.py:39
  78.5 0.5 collective-permute-start.24
  79.0 0.9 collective-permute-done.34.refs_7_
  79.8 1.5 %collective-permute-start.31 = (bf16[384,384]{1,0:T(8,128)(2,1)S(1)}, bf16[384,384]{1,0:T(8,128)(2,1)S(1)}, u32[]{:S(2)}, u32[]{:S(2)}) collective-permute-start(bf16[384,384]{1,0:T(8,128)(2,1)S(1)} %collective-permute-done.30.refs_3_), channel_id=1, source_target_pairs={{0,16},{16,0},{1,17},{17,1},{2,18},{18,2},{3,19},{19,3},{4,20},{20... | collective-permute-start | bytes 884744 | tf_op jit(solution)/shard_map/ppermute | solution.py:39
  81.3 0.5 collective-permute-start.33
  81.8 0.9 collective-permute-done.20.refs_9_
  82.7 1.5 %collective-permute-start.35 = (bf16[384,384]{1,0:T(8,128)(2,1)S(1)}, bf16[384,384]{1,0:T(8,128)(2,1)S(1)}, u32[]{:S(2)}, u32[]{:S(2)}) collective-permute-start(bf16[384,384]{1,0:T(8,128)(2,1)S(1)} %collective-permute-done.34.refs_7_), channel_id=1, source_target_pairs={{0,16},{16,0},{1,17},{17,1},{2,18},{18,2},{3,19},{19,3},{4,20},{20... | collective-permute-start | bytes 884744 | tf_op jit(solution)/shard_map/ppermute | solution.py:39
  84.3 4.3 %collective-permute-done.23.refs_12_ = bf16[352,384]{1,0:T(8,128)(2,1)S(1)} collective-permute-done((bf16[352,384]{1,0:T(8,128)(2,1)S(1)}, bf16[352,384]{1,0:T(8,128)(2,1)S(1)}, u32[]{:S(2)}, u32[]{:S(2)}) %collective-permute-start.23) | collective-permute-done | bytes 270368 | tf_op jit(solution)/shard_map/ppermute | solution.py:39
  88.5 2.0 %collective-permute-start.29 = (bf16[192,384]{1,0:T(8,128)(2,1)S(1)}, bf16[192,384]{1,0:T(8,128)(2,1)S(1)}, u32[]{:S(2)}, u32[]{:S(2)}) collective-permute-start(bf16[192,384]{1,0:T(8,128)(2,1)S(1)} %get-tuple-element.33), channel_id=1, source_target_pairs={{0,2},{1,3},{2,0},{3,1},{4,6},{5,7},{6,4},{7,5},{8,10},{9,11},{10,... | collective-permute-start | bytes 442376 | tf_op jit(solution)/shard_map/ppermute | solution.py:31
  90.6 3.7 %collective-permute-done.24.refs_13_ = bf16[352,384]{1,0:T(8,128)(2,1)S(1)} collective-permute-done((bf16[352,384]{1,0:T(8,128)(2,1)S(1)}, bf16[352,384]{1,0:T(8,128)(2,1)S(1)}, u32[]{:S(2)}, u32[]{:S(2)}) %collective-permute-start.24) | collective-permute-done | bytes 270368 | tf_op jit(solution)/shard_map/ppermute | solution.py:39
  94.3 5.5 %merge.1 = (bf16[2,256,768]{2,1,0:T(8,128)(2,1)S(1)}, bf16[2,768]{1,0:T(2,128)(2,1)S(1)}, bf16[2,768]{1,0:T(2,128)(2,1)S(1)}) custom-call(s32[4]{0:T(128)S(1)} %pad_add_fusion.idx, bf16[128,1536]{1,0:T(8,128)(2,1)S(1)} %output.1.act_own, bf16[128,1536]{1,0:T(8,128)(2,1)S(1)} %collective-permute-done.9.act_oth, bf16[256,1280]{1,0:T(8,128)(2,1)S(1)} %bitcast.16, ...), custom_call_target="tpu_custom_call" | custom-call | tf_op jit(solution)/shard_map/merge/pallas_call | solution.py:214
  99.8 4.0 %collective-permute-start.25 = (bf16[2,768]{1,0:T(2,128)(2,1)S(1)}, bf16[2,768]{1,0:T(2,128)(2,1)S(1)}, u32[]{:S(2)}, u32[]{:S(2)}) collective-permute-start(bf16[2,768]{1,0:T(2,128)(2,1)S(1)} %get-tuple-element.27), channel_id=1, source_target_pairs={{0,2},{1,3},{2,4},{3,5},{4,6},{5,7},{6,8},{7,9},{8,10},{9,11},{10,... | collective-permute-start | bytes 9224 | tf_op jit(solution)/shard_map/ppermute | solution.py:341
  103.8 1.5 %collective-permute-start.26 = (bf16[2,768]{1,0:T(2,128)(2,1)S(1)}, bf16[2,768]{1,0:T(2,128)(2,1)S(1)}, u32[]{:S(2)}, u32[]{:S(2)}) collective-permute-start(bf16[2,768]{1,0:T(2,128)(2,1)S(1)} %get-tuple-element.28), channel_id=1, source_target_pairs={{2,0},{3,1},{4,2},{5,3},{6,4},{7,5},{8,6},{9,7},{10,8},{11,9},{12,... | collective-permute-start | bytes 9224 | tf_op jit(solution)/shard_map/ppermute | solution.py:342
  105.3 1.6 %collective-permute-done.33.refs_6_ = bf16[384,384]{1,0:T(8,128)(2,1)S(1)} collective-permute-done((bf16[384,384]{1,0:T(8,128)(2,1)S(1)}, bf16[384,384]{1,0:T(8,128)(2,1)S(1)}, u32[]{:S(2)}, u32[]{:S(2)}) %collective-permute-start.33) | collective-permute-done | bytes 294944 | tf_op jit(solution)/shard_map/ppermute | solution.py:39
  106.9 5.0 %collective-permute-done.35.refs_8_ = bf16[384,384]{1,0:T(8,128)(2,1)S(1)} collective-permute-done((bf16[384,384]{1,0:T(8,128)(2,1)S(1)}, bf16[384,384]{1,0:T(8,128)(2,1)S(1)}, u32[]{:S(2)}, u32[]{:S(2)}) %collective-permute-start.35) | collective-permute-done | bytes 294944 | tf_op jit(solution)/shard_map/ppermute | solution.py:39
  111.9 5.4 %point.1 = (f32[2,128,1536]{2,1,0:T(8,128)S(1)}, bf16[2,128,1536]{2,1,0:T(8,128)(2,1)S(1)}) custom-call(s32[4]{0:T(128)S(1)} %pad_add_fusion.idx, f32[3,1536]{1,0:T(4,128)S(1)} %copy-done.6, bf16[2,256,768]{2,1,0:T(8,128)(2,1)S(1)} %get-tuple-element.26.merged, bf16[2,768]{1,0:T(2,128)(2,1)S(1)} %collective-permute-done.25.before, ...), custom_call_target="tpu_custom_call" | custom-call | tf_op jit(solution)/shard_map/point/pallas_call | solution.py:273
  117.4 2.3 %collective-permute-done.36 = bf16[2,128,1536]{2,1,0:T(8,128)(2,1)S(1)} collective-permute-done((bf16[2,128,1536]{2,1,0:T(8,128)(2,1)S(1)}, bf16[2,128,1536]{2,1,0:T(8,128)(2,1)S(1)}, u32[]{:S(2)}, u32[]{:S(2)}) %collective-permute-start.36) | collective-permute-done | bytes 786464 | tf_op jit(solution)/shard_map/ppermute | solution.py:31
  119.6 1.1 add_convert_fusion
  (55 shorter events, 0.6 us)
Async XLA Ops:
  0.8 1.7 %copy-start = (bf16[1536,768]{1,0:T(8,128)(2,1)S(1)}, bf16[1536,768]{1,0:T(8,128)(2,1)}, u32[]{:S(2)}) copy-start(bf16[1536,768]{1,0:T(8,128)(2,1)} %wv.1) | copy-start | bytes 7077892
  2.4 1.0 copy-start.2
  3.4 1.1 copy-start.4
  4.6 1.1 copy-start.5
  5.7 4.9 %copy-start.8 = (bf16[1536,96]{0,1:T(8,128)(2,1)S(1)}, bf16[1536,96]{0,1:T(8,128)(2,1)}, u32[]{:S(2)}) copy-start(bf16[1536,96]{0,1:T(8,128)(2,1)} %param.21) | copy-start | bytes 884740
  5.7 5.1 %copy-start.9 = (bf16[96,1536]{1,0:T(8,128)(2,1)S(1)}, bf16[96,1536]{1,0:T(8,128)(2,1)}, u32[]{:S(2)}) copy-start(bf16[96,1536]{1,0:T(8,128)(2,1)} %param.18) | copy-start | bytes 884740
  7.4 3.5 %copy-start.10 = (bf16[80,1536]{1,0:T(8,128)(2,1)S(1)}, bf16[80,1536]{1,0:T(8,128)(2,1)}, u32[]{:S(2)}) copy-start(bf16[80,1536]{1,0:T(8,128)(2,1)} %param.19) | copy-start | bytes 737284
  7.4 4.0 %collective-permute-start = (bf16[128,384]{1,0:T(8,128)(2,1)S(1)}, bf16[128,384]{1,0:T(8,128)(2,1)S(1)}, u32[]{:S(2)}, u32[]{:S(2)}) collective-permute-start(bf16[128,384]{1,0:T(8,128)(2,1)S(1)} %get-tuple-element.19), channel_id=1, source_target_pairs={{0,1},{1,0},{2,3},{3,2},{4,5},{5,4},{6,7},{7,6},{8,9},{9,8},{10,11... | collective-permute-start | bytes 294920 | tf_op jit(solution)/shard_map/ppermute | solution.py:31
  7.9 6.2 %collective-permute-start.1 = (bf16[128,384]{1,0:T(8,128)(2,1)S(1)}, bf16[128,384]{1,0:T(8,128)(2,1)S(1)}, u32[]{:S(2)}, u32[]{:S(2)}) collective-permute-start(bf16[128,384]{1,0:T(8,128)(2,1)S(1)} %get-tuple-element.20), channel_id=1, source_target_pairs={{0,2},{1,3},{2,0},{3,1},{4,6},{5,7},{6,4},{7,5},{8,10},{9,11},{10,... | collective-permute-start | bytes 294920 | tf_op jit(solution)/shard_map/ppermute | solution.py:31
  10.5 5.2 %collective-permute-start.2 = (bf16[128,384]{1,0:T(8,128)(2,1)S(1)}, bf16[128,384]{1,0:T(8,128)(2,1)S(1)}, u32[]{:S(2)}, u32[]{:S(2)}) collective-permute-start(bf16[128,384]{1,0:T(8,128)(2,1)S(1)} %get-tuple-element.21), channel_id=1, source_target_pairs={{0,3},{1,2},{2,1},{3,0},{4,7},{5,6},{6,5},{7,4},{8,11},{9,10},{10,... | collective-permute-start | bytes 294920 | tf_op jit(solution)/shard_map/ppermute | solution.py:31
  10.6 6.8 %collective-permute-start.27 = (bf16[96,768]{1,0:T(8,128)(2,1)S(1)}, bf16[96,768]{1,0:T(8,128)(2,1)S(1)}, u32[]{:S(2)}, u32[]{:S(2)}) collective-permute-start(bf16[96,768]{1,0:T(8,128)(2,1)S(1)} %get-tuple-element.36), channel_id=1, source_target_pairs={{0,1},{1,0},{2,3},{3,2},{4,5},{5,4},{6,7},{7,6},{8,9},{9,8},{10,11... | collective-permute-start | bytes 442376 | tf_op jit(solution)/shard_map/ppermute | solution.py:31
  10.9 8.2 %copy-start.7 = (bf16[2,128,1280]{2,1,0:T(8,128)(2,1)S(1)}, bf16[2,128,1280]{2,1,0:T(8,128)(2,1)}, u32[]{:S(2)}) copy-start(bf16[2,128,1280]{2,1,0:T(8,128)(2,1)} %param.12) | copy-start | bytes 1966084
  10.9 8.7 %collective-permute-start.11 = (bf16[176,768]{1,0:T(8,128)(2,1)S(1)}, bf16[176,768]{1,0:T(8,128)(2,1)S(1)}, u32[]{:S(2)}, u32[]{:S(2)}) collective-permute-start(bf16[176,768]{1,0:T(8,128)(2,1)S(1)} %get-tuple-element.32), channel_id=1, source_target_pairs={{0,1},{1,0},{2,3},{3,2},{4,5},{5,4},{6,7},{7,6},{8,9},{9,8},{10,11... | collective-permute-start | bytes 811016 | tf_op jit(solution)/shard_map/ppermute | solution.py:31
  15.8 11.0 %collective-permute-start.3 = (bf16[512,256]{1,0:T(8,128)(2,1)S(1)}, bf16[512,256]{1,0:T(8,128)(2,1)S(1)}, u32[]{:S(2)}, u32[]{:S(2)}) collective-permute-start(bf16[512,256]{1,0:T(8,128)(2,1)S(1)} %bitcast.19), channel_id=1, source_target_pairs={{0,4},{1,5},{2,6},{3,7},{4,8},{5,9},{6,10},{7,11},{8,12},{9,13},{1... | collective-permute-start | bytes 786440 | tf_op jit(solution)/shard_map/ppermute | solution.py:31
  17.5 5.8 %collective-permute-start.28 = (bf16[192,384]{1,0:T(8,128)(2,1)S(1)}, bf16[192,384]{1,0:T(8,128)(2,1)S(1)}, u32[]{:S(2)}, u32[]{:S(2)}) collective-permute-start(bf16[192,384]{1,0:T(8,128)(2,1)S(1)} %get-tuple-element.34), channel_id=1, source_target_pairs={{0,2},{1,3},{2,0},{3,1},{4,6},{5,7},{6,4},{7,5},{8,10},{9,11},{10,... | collective-permute-start | bytes 442376 | tf_op jit(solution)/shard_map/ppermute | solution.py:31
  19.5 24.9 %collective-permute-start.10 = (bf16[256,1280]{1,0:T(8,128)(2,1)S(1)}, bf16[256,1280]{1,0:T(8,128)(2,1)S(1)}, u32[]{:S(2)}, u32[]{:S(2)}) collective-permute-start(bf16[256,1280]{1,0:T(8,128)(2,1)S(1)} %bitcast.15), channel_id=1, source_target_pairs={{0,1},{1,0},{2,3},{3,2},{4,5},{5,4},{6,7},{7,6},{8,9},{9,8},{10,11... | collective-permute-start | bytes 1966088 | tf_op jit(solution)/shard_map/ppermute | solution.py:31
  19.7 12.9 %collective-permute-start.13 = (bf16[352,384]{1,0:T(8,128)(2,1)S(1)}, bf16[352,384]{1,0:T(8,128)(2,1)S(1)}, u32[]{:S(2)}, u32[]{:S(2)}) collective-permute-start(bf16[352,384]{1,0:T(8,128)(2,1)S(1)} %fusion.6), channel_id=1, source_target_pairs={{0,4},{1,5},{2,6},{3,7},{4,8},{5,9},{6,10},{7,11},{8,12},{9,13},{1... | collective-permute-start | bytes 811016 | tf_op jit(solution)/shard_map/ppermute | solution.py:31
  23.3 41.1 %copy-start.3 = (bf16[2,64,1536]{2,1,0:T(8,128)(2,1)S(1)}, bf16[2,64,1536]{2,1,0:T(8,128)(2,1)}, u32[]{:S(2)}) copy-start(bf16[2,64,1536]{2,1,0:T(8,128)(2,1)} %param.11) | copy-start | bytes 1179652
  23.3 41.1 %copy-start.1 = (bf16[768,1536]{1,0:T(8,128)(2,1)S(1)}, bf16[768,1536]{1,0:T(8,128)(2,1)}, u32[]{:S(2)}) copy-start(bf16[768,1536]{1,0:T(8,128)(2,1)} %wo.1) | copy-start | bytes 7077892
  23.3 15.5 %collective-permute-start.30 = (bf16[384,384]{1,0:T(8,128)(2,1)S(1)}, bf16[384,384]{1,0:T(8,128)(2,1)S(1)}, u32[]{:S(2)}, u32[]{:S(2)}) collective-permute-start(bf16[384,384]{1,0:T(8,128)(2,1)S(1)} %pad_maximum_fusion.2), channel_id=1, source_target_pairs={{0,4},{1,5},{2,6},{3,7},{4,8},{5,9},{6,10},{7,11},{8,12},{9,13},{1... | collective-permute-start | bytes 884744 | tf_op jit(solution)/shard_map/ppermute | solution.py:31
  26.7 17.7 %collective-permute-start.4 = (bf16[512,256]{1,0:T(8,128)(2,1)S(1)}, bf16[512,256]{1,0:T(8,128)(2,1)S(1)}, u32[]{:S(2)}, u32[]{:S(2)}) collective-permute-start(bf16[512,256]{1,0:T(8,128)(2,1)S(1)} %collective-permute-done.3.refs_5_), channel_id=1, source_target_pairs={{0,4},{1,5},{2,6},{3,7},{4,8},{5,9},{6,10},{7,11},{8,12},{9,13},{1... | collective-permute-start | bytes 786440 | tf_op jit(solution)/shard_map/ppermute | solution.py:31
  26.8 30.5 %collective-permute-start.12 = (bf16[352,768]{1,0:T(8,128)(2,1)S(1)}, bf16[352,768]{1,0:T(8,128)(2,1)S(1)}, u32[]{:S(2)}, u32[]{:S(2)}) collective-permute-start(bf16[352,768]{1,0:T(8,128)(2,1)S(1)} %pad_maximum_fusion.refs_0_), channel_id=1, source_target_pairs={{0,2},{1,3},{2,0},{3,1},{4,6},{5,7},{6,4},{7,5},{8,10},{9,11},{10,... | collective-permute-start | bytes 1622024 | tf_op jit(solution)/shard_map/ppermute | solution.py:31
  32.5 17.7 %collective-permute-start.17 = (bf16[352,384]{1,0:T(8,128)(2,1)S(1)}, bf16[352,384]{1,0:T(8,128)(2,1)S(1)}, u32[]{:S(2)}, u32[]{:S(2)}) collective-permute-start(bf16[352,384]{1,0:T(8,128)(2,1)S(1)} %collective-permute-done.13.refs_2_), channel_id=1, source_target_pairs={{0,4},{1,5},{2,6},{3,7},{4,8},{5,9},{6,10},{7,11},{8,12},{9,13},{1... | collective-permute-start | bytes 811016 | tf_op jit(solution)/shard_map/ppermute | solution.py:31
  38.8 18.3 %collective-permute-start.14 = (bf16[352,384]{1,0:T(8,128)(2,1)S(1)}, bf16[352,384]{1,0:T(8,128)(2,1)S(1)}, u32[]{:S(2)}, u32[]{:S(2)}) collective-permute-start(bf16[352,384]{1,0:T(8,128)(2,1)S(1)} %collective-permute-done.13.refs_2_), channel_id=1, source_target_pairs={{0,2},{1,3},{2,0},{3,1},{4,6},{5,7},{6,4},{7,5},{8,10},{9,11},{10,... | collective-permute-start | bytes 811016 | tf_op jit(solution)/shard_map/ppermute | solution.py:31
  44.5 11.4 %collective-permute-start.5 = (bf16[512,256]{1,0:T(8,128)(2,1)S(1)}, bf16[512,256]{1,0:T(8,128)(2,1)S(1)}, u32[]{:S(2)}, u32[]{:S(2)}) collective-permute-start(bf16[512,256]{1,0:T(8,128)(2,1)S(1)} %collective-permute-done.4.refs_6_), channel_id=1, source_target_pairs={{0,4},{1,5},{2,6},{3,7},{4,8},{5,9},{6,10},{7,11},{8,12},{9,13},{1... | collective-permute-start | bytes 786440 | tf_op jit(solution)/shard_map/ppermute | solution.py:31
  44.5 14.4 %collective-permute-start.15 = (bf16[352,384]{1,0:T(8,128)(2,1)S(1)}, bf16[352,384]{1,0:T(8,128)(2,1)S(1)}, u32[]{:S(2)}, u32[]{:S(2)}) collective-permute-start(bf16[352,384]{1,0:T(8,128)(2,1)S(1)} %collective-permute-done.13.refs_2_), channel_id=1, source_target_pairs={{0,16},{16,0},{1,17},{17,1},{2,18},{18,2},{3,19},{19,3},{4,20},{20... | collective-permute-start | bytes 811016 | tf_op jit(solution)/shard_map/ppermute | solution.py:39
  50.2 15.5 %collective-permute-start.32 = (bf16[384,384]{1,0:T(8,128)(2,1)S(1)}, bf16[384,384]{1,0:T(8,128)(2,1)S(1)}, u32[]{:S(2)}, u32[]{:S(2)}) collective-permute-start(bf16[384,384]{1,0:T(8,128)(2,1)S(1)} %collective-permute-done.30.refs_3_), channel_id=1, source_target_pairs={{0,4},{1,5},{2,6},{3,7},{4,8},{5,9},{6,10},{7,11},{8,12},{9,13},{1... | collective-permute-start | bytes 884744 | tf_op jit(solution)/shard_map/ppermute | solution.py:31
  55.9 11.6 %collective-permute-start.21 = (bf16[352,384]{1,0:T(8,128)(2,1)S(1)}, bf16[352,384]{1,0:T(8,128)(2,1)S(1)}, u32[]{:S(2)}, u32[]{:S(2)}) collective-permute-start(bf16[352,384]{1,0:T(8,128)(2,1)S(1)} %collective-permute-done.17.refs_6_), channel_id=1, source_target_pairs={{0,4},{1,5},{2,6},{3,7},{4,8},{5,9},{6,10},{7,11},{8,12},{9,13},{1... | collective-permute-start | bytes 811016 | tf_op jit(solution)/shard_map/ppermute | solution.py:31
  57.1 2.0 %collective-permute-start.6 = (bf16[128,256]{1,0:T(8,128)(2,1)S(1)}, bf16[128,256]{1,0:T(8,128)(2,1)S(1)}, u32[]{:S(2)}, u32[]{:S(2)}) collective-permute-start(bf16[128,256]{1,0:T(8,128)(2,1)S(1)} %get-tuple-element.23), channel_id=1, source_target_pairs={{0,1},{1,0},{2,3},{3,2},{4,5},{5,4},{6,7},{7,6},{8,9},{9,8},{10,11... | collective-permute-start | bytes 196616 | tf_op jit(solution)/shard_map/ppermute | solution.py:31
  57.2 4.5 %collective-permute-start.7 = (bf16[128,256]{1,0:T(8,128)(2,1)S(1)}, bf16[128,256]{1,0:T(8,128)(2,1)S(1)}, u32[]{:S(2)}, u32[]{:S(2)}) collective-permute-start(bf16[128,256]{1,0:T(8,128)(2,1)S(1)} %get-tuple-element.24), channel_id=1, source_target_pairs={{0,2},{1,3},{2,0},{3,1},{4,6},{5,7},{6,4},{7,5},{8,10},{9,11},{10,... | collective-permute-start | bytes 196616 | tf_op jit(solution)/shard_map/ppermute | solution.py:31
  58.9 4.4 %collective-permute-start.8 = (bf16[128,256]{1,0:T(8,128)(2,1)S(1)}, bf16[128,256]{1,0:T(8,128)(2,1)S(1)}, u32[]{:S(2)}, u32[]{:S(2)}) collective-permute-start(bf16[128,256]{1,0:T(8,128)(2,1)S(1)} %get-tuple-element.25), channel_id=1, source_target_pairs={{0,3},{1,2},{2,1},{3,0},{4,7},{5,6},{6,5},{7,4},{8,11},{9,10},{10,... | collective-permute-start | bytes 196616 | tf_op jit(solution)/shard_map/ppermute | solution.py:31
  59.1 10.0 %collective-permute-start.18 = (bf16[352,384]{1,0:T(8,128)(2,1)S(1)}, bf16[352,384]{1,0:T(8,128)(2,1)S(1)}, u32[]{:S(2)}, u32[]{:S(2)}) collective-permute-start(bf16[352,384]{1,0:T(8,128)(2,1)S(1)} %collective-permute-done.17.refs_6_), channel_id=1, source_target_pairs={{0,2},{1,3},{2,0},{3,1},{4,6},{5,7},{6,4},{7,5},{8,10},{9,11},{10,... | collective-permute-start | bytes 811016 | tf_op jit(solution)/shard_map/ppermute | solution.py:31
  61.7 9.4 %collective-permute-start.16 = (bf16[352,384]{1,0:T(8,128)(2,1)S(1)}, bf16[352,384]{1,0:T(8,128)(2,1)S(1)}, u32[]{:S(2)}, u32[]{:S(2)}) collective-permute-start(bf16[352,384]{1,0:T(8,128)(2,1)S(1)} %collective-permute-done.14.refs_3_), channel_id=1, source_target_pairs={{0,16},{16,0},{1,17},{17,1},{2,18},{18,2},{3,19},{19,3},{4,20},{20... | collective-permute-start | bytes 811016 | tf_op jit(solution)/shard_map/ppermute | solution.py:39
  63.3 13.6 %collective-permute-start.19 = (bf16[352,384]{1,0:T(8,128)(2,1)S(1)}, bf16[352,384]{1,0:T(8,128)(2,1)S(1)}, u32[]{:S(2)}, u32[]{:S(2)}) collective-permute-start(bf16[352,384]{1,0:T(8,128)(2,1)S(1)} %collective-permute-done.17.refs_6_), channel_id=1, source_target_pairs={{0,16},{16,0},{1,17},{17,1},{2,18},{18,2},{3,19},{19,3},{4,20},{20... | collective-permute-start | bytes 811016 | tf_op jit(solution)/shard_map/ppermute | solution.py:39
  65.8 15.5 %collective-permute-start.9 = (bf16[128,1536]{1,0:T(8,128)(2,1)S(1)}, bf16[128,1536]{1,0:T(8,128)(2,1)S(1)}, u32[]{:S(2)}, u32[]{:S(2)}) collective-permute-start(bf16[128,1536]{1,0:T(8,128)(2,1)S(1)} %output.1.act_own), channel_id=1, source_target_pairs={{0,1},{1,0},{2,3},{3,2},{4,5},{5,4},{6,7},{7,6},{8,9},{9,8},{10,11... | collective-permute-start | bytes 1179656 | tf_op jit(solution)/shard_map/ppermute | solution.py:31
  67.5 11.0 %collective-permute-start.22 = (bf16[352,384]{1,0:T(8,128)(2,1)S(1)}, bf16[352,384]{1,0:T(8,128)(2,1)S(1)}, u32[]{:S(2)}, u32[]{:S(2)}) collective-permute-start(bf16[352,384]{1,0:T(8,128)(2,1)S(1)} %collective-permute-done.21.refs_10_), channel_id=1, source_target_pairs={{0,2},{1,3},{2,0},{3,1},{4,6},{5,7},{6,4},{7,5},{8,10},{9,11},{10,... | collective-permute-start | bytes 811016 | tf_op jit(solution)/shard_map/ppermute | solution.py:31
  69.1 10.8 %collective-permute-start.34 = (bf16[384,384]{1,0:T(8,128)(2,1)S(1)}, bf16[384,384]{1,0:T(8,128)(2,1)S(1)}, u32[]{:S(2)}, u32[]{:S(2)}) collective-permute-start(bf16[384,384]{1,0:T(8,128)(2,1)S(1)} %collective-permute-done.32.refs_5_), channel_id=1, source_target_pairs={{0,4},{1,5},{2,6},{3,7},{4,8},{5,9},{6,10},{7,11},{8,12},{9,13},{1... | collective-permute-start | bytes 884744 | tf_op jit(solution)/shard_map/ppermute | solution.py:31
  71.1 11.6 %collective-permute-start.20 = (bf16[352,384]{1,0:T(8,128)(2,1)S(1)}, bf16[352,384]{1,0:T(8,128)(2,1)S(1)}, u32[]{:S(2)}, u32[]{:S(2)}) collective-permute-start(bf16[352,384]{1,0:T(8,128)(2,1)S(1)} %collective-permute-done.18.refs_7_), channel_id=1, source_target_pairs={{0,16},{16,0},{1,17},{17,1},{2,18},{18,2},{3,19},{19,3},{4,20},{20... | collective-permute-start | bytes 811016 | tf_op jit(solution)/shard_map/ppermute | solution.py:39
  76.9 11.6 %collective-permute-start.23 = (bf16[352,384]{1,0:T(8,128)(2,1)S(1)}, bf16[352,384]{1,0:T(8,128)(2,1)S(1)}, u32[]{:S(2)}, u32[]{:S(2)}) collective-permute-start(bf16[352,384]{1,0:T(8,128)(2,1)S(1)} %collective-permute-done.21.refs_10_), channel_id=1, source_target_pairs={{0,16},{16,0},{1,17},{17,1},{2,18},{18,2},{3,19},{19,3},{4,20},{20... | collective-permute-start | bytes 811016 | tf_op jit(solution)/shard_map/ppermute | solution.py:39
  78.5 15.8 %collective-permute-start.24 = (bf16[352,384]{1,0:T(8,128)(2,1)S(1)}, bf16[352,384]{1,0:T(8,128)(2,1)S(1)}, u32[]{:S(2)}, u32[]{:S(2)}) collective-permute-start(bf16[352,384]{1,0:T(8,128)(2,1)S(1)} %collective-permute-done.22.refs_11_), channel_id=1, source_target_pairs={{0,16},{16,0},{1,17},{17,1},{2,18},{18,2},{3,19},{19,3},{4,20},{20... | collective-permute-start | bytes 811016 | tf_op jit(solution)/shard_map/ppermute | solution.py:39
  79.8 25.5 %collective-permute-start.31 = (bf16[384,384]{1,0:T(8,128)(2,1)S(1)}, bf16[384,384]{1,0:T(8,128)(2,1)S(1)}, u32[]{:S(2)}, u32[]{:S(2)}) collective-permute-start(bf16[384,384]{1,0:T(8,128)(2,1)S(1)} %collective-permute-done.30.refs_3_), channel_id=1, source_target_pairs={{0,16},{16,0},{1,17},{17,1},{2,18},{18,2},{3,19},{19,3},{4,20},{20... | collective-permute-start | bytes 884744 | tf_op jit(solution)/shard_map/ppermute | solution.py:39
  81.3 25.6 %collective-permute-start.33 = (bf16[384,384]{1,0:T(8,128)(2,1)S(1)}, bf16[384,384]{1,0:T(8,128)(2,1)S(1)}, u32[]{:S(2)}, u32[]{:S(2)}) collective-permute-start(bf16[384,384]{1,0:T(8,128)(2,1)S(1)} %collective-permute-done.32.refs_5_), channel_id=1, source_target_pairs={{0,16},{16,0},{1,17},{17,1},{2,18},{18,2},{3,19},{19,3},{4,20},{20... | collective-permute-start | bytes 884744 | tf_op jit(solution)/shard_map/ppermute | solution.py:39
  82.7 29.2 %collective-permute-start.35 = (bf16[384,384]{1,0:T(8,128)(2,1)S(1)}, bf16[384,384]{1,0:T(8,128)(2,1)S(1)}, u32[]{:S(2)}, u32[]{:S(2)}) collective-permute-start(bf16[384,384]{1,0:T(8,128)(2,1)S(1)} %collective-permute-done.34.refs_7_), channel_id=1, source_target_pairs={{0,16},{16,0},{1,17},{17,1},{2,18},{18,2},{3,19},{19,3},{4,20},{20... | collective-permute-start | bytes 884744 | tf_op jit(solution)/shard_map/ppermute | solution.py:39
  88.5 23.4 %copy-start.6 = (f32[3,1536]{1,0:T(4,128)S(1)}, f32[3,1536]{1,0:T(4,128)}, u32[]{:S(2)}) copy-start(f32[3,1536]{1,0:T(4,128)} %depth.1) | copy-start | bytes 55300
  88.5 15.3 %collective-permute-start.29 = (bf16[192,384]{1,0:T(8,128)(2,1)S(1)}, bf16[192,384]{1,0:T(8,128)(2,1)S(1)}, u32[]{:S(2)}, u32[]{:S(2)}) collective-permute-start(bf16[192,384]{1,0:T(8,128)(2,1)S(1)} %get-tuple-element.33), channel_id=1, source_target_pairs={{0,2},{1,3},{2,0},{3,1},{4,6},{5,7},{6,4},{7,5},{8,10},{9,11},{10,... | collective-permute-start | bytes 442376 | tf_op jit(solution)/shard_map/ppermute | solution.py:31
  99.8 12.1 %collective-permute-start.25 = (bf16[2,768]{1,0:T(2,128)(2,1)S(1)}, bf16[2,768]{1,0:T(2,128)(2,1)S(1)}, u32[]{:S(2)}, u32[]{:S(2)}) collective-permute-start(bf16[2,768]{1,0:T(2,128)(2,1)S(1)} %get-tuple-element.27), channel_id=1, source_target_pairs={{0,2},{1,3},{2,4},{3,5},{4,6},{5,7},{6,8},{7,9},{8,10},{9,11},{10,... | collective-permute-start | bytes 9224 | tf_op jit(solution)/shard_map/ppermute | solution.py:341
  103.8 8.1 %collective-permute-start.26 = (bf16[2,768]{1,0:T(2,128)(2,1)S(1)}, bf16[2,768]{1,0:T(2,128)(2,1)S(1)}, u32[]{:S(2)}, u32[]{:S(2)}) collective-permute-start(bf16[2,768]{1,0:T(2,128)(2,1)S(1)} %get-tuple-element.28), channel_id=1, source_target_pairs={{2,0},{3,1},{4,2},{5,3},{6,4},{7,5},{8,6},{9,7},{10,8},{11,9},{12,... | collective-permute-start | bytes 9224 | tf_op jit(solution)/shard_map/ppermute | solution.py:342
  117.3 2.4 %collective-permute-start.36 = (bf16[2,128,1536]{2,1,0:T(8,128)(2,1)S(1)}, bf16[2,128,1536]{2,1,0:T(8,128)(2,1)S(1)}, u32[]{:S(2)}, u32[]{:S(2)}) collective-permute-start(bf16[2,128,1536]{2,1,0:T(8,128)(2,1)S(1)} %get-tuple-element.30), channel_id=1, source_target_pairs={{0,1},{1,0},{2,3},{3,2},{4,5},{5,4},{6,7},{7,6},{8,9},{9,8},{10,11... | collective-permute-start | bytes 2359304 | tf_op jit(solution)/shard_map/ppermute | solution.py:31

commit v2 on v1

--- a/solution.py
+++ b/solution.py
@@ -14,8 +14,41 @@
 BF16 = jnp.bfloat16
 ANY = pl.BlockSpec(memory_space=pl.ANY)
 VMEM = pl.BlockSpec(memory_space=pltpu.VMEM)
+HBM = pl.BlockSpec(memory_space=pltpu.HBM)
 SMEM = pl.BlockSpec(memory_space=pltpu.SMEM)
-LIMIT = pltpu.CompilerParams(vmem_limit_bytes=40 * 1024 * 1024)
+LIMIT = pltpu.CompilerParams(vmem_limit_bytes=20 * 1024 * 1024)
+
+WIDTH = 5
+CUMULATIVE = False
+SENDS = (
+    ("u1", "z", "u0"),
+    ("qy", "y", "py"),
+    ("qcy", "cy", "pcy"),
+    ("qc", "c", "pc"),
+    ("k1", "z", "k0"),
+    ("b1", "y", "u1"),
+    ("u2", "z", "u1"),
+    ("c1", "x", "u1"),
+    ("b0", "y", "u0"),
+    ("skipc", "c", "skip"),
+    ("k2", "z", "k1"),
+    ("d1", "x", "b1"),
+    ("c2", "x", "u2"),
+    ("b2", "y", "u2"),
+    ("u3", "z", "u2"),
+    ("k3", "z", "k2"),
+    ("d2", "x", "b2"),
+    ("b3", "y", "u3"),
+    ("mc", "c", "oc"),
+    ("my", "y", "oy"),
+    ("mcy", "cy", "ocy"),
+    ("c3", "z", "c2"),
+    ("d0", "y", "c0"),
+    ("actc", "c", "act"),
+    ("before", "up", "high"),
+    ("after", "down", "low"),
+    ("d3", "x", "b3"),
+)
 
 POS = 16
 C_SWAP = [(i, i ^ 1) for i in range(POS)]
@@ -39,12 +72,24 @@
     return lax.ppermute(v, "group", X_SWAP)
 
 
-def project_kernel(idx, acts, gain, wq, wk, wv, *outs):
+def project_kernel(idx, acts_hbm, gain, wq_hbm, wk_hbm, wv_hbm, *refs):
+    outs, (acts, wq, wk, wv, sems) = refs[:4], refs[4:]
+    copies = [
+        pltpu.make_async_copy(src, dst, sems.at[n])
+        for n, (src, dst) in enumerate(
+            ((acts_hbm, acts), (wq_hbm, wq), (wk_hbm, wk), (wv_hbm, wv))
+        )
+    ]
+    for copy in copies:
+        copy.start()
+    copies.pop(0).wait()
     a = acts[...].astype(F32)
     centre = a - jnp.mean(a, axis=-1, keepdims=True)
     normed = (
         centre * lax.rsqrt(jnp.mean(centre * centre, axis=-1, keepdims=True) + 1e-05) * gain[...]
     ).astype(BF16)
+    for copy in copies:
+        copy.wait()
     q = (jnp.dot(normed, wq[...], preferred_element_type=F32) * HK ** (-0.5))
     k = jnp.dot(normed, wk[...], preferred_element_type=F32)
     v = jnp.dot(normed, wv[...], preferred_element_type=F32)
@@ -76,8 +121,15 @@
     return pl.pallas_call(
         project_kernel,
         out_shape=[jax.ShapeDtypeStruct((rows, 384), BF16)] * HEADS,
-        in_specs=[SMEM] + [VMEM] * 5,
+        in_specs=[SMEM, HBM, VMEM] + [HBM] * 3,
         out_specs=[VMEM] * HEADS,
+        scratch_shapes=[
+            pltpu.VMEM((128, 1536), BF16),
+            pltpu.VMEM((1536, 256), BF16),
+            pltpu.VMEM((1536, 256), BF16),
+            pltpu.VMEM((1536, 768), BF16),
+            pltpu.SemaphoreType.DMA((4,)),
+        ],
         compiler_params=LIMIT,
         name="project",
     )(idx, acts, gain, wq, wk, wv)
@@ -137,25 +189,6 @@
     )(idx, acts, wo, *mixed)
 
 
-def start_all(copies, sems):
-    started = []
-    for n, (src, dst) in enumerate(copies):
-        copy = pltpu.make_async_copy(src, dst, sems.at[n])
-        copy.start()
-        started.append(copy)
-    return started
-
-
-def place(ref, blocks, columns, dst, height, pos, col):
-    return [
-        (
-            ref.at[pl.ds(row, height), columns],
-            dst.at[pl.ds(pl.multiple_of(p * height, height), height), col],
-        )
-        for row, p in zip(blocks, pos)
-    ]
-
-
 ALL = slice(None)
 
 
@@ -163,27 +196,34 @@
     return pl.ds(pl.multiple_of(x * 384, 384), 384)
 
 
-def merge_kernel(idx, act_own, act_oth, skip_own, skip_oth, *refs):
-    pieces, (merged, first, last), (wl, ws, act, skip, sems) = refs[:14], refs[14:17], refs[17:]
+def rows_of(p, height):
+    return pl.ds(pl.multiple_of(p * height, height), height)
+
+
+A_ROWS = 352
+
+
+def merge_kernel(idx, act_own, act_oth, skip_own, skip_oth, before, after, *refs):
+    pieces, (merged, ends), (wl, ws, act, skip) = refs[:15], refs[15:17], refs[17:]
     x, y, z, c = idx[0], idx[1], idx[2], idx[3]
-    copies = []
 
     def add(ref, zz, yy, col):
-        pos = [4 * zz + 2 * yy + c, 4 * zz + 2 * yy + 1 - c]
-        copies.extend(place(ref, (0, 176), ALL, wl, 96, pos, col))
-        copies.extend(place(ref, (96, 272), ALL, ws, 80, pos, col))
-
-    own, yown = pieces[:2]
+        for n, cc in ((0, c), (176, 1 - c)):
+            p = 4 * zz + 2 * yy + cc
+            wl[rows_of(p, 96), col] = ref[n : n + 96, :]
+            ws[rows_of(p, 80), col] = ref[n + 96 : n + 176, :]
+
+    own, b0, xb0 = pieces[:3]
     add(own, z, y, ALL)
-    add(yown, z, 1 - y, ALL)
+    add(b0, z, 1 - y, quarter(x))
+    add(xb0, z, 1 - y, quarter(1 - x))
     for k in range(1, 4):
         zz = lax.rem(z + 4 - k, 4)
-        a, b, xa, xb = pieces[2 + 4 * (k - 1) : 2 + 4 * k]
+        a, b, xa, xb = pieces[4 * k - 1 : 4 * k + 3]
         add(a, zz, y, quarter(x))
         add(b, zz, 1 - y, quarter(x))
         add(xa, zz, y, quarter(1 - x))
         add(xb, zz, 1 - y, quarter(1 - x))
-    started = start_all(copies, sems)
     for s in range(2):
         for src_a, src_s, cc in ((act_own, skip_own, c), (act_oth, skip_oth, 1 - c)):
             act[pl.ds(pl.multiple_of(128 * s + 64 * cc, 64), 64), :] = src_a[
@@ -192,104 +232,215 @@
             skip[pl.ds(pl.multiple_of(256 * s + 128 * cc, 128), 128), :] = src_s[
                 pl.ds(128 * s, 128), :
             ]
+    act[256:272, :] = jnp.concatenate(
+        [before[:, :1536], after[:, :1536], jnp.zeros((12, 1536), BF16)], axis=0
+    )
+    skip[512:528, :] = jnp.concatenate(
+        [before[:, 1536:], after[:, 1536:], jnp.zeros((12, 1280), BF16)], axis=0
+    )
     twice = (
         lax.broadcasted_iota(jnp.int32, (256, 128), 0) // 2
         == lax.broadcasted_iota(jnp.int32, (256, 128), 1)
     ).astype(BF16)
-    for copy in started:
-        copy.wait()
     lifted = jnp.dot(act[...], wl[...], preferred_element_type=F32).astype(BF16)
+    terms = jnp.dot(skip[...], ws[...], preferred_element_type=F32)
     for s in range(2):
-        term = jnp.dot(
-            skip[pl.ds(256 * s, 256), :], ws[...], preferred_element_type=F32
-        )
+        term = terms[256 * s : 256 * (s + 1)]
         raised = jnp.dot(twice, lifted[128 * s : 128 * (s + 1)], preferred_element_type=F32)
         total = (raised + term).astype(BF16)
         merged[s, :, :] = total
-        first[s : s + 1, :] = total[0:1, :]
-        last[s : s + 1, :] = total[255:256, :]
-
-
-def merge(idx, act_own, act_oth, skip_own, skip_oth, pieces):
+    ends[...] = (lifted[256:272].astype(F32) + terms[512:528]).astype(BF16)
+
+
+def merge(idx, act_own, act_oth, skip_own, skip_oth, before, after, pieces):
     return pl.pallas_call(
         merge_kernel,
         out_shape=[
             jax.ShapeDtypeStruct((2, 256, 768), BF16),
-            jax.ShapeDtypeStruct((2, 768), BF16),
-            jax.ShapeDtypeStruct((2, 768), BF16),
+            jax.ShapeDtypeStruct((16, 768), BF16),
         ],
-        in_specs=[SMEM] + [VMEM] * 4 + [ANY] * len(pieces),
-        out_specs=[VMEM] * 3,
+        in_specs=[SMEM] + [VMEM] * (6 + len(pieces)),
+        out_specs=[VMEM] * 2,
         scratch_shapes=[
             pltpu.VMEM((1536, 768), BF16),
             pltpu.VMEM((1280, 768), BF16),
-            pltpu.VMEM((256, 1536), BF16),
-            pltpu.VMEM((512, 1280), BF16),
-            pltpu.SemaphoreType.DMA((56,)),
+            pltpu.VMEM((272, 1536), BF16),
+            pltpu.VMEM((528, 1280), BF16),
         ],
         compiler_params=LIMIT,
         name="merge",
-    )(idx, act_own, act_oth, skip_own, skip_oth, *pieces)
-
-
-def point_kernel(idx, depth, merged, before, after, *refs):
-    pieces, (own, oth), (wp, spread, sems) = refs[:9], refs[9:11], refs[11:]
+    )(idx, act_own, act_oth, skip_own, skip_oth, before, after, *pieces)
+
+
+def point_kernel(idx, depth, merged, ends, *refs):
+    pieces, (own, oth), (wp, spread) = refs[:15], refs[15:17], refs[17:]
     x, y, z, c = idx[0], idx[1], idx[2], idx[3]
-    copies = []
-
-    def add(ref, zz, yy, col, row=0):
-        pos = [4 * zz + 2 * yy + c, 4 * zz + 2 * yy + 1 - c]
-        copies.extend(place(ref, (row, row + 96), ALL, wp, 96, pos, col))
-
-    add(pieces[0], z, y, ALL)
-    add(pieces[1], z, 1 - y, quarter(x))
-    add(pieces[2], z, 1 - y, quarter(1 - x))
+
+    def add(ref, zz, yy, col):
+        base = A_ROWS
+        for n, cc in ((base, c), (base + 96, 1 - c)):
+            wp[rows_of(4 * zz + 2 * yy + cc, 96), col] = ref[n : n + 96, :]
+
+    full, b0, xb0 = pieces[:3]
+    add(full, z, y, ALL)
+    add(b0, z, 1 - y, quarter(x))
+    add(xb0, z, 1 - y, quarter(1 - x))
     for k in range(1, 4):
         zz = lax.rem(z + 4 - k, 4)
-        for ref, col in ((pieces[2 * k + 1], quarter(x)), (pieces[2 * k + 2], quarter(1 - x))):
-            add(ref, zz, y, col)
-            add(ref, zz, 1 - y, col, 192)
-    started = start_all(copies, sems)
+        a, b, xa, xb = pieces[4 * k - 1 : 4 * k + 3]
+        add(a, zz, y, quarter(x))
+        add(b, zz, 1 - y, quarter(x))
+        add(xa, zz, y, quarter(1 - x))
+        add(xb, zz, 1 - y, quarter(1 - x))
     taps = depth[:, pl.ds(pl.multiple_of(c * 768, 768), 768)]
     row = lax.broadcasted_iota(jnp.int32, (256, 768), 0)
     for s in range(2):
         here = merged[s, :, :].astype(F32)
-        up = jnp.where(row == 0, before[s : s + 1, :].astype(F32), pltpu.roll(here, 1, 0))
-        down = jnp.where(row == 255, after[s : s + 1, :].astype(F32), pltpu.roll(here, 255, 0))
+        up = jnp.where(row == 0, ends[s : s + 1, :].astype(F32), pltpu.roll(here, 1, 0))
+        down = jnp.where(row == 255, ends[s + 2 : s + 3, :].astype(F32), pltpu.roll(here, 255, 0))
         spread[pl.ds(256 * s, 256), :] = (
             taps[0:1] * up + taps[1:2] * here + taps[2:3] * down
         ).astype(BF16)
-    for copy in started:
-        copy.wait()
-    for s in range(2):
-        for out, cc in ((oth, 1 - c), (own, c)):
-            part = spread[pl.ds(pl.multiple_of(256 * s + 128 * cc, 128), 128), :]
-            out[s, :, :] = lax.dot_general(
-                part, wp[...], (((1,), (1,)), ((), ())), preferred_element_type=F32
-            ).astype(out.dtype)
-
-
-def point(idx, depth, merged, before, after, pieces):
+    for out, cc in ((oth, 1 - c), (own, c)):
+        part = jnp.concatenate(
+            [
+                spread[pl.ds(pl.multiple_of(256 * s + 128 * cc, 128), 128), :]
+                for s in range(2)
+            ],
+            axis=0,
+        )
+        out[...] = (
+            lax.dot_general(part, wp[...], (((1,), (1,)), ((), ())), preferred_element_type=F32)
+            .astype(out.dtype)
+            .reshape(out.shape)
+        )
+
+
+def point(idx, depth, merged, ends, pieces):
     return pl.pallas_call(
         point_kernel,
         out_shape=[
             jax.ShapeDtypeStruct((2, 128, 1536), F32),
             jax.ShapeDtypeStruct((2, 128, 1536), BF16),
         ],
-        in_specs=[SMEM] + [VMEM] * 4 + [ANY] * len(pieces),
+        in_specs=[SMEM] + [VMEM] * (3 + len(pieces)),
         out_specs=[VMEM] * 2,
         scratch_shapes=[
             pltpu.VMEM((1536, 768), BF16),
             pltpu.VMEM((512, 768), BF16),
-            pltpu.SemaphoreType.DMA((30,)),
         ],
         compiler_params=LIMIT,
         name="point",
-    )(idx, depth, merged, before, after, *pieces)
-
-
-def columns(v, i, width):
-    return lax.dynamic_slice_in_dim(v, i * width, width, axis=1)
+    )(idx, depth, merged, ends, *pieces)
+
+
+def behind(v, *tokens):
+    return lax.optimization_barrier((v,) + tokens)[0]
+
+
+class Plan:
+    def __init__(self, width, makers):
+        self.width, self.makers, self.made, self.done = width, makers, {}, []
+
+    def __getitem__(self, name):
+        if name not in self.made:
+            self.made[name] = self.makers[name]()
+        return self.made[name]
+
+    def send(self, how, name):
+        v = self[name]
+        if len(self.done) >= self.width:
+            late = self.done[: len(self.done) - self.width + 1]
+            v = behind(v, *(late if CUMULATIVE else late[-1:]))
+        got = how(v)
+        if how is not c_swap:
+            self.done.append(got)
+        return got
+
+
+def in_hbm(v):
+    return pltpu.with_memory_space_constraint(v, pltpu.HBM)
+
+
+def split_kernel(idx, wl, ws, wp, keep, send, sems):
+    c = idx[3]
+    copies = []
+    for out, cc in ((send, 1 - c), (keep, c)):
+        cols = pl.ds(pl.multiple_of(768 * cc, 768), 768)
+        for src, lo, hi in ((wl, 0, 96), (ws, 96, 176), (wp, 176, 272)):
+            copies.append(
+                pltpu.make_async_copy(src.at[:, cols], out.at[lo:hi], sems.at[len(copies)])
+            )
+    for copy in copies:
+        copy.start()
+    for copy in copies:
+        copy.wait()
+
+
+def split(idx, wl, ws, wp):
+    return pl.pallas_call(
+        split_kernel,
+        out_shape=[jax.ShapeDtypeStruct((272, 768), BF16)] * 2,
+        in_specs=[SMEM] + [HBM] * 3,
+        out_specs=[VMEM] * 2,
+        scratch_shapes=[
+            pltpu.SemaphoreType.DMA((6,)),
+        ],
+        compiler_params=LIMIT,
+        name="split",
+    )(idx, wl, ws, wp)
+
+
+def join_kernel(idx, keep, got, full, quart, rest):
+    x = idx[0]
+    for n, ref in enumerate((keep, got)):
+        for dst, src in (
+            (slice(176 * n, 176 * (n + 1)), slice(0, 176)),
+            (slice(352 + 96 * n, 352 + 96 * (n + 1)), slice(176, 272)),
+        ):
+            full[dst, :] = ref[src, :]
+            quart[dst, :] = ref[src, quarter(x)]
+            rest[dst, :] = ref[src, quarter(1 - x)]
+
+
+def join(idx, keep, got):
+    return pl.pallas_call(
+        join_kernel,
+        out_shape=[
+            jax.ShapeDtypeStruct(shape, BF16) for shape in ((544, 768), (544, 384), (544, 384))
+        ],
+        in_specs=[SMEM] + [VMEM] * 2,
+        out_specs=[VMEM] * 3,
+        compiler_params=LIMIT,
+        name="join",
+    )(idx, keep, got)
+
+
+def edges_kernel(idx, act_own, act_oth, skip_own, skip_oth, low, high):
+    c = idx[3]
+    for first, last, mine in (
+        ((act_own, skip_own), (act_oth, skip_oth), 0),
+        ((act_oth, skip_oth), (act_own, skip_own), 1),
+    ):
+
+        @pl.when(c == mine)
+        def _():
+            for s in range(2):
+                for cols, n, rows in ((slice(0, 1536), 0, 64), (slice(1536, 2816), 1, 128)):
+                    low[s : s + 1, cols] = first[n][rows * s : rows * s + 1, :]
+                    end = rows * (s + 1)
+                    high[s : s + 1, cols] = last[n][end - 1 : end, :]
+
+
+def edges(idx, act_own, act_oth, skip_own, skip_oth):
+    return pl.pallas_call(
+        edges_kernel,
+        out_shape=[jax.ShapeDtypeStruct((2, 2816), BF16)] * 2,
+        in_specs=[SMEM] + [VMEM] * 4,
+        out_specs=[VMEM] * 2,
+        compiler_params=LIMIT,
+        name="edges",
+    )(idx, act_own, act_oth, skip_own, skip_oth)
 
 
 def on_device(
@@ -299,48 +450,64 @@
     x, c, y, z = lax.axis_index("group"), pos % 2, pos // 2 % 2, pos // 4
     idx = jnp.stack([x, y, z, c]).astype(jnp.int32)
     flat = acts.reshape(128, 1536)
-
-    def chip_half(shard):
+    keep, send = split(idx, *map(in_hbm, (w_lift, w_skip, w_point.T)))
+    full, u0, c0 = join(idx, keep, c_swap(send))
+
+    def projected():
+        return project(
+            idx,
+            in_hbm(behind(flat, u0)),
+            norm_gain.reshape(1, -1),
+            *map(in_hbm, (w_query, w_key, w_value)),
+        )
+
+    def joined():
+        packs = [plan[n] for n in ("q0", "qc", "qy", "qcy")]
         return jnp.concatenate(
-            [columns(shard, c, 768), c_swap(columns(shard, 1 - c, 768))], axis=0
-        )
-
-    half_a = chip_half(jnp.concatenate([w_lift, w_skip], axis=0))
-    half_b = chip_half(w_point.T)
-    pieces_a = [half_a, y_swap(half_a)]
-    a = columns(half_a, x, 384)
-    for _ in range(3):
-        a = z_ring(a)
-        b = y_swap(a)
-        pieces_a += [a, b, x_swap(a), x_swap(b)]
-    mine_b = columns(half_b, x, 384)
-    y_mine_b = y_swap(mine_b)
-    pieces_b = [half_b, y_mine_b, y_swap(columns(half_b, 1 - x, 384))]
-    b = jnp.concatenate([mine_b, y_mine_b], axis=0)
-    for _ in range(3):
-        b = z_ring(b)
-        pieces_b += [b, x_swap(b)]
-
-    packs = project(idx, flat, norm_gain.reshape(1, -1), w_query, w_key, w_value)
-    swaps = [lambda v: v, c_swap, y_swap, cy_swap]
-    packs = [swap(p) for swap, p in zip(swaps, packs)]
-    kv = jnp.concatenate(
-        [p[:, :256].reshape(2, 64, 256) for p in packs], axis=1
-    ).reshape(512, 256)
-    kvs = [kv]
-    for _ in range(3):
-        kv = z_ring(kv)
-        kvs.append(kv)
-    mixed = attend(packs, kvs)
-    mixed = [swap(m) for swap, m in zip(swaps, mixed)]
-    activated = output(idx, flat, w_out, mixed)
-    skip_act = jax.nn.gelu(skips.astype(F32)).astype(BF16).reshape(256, 1280)
-    merged, first, last = merge(
-        idx, activated, c_swap(activated), skip_act, c_swap(skip_act), pieces_a
-    )
-    before = lax.ppermute(last, "pos", CHIP_UP)
-    after = lax.ppermute(first, "pos", CHIP_DOWN)
-    own, oth = point(idx, depth_kernel, merged, before, after, pieces_b)
+            [p[:, :256].reshape(2, 64, 256) for p in packs], axis=1
+        ).reshape(512, 256)
+
+    def attended():
+        return attend(
+            [plan[n] for n in ("q0", "qc", "qy", "qcy")],
+            [plan[n] for n in ("k0", "k1", "k2", "k3")],
+        )
+
+    makers = {
+        "u0": lambda: u0,
+        "c0": lambda: c0,
+        "packs": projected,
+        "k0": joined,
+        "mixes": attended,
+        "act": lambda: output(idx, flat, w_out, [plan[n] for n in ("m0", "mc", "my", "mcy")]),
+        "skip": lambda: jax.nn.gelu(skips.astype(F32)).astype(BF16).reshape(256, 1280),
+        "edges": lambda: edges(idx, *(plan[n] for n in ("act", "actc", "skip", "skipc"))),
+        "low": lambda: plan["edges"][0],
+        "high": lambda: plan["edges"][1],
+    }
+    for n, way in enumerate(("0", "c", "y", "cy")):
+        makers["p" + way] = lambda n=n: plan["packs"][n]
+        makers["o" + way] = lambda n=n: plan["mixes"][n]
+    makers["q0"], makers["m0"] = makers["p0"], makers["o0"]
+    swaps = {"c": c_swap, "y": y_swap, "cy": cy_swap, "x": x_swap, "z": z_ring}
+    swaps |= {"up": over_pos(CHIP_UP), "down": over_pos(CHIP_DOWN)}
+
+    def sender(how, src):
+        return lambda: plan.send(swaps[how], src)
+
+    for name, how, src in SENDS:
+        makers[name] = sender(how, src)
+    plan = Plan(WIDTH, makers)
+    for name, _, _ in SENDS:
+        plan[name]
+    pieces = [full, plan["b0"], plan["d0"]] + [
+        plan[part + str(k)] for k in (1, 2, 3) for part in "ubcd"
+    ]
+    merged, ends = merge(
+        idx, plan["act"], plan["actc"], plan["skip"], plan["skipc"], plan["before"],
+        plan["after"], pieces,
+    )
+    own, oth = point(idx, depth_kernel, merged, ends, pieces)
     return (own + c_swap(oth).astype(F32)).astype(BF16)
 
 

time: 121 us -> 93 us (0.77)
  waiting for transfers between devices: 58.3 us -> 45.1 us
  starting transfers between devices: 39.5 us -> 29.4 us
  local copies, waits for them, and re-layouts: 5.79 us -> 0.05 us
    ppermute x9 -> x5, waiting for transfers between devices: 20.4 us -> 0.01 us  [x_swap(): return lax.ppermute(v, 'group', X_SWAP)]
    ppermute x26 -> x24, waiting for transfers between devices: 37.8 us -> 45.1 us  [over_pos(): return lambda v: lax.ppermute(v, 'pos', pairs)]
    ppermute x2 -> x0, starting transfers between devices: 5.43 us -> none  [the longest x1 3.95 us: on_device(): before = lax.ppermute(last, 'pos', CHIP_UP)]
    unnamed x23 -> x10, local copies, waits for them, and re-layouts: 4.98 us -> 0.03 us
    ppermute x9 -> x5, starting transfers between devices: 11.4 us -> 7.28 us  [x_swap(): return lax.ppermute(v, 'group', X_SWAP)]
    pallas_call x0 -> x3, Pallas kernels: none -> 3.07 us  [the longest x1 1.82 us: split(): pl.pallas_call(split_kernel, out_shape=[jax.ShapeDtypeStruct((272, 768),...]
    pallas_call x1, Pallas kernels: 5.51 us -> 3.07 us  [merge(): pl.pallas_call(merge_kernel, out_shape=[jax.ShapeDtypeStruct((2, 256, 768...]
    pallas_call x1, Pallas kernels: 5.37 us -> 3.25 us  [point(): pl.pallas_call(point_kernel, out_shape=[jax.ShapeDtypeStruct((2, 128, 153...]
  transfers between devices with their start and end apart: 37 -> 29, of which waited for: 21 -> 13; matrix products, arithmetic and copies ran while one was open for 1% -> 1% of each run, Pallas kernels for 7% -> 7%
where the time goes in v2:
time: 93 us; the launch traced here: 92.1 us
  waiting for transfers between devices  45.1 us (48%)
  starting transfers between devices  29.4 us (32%)
  Pallas kernels  15.7 us (17%)
  other arithmetic  1.64 us (2%)
    ppermute x24, waiting for transfers between devices, over_pos(): return lambda v: lax.ppermute(v, 'pos', pairs)  45.1 us
    ppermute x24, starting transfers between devices, over_pos(): return lambda v: lax.ppermute(v, 'pos', pairs)  22.1 us
    ppermute x5, starting transfers between devices, x_swap(): return lax.ppermute(v, 'group', X_SWAP)  7.28 us
    pallas_call x1, Pallas kernels, project(): pl.pallas_call(project_kernel, out_shape=[jax.ShapeDtypeStruct((rows, 384...  3.71 us
    pallas_call x1, Pallas kernels, point(): pl.pallas_call(point_kernel, out_shape=[jax.ShapeDtypeStruct((2, 128, 153...  3.25 us
    pallas_call x1, Pallas kernels, merge(): pl.pallas_call(merge_kernel, out_shape=[jax.ShapeDtypeStruct((2, 256, 768...  3.07 us
  transfers between devices with their start and end apart: 29, of which 13 were waited for; matrix products, arithmetic and copies ran while one was open for 1% of the time, Pallas kernels for 7%

profile of v2, /device:TPU:0, one launch (start us, length us, event | category | flops | bytes accessed | tf_op | source)
XLA Modules:
  0.0 92.1 jit_solution(7990732967737770845)
XLA Ops:
  0.0 0.1 pad_add_fusion.idx
  0.1 1.8 %split.1 = (bf16[272,768]{1,0:T(8,128)(2,1)S(1)}, bf16[272,768]{1,0:T(8,128)(2,1)S(1)}) custom-call(s32[4]{0:T(128)S(1)} %pad_add_fusion.idx, bf16[96,1536]{1,0:T(8,128)(2,1)} %wl.1, bf16[80,1536]{1,0:T(8,128)(2,1)} %ws.1, bf16[96,1536]{1,0:T(8,128)(2,1)} %bitcast.19), custom_call_target="tpu_custom_call" | custom-call | tf_op jit(solution)/shard_map/split/pallas_call | solution.py:381
  1.9 0.5 collective-permute-start
  2.4 1.4 %collective-permute-done.got = bf16[272,768]{1,0:T(8,128)(2,1)S(1)} collective-permute-done((bf16[272,768]{1,0:T(8,128)(2,1)S(1)}, bf16[272,768]{1,0:T(8,128)(2,1)S(1)}, u32[]{:S(2)}, u32[]{:S(2)}) %collective-permute-start) | collective-permute-done | bytes 417824 | tf_op jit(solution)/shard_map/ppermute | solution.py:64
  3.8 0.7 join.1
  4.5 3.0 %collective-permute-start.7 = (bf16[544,384]{1,0:T(8,128)(2,1)S(1)}, bf16[544,384]{1,0:T(8,128)(2,1)S(1)}, u32[]{:S(2)}, u32[]{:S(2)}) collective-permute-start(bf16[544,384]{1,0:T(8,128)(2,1)S(1)} %get-tuple-element.65), channel_id=1, source_target_pairs={{0,4},{1,5},{2,6},{3,7},{4,8},{5,9},{6,10},{7,11},{8,12},{9,13},{1... | collective-permute-start | bytes 1253384 | tf_op jit(solution)/shard_map/ppermute | solution.py:64
  7.5 3.7 %project.1 = (bf16[128,384]{1,0:T(8,128)(2,1)S(1)}, bf16[128,384]{1,0:T(8,128)(2,1)S(1)}, bf16[128,384]{1,0:T(8,128)(2,1)S(1)}, bf16[128,384]{1,0:T(8,128)(2,1)S(1)}) custom-call(s32[4]{0:T(128)S(1)} %pad_add_fusion.idx, bf16[128,1536]{1,0:T(8,128)(2,1)} %bitcast.15, f32[1,1536]{1,0:T(1,128)S(1)} %reshape.25.gain, bf16[1536,256]{1,0:T(8,128)(2,1)} %wq_hbm.1, ...), custom_call_target="tpu_custom_call" | custom-call | tf_op jit(solution)/shard_map/project/pallas_call | solution.py:121
  11.2 0.0 copy-start.3
  11.2 1.0 %collective-permute-start.3 = (bf16[128,384]{1,0:T(8,128)(2,1)S(1)}, bf16[128,384]{1,0:T(8,128)(2,1)S(1)}, u32[]{:S(2)}, u32[]{:S(2)}) collective-permute-start(bf16[128,384]{1,0:T(8,128)(2,1)S(1)} %get-tuple-element.53), channel_id=1, source_target_pairs={{0,3},{1,2},{2,1},{3,0},{4,7},{5,6},{6,5},{7,4},{8,11},{9,10},{10,... | collective-permute-start | bytes 294920 | tf_op jit(solution)/shard_map/ppermute | solution.py:64
  12.3 0.6 collective-permute-start.2
  12.9 3.4 %collective-permute-done.3.refs_3_ = bf16[128,384]{1,0:T(8,128)(2,1)S(1)} collective-permute-done((bf16[128,384]{1,0:T(8,128)(2,1)S(1)}, bf16[128,384]{1,0:T(8,128)(2,1)S(1)}, u32[]{:S(2)}, u32[]{:S(2)}) %collective-permute-start.3) | collective-permute-done | bytes 98336 | tf_op jit(solution)/shard_map/ppermute | solution.py:64
  16.3 3.1 %collective-permute-done.7.refs_3_ = bf16[544,384]{1,0:T(8,128)(2,1)S(1)} collective-permute-done((bf16[544,384]{1,0:T(8,128)(2,1)S(1)}, bf16[544,384]{1,0:T(8,128)(2,1)S(1)}, u32[]{:S(2)}, u32[]{:S(2)}) %collective-permute-start.7) | collective-permute-done | bytes 417824 | tf_op jit(solution)/shard_map/ppermute | solution.py:64
  19.5 1.5 %collective-permute-start.13 = (bf16[544,384]{1,0:T(8,128)(2,1)S(1)}, bf16[544,384]{1,0:T(8,128)(2,1)S(1)}, u32[]{:S(2)}, u32[]{:S(2)}) collective-permute-start(bf16[544,384]{1,0:T(8,128)(2,1)S(1)} %get-tuple-element.65), channel_id=1, source_target_pairs={{0,2},{1,3},{2,0},{3,1},{4,6},{5,7},{6,4},{7,5},{8,10},{9,11},{10,... | collective-permute-start | bytes 1253384 | tf_op jit(solution)/shard_map/ppermute | solution.py:64
  21.0 0.0 collective-permute-done.2.refs_2_
  21.0 1.5 %collective-permute-start.9 = (bf16[544,384]{1,0:T(8,128)(2,1)S(1)}, bf16[544,384]{1,0:T(8,128)(2,1)S(1)}, u32[]{:S(2)}, u32[]{:S(2)}) collective-permute-start(bf16[544,384]{1,0:T(8,128)(2,1)S(1)} %collective-permute-done.7.refs_3_), channel_id=1, source_target_pairs={{0,16},{16,0},{1,17},{17,1},{2,18},{18,2},{3,19},{19,3},{4,20},{20... | collective-permute-start | bytes 1253384 | tf_op jit(solution)/shard_map/ppermute | solution.py:72
  22.5 0.5 collective-permute-start.22
  23.0 0.0 collective-permute-start.1
  23.0 1.3 %collective-permute-done.1.refs_1_ = bf16[128,384]{1,0:T(8,128)(2,1)S(1)} collective-permute-done((bf16[128,384]{1,0:T(8,128)(2,1)S(1)}, bf16[128,384]{1,0:T(8,128)(2,1)S(1)}, u32[]{:S(2)}, u32[]{:S(2)}) %collective-permute-start.1) | collective-permute-done | bytes 98336 | tf_op jit(solution)/shard_map/ppermute | solution.py:64
  24.3 0.0 copy-start
  24.3 0.0 copy-start.1
  24.3 1.3 %collective-permute-start.4 = (bf16[512,256]{1,0:T(8,128)(2,1)S(1)}, bf16[512,256]{1,0:T(8,128)(2,1)S(1)}, u32[]{:S(2)}, u32[]{:S(2)}) collective-permute-start(bf16[512,256]{1,0:T(8,128)(2,1)S(1)} %bitcast.17), channel_id=1, source_target_pairs={{0,4},{1,5},{2,6},{3,7},{4,8},{5,9},{6,10},{7,11},{8,12},{9,13},{1... | collective-permute-start | bytes 786440 | tf_op jit(solution)/shard_map/ppermute | solution.py:64
  25.7 8.1 %collective-permute-done.8.refs_7_ = bf16[544,384]{1,0:T(8,128)(2,1)S(1)} collective-permute-done((bf16[544,384]{1,0:T(8,128)(2,1)S(1)}, bf16[544,384]{1,0:T(8,128)(2,1)S(1)}, u32[]{:S(2)}, u32[]{:S(2)}) %collective-permute-start.8) | collective-permute-done | bytes 417824 | tf_op jit(solution)/shard_map/ppermute | solution.py:64
  33.8 0.0 collective-permute-done.13.refs_1_
  33.8 0.0 collective-permute-start.14
  33.8 1.5 %collective-permute-start.16 = (bf16[544,384]{1,0:T(8,128)(2,1)S(1)}, bf16[544,384]{1,0:T(8,128)(2,1)S(1)}, u32[]{:S(2)}, u32[]{:S(2)}) collective-permute-start(bf16[544,384]{1,0:T(8,128)(2,1)S(1)} %collective-permute-done.8.refs_7_), channel_id=1, source_target_pairs={{0,16},{16,0},{1,17},{17,1},{2,18},{18,2},{3,19},{19,3},{4,20},{20... | collective-permute-start | bytes 1253384 | tf_op jit(solution)/shard_map/ppermute | solution.py:72
  35.3 0.0 collective-permute-done.9.refs_5_
  35.3 1.5 %collective-permute-start.10 = (bf16[544,384]{1,0:T(8,128)(2,1)S(1)}, bf16[544,384]{1,0:T(8,128)(2,1)S(1)}, u32[]{:S(2)}, u32[]{:S(2)}) collective-permute-start(bf16[544,384]{1,0:T(8,128)(2,1)S(1)} %collective-permute-done.8.refs_7_), channel_id=1, source_target_pairs={{0,2},{1,3},{2,0},{3,1},{4,6},{5,7},{6,4},{7,5},{8,10},{9,11},{10,... | collective-permute-start | bytes 1253384 | tf_op jit(solution)/shard_map/ppermute | solution.py:64
  36.9 4.1 %collective-permute-done.22.refs_4_ = bf16[544,384]{1,0:T(8,128)(2,1)S(1)} collective-permute-done((bf16[544,384]{1,0:T(8,128)(2,1)S(1)}, bf16[544,384]{1,0:T(8,128)(2,1)S(1)}, u32[]{:S(2)}, u32[]{:S(2)}) %collective-permute-start.22) | collective-permute-done | bytes 417824 | tf_op jit(solution)/shard_map/ppermute | solution.py:64
  41.0 1.5 %collective-permute-start.23 = (bf16[544,384]{1,0:T(8,128)(2,1)S(1)}, bf16[544,384]{1,0:T(8,128)(2,1)S(1)}, u32[]{:S(2)}, u32[]{:S(2)}) collective-permute-start(bf16[544,384]{1,0:T(8,128)(2,1)S(1)} %collective-permute-done.22.refs_4_), channel_id=1, source_target_pairs={{0,16},{16,0},{1,17},{17,1},{2,18},{18,2},{3,19},{19,3},{4,20},{20... | collective-permute-start | bytes 1253384 | tf_op jit(solution)/shard_map/ppermute | solution.py:72
  42.5 1.3 %collective-permute-start.5 = (bf16[512,256]{1,0:T(8,128)(2,1)S(1)}, bf16[512,256]{1,0:T(8,128)(2,1)S(1)}, u32[]{:S(2)}, u32[]{:S(2)}) collective-permute-start(bf16[512,256]{1,0:T(8,128)(2,1)S(1)} %collective-permute-done.4.refs_5_), channel_id=1, source_target_pairs={{0,4},{1,5},{2,6},{3,7},{4,8},{5,9},{6,10},{7,11},{8,12},{9,13},{1... | collective-permute-start | bytes 786440 | tf_op jit(solution)/shard_map/ppermute | solution.py:64
  43.8 8.8 %collective-permute-done.5.refs_6_ = bf16[512,256]{1,0:T(8,128)(2,1)S(1)} collective-permute-done((bf16[512,256]{1,0:T(8,128)(2,1)S(1)}, bf16[512,256]{1,0:T(8,128)(2,1)S(1)}, u32[]{:S(2)}, u32[]{:S(2)}) %collective-permute-start.5) | collective-permute-done | bytes 262176 | tf_op jit(solution)/shard_map/ppermute | solution.py:64
  52.6 0.0 collective-permute-start.6
  52.6 0.0 collective-permute-done.14.refs_11_
  52.6 1.3 %collective-permute-start.17 = (bf16[544,384]{1,0:T(8,128)(2,1)S(1)}, bf16[544,384]{1,0:T(8,128)(2,1)S(1)}, u32[]{:S(2)}, u32[]{:S(2)}) collective-permute-start(bf16[544,384]{1,0:T(8,128)(2,1)S(1)} %collective-permute-done.14.refs_11_), channel_id=1, source_target_pairs={{0,2},{1,3},{2,0},{3,1},{4,6},{5,7},{6,4},{7,5},{8,10},{9,11},{10,... | collective-permute-start | bytes 1253384 | tf_op jit(solution)/shard_map/ppermute | solution.py:64
  54.0 0.0 collective-permute-done.10.refs_8_
  54.0 0.0 collective-permute-done.23.refs_6_
  54.0 1.5 %collective-permute-start.24 = (bf16[544,384]{1,0:T(8,128)(2,1)S(1)}, bf16[544,384]{1,0:T(8,128)(2,1)S(1)}, u32[]{:S(2)}, u32[]{:S(2)}) collective-permute-start(bf16[544,384]{1,0:T(8,128)(2,1)S(1)} %collective-permute-done.10.refs_8_), channel_id=1, source_target_pairs={{0,16},{16,0},{1,17},{17,1},{2,18},{18,2},{3,19},{19,3},{4,20},{20... | collective-permute-start | bytes 1253384 | tf_op jit(solution)/shard_map/ppermute | solution.py:72
  55.5 0.4 fusion.5
  55.9 0.1 collective-permute-start.19
  56.0 5.4 %collective-permute-done.6.refs_7_ = bf16[512,256]{1,0:T(8,128)(2,1)S(1)} collective-permute-done((bf16[512,256]{1,0:T(8,128)(2,1)S(1)}, bf16[512,256]{1,0:T(8,128)(2,1)S(1)}, u32[]{:S(2)}, u32[]{:S(2)}) %collective-permute-start.6) | collective-permute-done | bytes 262176 | tf_op jit(solution)/shard_map/ppermute | solution.py:64
  61.4 1.3 %attend.1 = (bf16[128,256]{1,0:T(8,128)(2,1)S(1)}, bf16[128,256]{1,0:T(8,128)(2,1)S(1)}, bf16[128,256]{1,0:T(8,128)(2,1)S(1)}, bf16[128,256]{1,0:T(8,128)(2,1)S(1)}) custom-call(bf16[128,384]{1,0:T(8,128)(2,1)S(1)} %get-tuple-element.50.refs_0_, bf16[128,384]{1,0:T(8,128)(2,1)S(1)} %collective-permute-done.1.refs_1_, ...), custom_call_target="tpu_custom_call" | custom-call | tf_op jit(solution)/shard_map/attend/pallas_call | solution.py:158
  62.6 0.1 collective-permute-start.15
  62.7 1.1 %collective-permute-start.11 = (bf16[128,256]{1,0:T(8,128)(2,1)S(1)}, bf16[128,256]{1,0:T(8,128)(2,1)S(1)}, u32[]{:S(2)}, u32[]{:S(2)}) collective-permute-start(bf16[128,256]{1,0:T(8,128)(2,1)S(1)} %get-tuple-element.61), channel_id=1, source_target_pairs={{0,1},{1,0},{2,3},{3,2},{4,5},{5,4},{6,7},{7,6},{8,9},{9,8},{10,11... | collective-permute-start | bytes 196616 | tf_op jit(solution)/shard_map/ppermute | solution.py:64
  63.8 2.8 %collective-permute-done.15.refs_3_ = bf16[128,256]{1,0:T(8,128)(2,1)S(1)} collective-permute-done((bf16[128,256]{1,0:T(8,128)(2,1)S(1)}, bf16[128,256]{1,0:T(8,128)(2,1)S(1)}, u32[]{:S(2)}, u32[]{:S(2)}) %collective-permute-start.15) | collective-permute-done | bytes 65568 | tf_op jit(solution)/shard_map/ppermute | solution.py:64
  66.6 1.0 %collective-permute-start.12 = (bf16[128,256]{1,0:T(8,128)(2,1)S(1)}, bf16[128,256]{1,0:T(8,128)(2,1)S(1)}, u32[]{:S(2)}, u32[]{:S(2)}) collective-permute-start(bf16[128,256]{1,0:T(8,128)(2,1)S(1)} %get-tuple-element.63), channel_id=1, source_target_pairs={{0,2},{1,3},{2,0},{3,1},{4,6},{5,7},{6,4},{7,5},{8,10},{9,11},{10,... | collective-permute-start | bytes 196616 | tf_op jit(solution)/shard_map/ppermute | solution.py:64
  67.7 0.0 collective-permute-done.17.refs_12_
  67.7 1.3 %collective-permute-start.27 = (bf16[544,384]{1,0:T(8,128)(2,1)S(1)}, bf16[544,384]{1,0:T(8,128)(2,1)S(1)}, u32[]{:S(2)}, u32[]{:S(2)}) collective-permute-start(bf16[544,384]{1,0:T(8,128)(2,1)S(1)} %collective-permute-done.17.refs_12_), channel_id=1, source_target_pairs={{0,16},{16,0},{1,17},{17,1},{2,18},{18,2},{3,19},{19,3},{4,20},{20... | collective-permute-start | bytes 1253384 | tf_op jit(solution)/shard_map/ppermute | solution.py:72
  68.9 0.0 collective-permute-done.11.refs_1_
  68.9 1.1 %collective-permute-start.25 = (bf16[544,384]{1,0:T(8,128)(2,1)S(1)}, bf16[544,384]{1,0:T(8,128)(2,1)S(1)}, u32[]{:S(2)}, u32[]{:S(2)}) collective-permute-start(bf16[544,384]{1,0:T(8,128)(2,1)S(1)} %get-tuple-element.80), channel_id=1, source_target_pairs={{0,2},{1,3},{2,0},{3,1},{4,6},{5,7},{6,4},{7,5},{8,10},{9,11},{10,... | collective-permute-start | bytes 1253384 | tf_op jit(solution)/shard_map/ppermute | solution.py:64
  70.1 1.2 %collective-permute-done.12.refs_2_ = bf16[128,256]{1,0:T(8,128)(2,1)S(1)} collective-permute-done((bf16[128,256]{1,0:T(8,128)(2,1)S(1)}, bf16[128,256]{1,0:T(8,128)(2,1)S(1)}, u32[]{:S(2)}, u32[]{:S(2)}) %collective-permute-start.12) | collective-permute-done | bytes 65568 | tf_op jit(solution)/shard_map/ppermute | solution.py:64
  71.3 1.3 %output.1.act_own = bf16[128,1536]{1,0:T(8,128)(2,1)S(1)} custom-call(s32[4]{0:T(128)S(1)} %pad_add_fusion.idx, bf16[128,1536]{1,0:T(8,128)(2,1)S(1)} %bitcast.16, bf16[768,1536]{1,0:T(8,128)(2,1)S(1)} %copy-done, bf16[128,256]{1,0:T(8,128)(2,1)S(1)} %get-tuple-element.56.refs_0_, bf16[128,256]{1,0:T(8,128)(2,1)S(1)} %collective-permute-done.11.refs_1_, ...), custom_call_target="tpu_custom_call" | custom-call | tf_op jit(solution)/shard_map/output/pallas_call | solution.py:182
  72.7 0.1 collective-permute-start.18
  72.7 1.7 %collective-permute-done.18.act_oth = bf16[128,1536]{1,0:T(8,128)(2,1)S(1)} collective-permute-done((bf16[128,1536]{1,0:T(8,128)(2,1)S(1)}, bf16[128,1536]{1,0:T(8,128)(2,1)S(1)}, u32[]{:S(2)}, u32[]{:S(2)}) %collective-permute-start.18) | collective-permute-done | bytes 393248 | tf_op jit(solution)/shard_map/ppermute | solution.py:64
  74.4 0.6 edges.1
  75.0 1.3 %collective-permute-start.21 = (bf16[2,2816]{1,0:T(2,128)(2,1)S(1)}, bf16[2,2816]{1,0:T(2,128)(2,1)S(1)}, u32[]{:S(2)}, u32[]{:S(2)}) collective-permute-start(bf16[2,2816]{1,0:T(2,128)(2,1)S(1)} %get-tuple-element.75), channel_id=1, source_target_pairs={{2,0},{3,1},{4,2},{5,3},{6,4},{7,5},{8,6},{9,7},{10,8},{11,9},{12,... | collective-permute-start | bytes 33800 | tf_op jit(solution)/shard_map/ppermute | solution.py:64
  76.3 4.5 %collective-permute-start.20 = (bf16[2,2816]{1,0:T(2,128)(2,1)S(1)}, bf16[2,2816]{1,0:T(2,128)(2,1)S(1)}, u32[]{:S(2)}, u32[]{:S(2)}) collective-permute-start(bf16[2,2816]{1,0:T(2,128)(2,1)S(1)} %get-tuple-element.73), channel_id=1, source_target_pairs={{0,2},{1,3},{2,4},{3,5},{4,6},{5,7},{6,8},{7,9},{8,10},{9,11},{10,... | collective-permute-start | bytes 33800 | tf_op jit(solution)/shard_map/ppermute | solution.py:64
  80.9 0.0 collective-permute-done.21.after
  80.9 1.4 %collective-permute-done.20.before = bf16[2,2816]{1,0:T(2,128)(2,1)S(1)} collective-permute-done((bf16[2,2816]{1,0:T(2,128)(2,1)S(1)}, bf16[2,2816]{1,0:T(2,128)(2,1)S(1)}, u32[]{:S(2)}, u32[]{:S(2)}) %collective-permute-start.20) | collective-permute-done | bytes 11296 | tf_op jit(solution)/shard_map/ppermute | solution.py:64
  82.3 0.0 collective-permute-done.25.refs_2_
  82.3 3.1 %merge.1 = (bf16[2,256,768]{2,1,0:T(8,128)(2,1)S(1)}, bf16[16,768]{1,0:T(8,128)(2,1)S(1)}) custom-call(s32[4]{0:T(128)S(1)} %pad_add_fusion.idx, bf16[128,1536]{1,0:T(8,128)(2,1)S(1)} %output.1.act_own, bf16[128,1536]{1,0:T(8,128)(2,1)S(1)} %collective-permute-done.18.act_oth, bf16[256,1280]{1,0:T(8,128)(2,1)S(1)} %bitcast.14, ...), custom_call_target="tpu_custom_call" | custom-call | tf_op jit(solution)/shard_map/merge/pallas_call | solution.py:256
  85.4 3.2 %point.1 = (f32[2,128,1536]{2,1,0:T(8,128)S(1)}, bf16[2,128,1536]{2,1,0:T(8,128)(2,1)S(1)}) custom-call(s32[4]{0:T(128)S(1)} %pad_add_fusion.idx, f32[3,1536]{1,0:T(4,128)S(1)} %copy-done.2, bf16[2,256,768]{2,1,0:T(8,128)(2,1)S(1)} %get-tuple-element.83.merged, bf16[16,768]{1,0:T(8,128)(2,1)S(1)} %get-tuple-element.84.ends, ...), custom_call_target="tpu_custom_call" | custom-call | tf_op jit(solution)/shard_map/point/pallas_call | solution.py:320
  88.6 0.1 collective-permute-start.28
  88.7 2.3 %collective-permute-done.28 = bf16[2,128,1536]{2,1,0:T(8,128)(2,1)S(1)} collective-permute-done((bf16[2,128,1536]{2,1,0:T(8,128)(2,1)S(1)}, bf16[2,128,1536]{2,1,0:T(8,128)(2,1)S(1)}, u32[]{:S(2)}, u32[]{:S(2)}) %collective-permute-start.28) | collective-permute-done | bytes 786464 | tf_op jit(solution)/shard_map/ppermute | solution.py:64
  91.0 1.1 %add_convert_fusion = bf16[2,128,1536]{2,1,0:T(8,128)(2,1)} fusion(f32[2,128,1536]{2,1,0:T(8,128)S(1)} %get-tuple-element.85, bf16[2,128,1536]{2,1,0:T(8,128)(2,1)S(1)} %collective-permute-done.28), kind=kLoop, calls=%fused_computation.4 | loop fusion | flops 1179648 | bytes 3145728 | tf_op jit(solution)/shard_map/convert_element_type | solution.py:511
  (21 shorter events, 0.1 us)
Async XLA Ops:
  0.0 7.5 %copy-start.4 = (f32[1536]{0:T(1024)S(1)}, f32[1536]{0:T(1024)}, u32[]{:S(2)}) copy-start(f32[1536]{0:T(1024)} %param.13) | copy-start | bytes 18436
  1.9 1.9 %collective-permute-start = (bf16[272,768]{1,0:T(8,128)(2,1)S(1)}, bf16[272,768]{1,0:T(8,128)(2,1)S(1)}, u32[]{:S(2)}, u32[]{:S(2)}) collective-permute-start(bf16[272,768]{1,0:T(8,128)(2,1)S(1)} %get-tuple-element.47), channel_id=1, source_target_pairs={{0,1},{1,0},{2,3},{3,2},{4,5},{5,4},{6,7},{7,6},{8,9},{9,8},{10,11... | collective-permute-start | bytes 1253384 | tf_op jit(solution)/shard_map/ppermute | solution.py:64
  4.5 15.0 %collective-permute-start.7 = (bf16[544,384]{1,0:T(8,128)(2,1)S(1)}, bf16[544,384]{1,0:T(8,128)(2,1)S(1)}, u32[]{:S(2)}, u32[]{:S(2)}) collective-permute-start(bf16[544,384]{1,0:T(8,128)(2,1)S(1)} %get-tuple-element.65), channel_id=1, source_target_pairs={{0,4},{1,5},{2,6},{3,7},{4,8},{5,9},{6,10},{7,11},{8,12},{9,13},{1... | collective-permute-start | bytes 1253384 | tf_op jit(solution)/shard_map/ppermute | solution.py:64
  11.2 44.3 %copy-start.3 = (bf16[2,128,1280]{2,1,0:T(8,128)(2,1)S(1)}, bf16[2,128,1280]{2,1,0:T(8,128)(2,1)}, u32[]{:S(2)}) copy-start(bf16[2,128,1280]{2,1,0:T(8,128)(2,1)} %param.12) | copy-start | bytes 1966084
  11.2 5.1 %collective-permute-start.3 = (bf16[128,384]{1,0:T(8,128)(2,1)S(1)}, bf16[128,384]{1,0:T(8,128)(2,1)S(1)}, u32[]{:S(2)}, u32[]{:S(2)}) collective-permute-start(bf16[128,384]{1,0:T(8,128)(2,1)S(1)} %get-tuple-element.53), channel_id=1, source_target_pairs={{0,3},{1,2},{2,1},{3,0},{4,7},{5,6},{6,5},{7,4},{8,11},{9,10},{10,... | collective-permute-start | bytes 294920 | tf_op jit(solution)/shard_map/ppermute | solution.py:64
  12.3 8.7 %collective-permute-start.2 = (bf16[128,384]{1,0:T(8,128)(2,1)S(1)}, bf16[128,384]{1,0:T(8,128)(2,1)S(1)}, u32[]{:S(2)}, u32[]{:S(2)}) collective-permute-start(bf16[128,384]{1,0:T(8,128)(2,1)S(1)} %get-tuple-element.52), channel_id=1, source_target_pairs={{0,2},{1,3},{2,0},{3,1},{4,6},{5,7},{6,4},{7,5},{8,10},{9,11},{10,... | collective-permute-start | bytes 294920 | tf_op jit(solution)/shard_map/ppermute | solution.py:64
  19.5 14.4 %collective-permute-start.8 = (bf16[544,384]{1,0:T(8,128)(2,1)S(1)}, bf16[544,384]{1,0:T(8,128)(2,1)S(1)}, u32[]{:S(2)}, u32[]{:S(2)}) collective-permute-start(bf16[544,384]{1,0:T(8,128)(2,1)S(1)} %collective-permute-done.7.refs_3_), channel_id=1, source_target_pairs={{0,4},{1,5},{2,6},{3,7},{4,8},{5,9},{6,10},{7,11},{8,12},{9,13},{1... | collective-permute-start | bytes 1253384 | tf_op jit(solution)/shard_map/ppermute | solution.py:64
  19.5 14.4 %collective-permute-start.13 = (bf16[544,384]{1,0:T(8,128)(2,1)S(1)}, bf16[544,384]{1,0:T(8,128)(2,1)S(1)}, u32[]{:S(2)}, u32[]{:S(2)}) collective-permute-start(bf16[544,384]{1,0:T(8,128)(2,1)S(1)} %get-tuple-element.65), channel_id=1, source_target_pairs={{0,2},{1,3},{2,0},{3,1},{4,6},{5,7},{6,4},{7,5},{8,10},{9,11},{10,... | collective-permute-start | bytes 1253384 | tf_op jit(solution)/shard_map/ppermute | solution.py:64
  21.0 14.4 %collective-permute-start.9 = (bf16[544,384]{1,0:T(8,128)(2,1)S(1)}, bf16[544,384]{1,0:T(8,128)(2,1)S(1)}, u32[]{:S(2)}, u32[]{:S(2)}) collective-permute-start(bf16[544,384]{1,0:T(8,128)(2,1)S(1)} %collective-permute-done.7.refs_3_), channel_id=1, source_target_pairs={{0,16},{16,0},{1,17},{17,1},{2,18},{18,2},{3,19},{19,3},{4,20},{20... | collective-permute-start | bytes 1253384 | tf_op jit(solution)/shard_map/ppermute | solution.py:72
  22.5 18.5 %collective-permute-start.22 = (bf16[544,384]{1,0:T(8,128)(2,1)S(1)}, bf16[544,384]{1,0:T(8,128)(2,1)S(1)}, u32[]{:S(2)}, u32[]{:S(2)}) collective-permute-start(bf16[544,384]{1,0:T(8,128)(2,1)S(1)} %collective-permute-done.7.refs_3_), channel_id=1, source_target_pairs={{0,2},{1,3},{2,0},{3,1},{4,6},{5,7},{6,4},{7,5},{8,10},{9,11},{10,... | collective-permute-start | bytes 1253384 | tf_op jit(solution)/shard_map/ppermute | solution.py:64
  23.0 1.3 %collective-permute-start.1 = (bf16[128,384]{1,0:T(8,128)(2,1)S(1)}, bf16[128,384]{1,0:T(8,128)(2,1)S(1)}, u32[]{:S(2)}, u32[]{:S(2)}) collective-permute-start(bf16[128,384]{1,0:T(8,128)(2,1)S(1)} %get-tuple-element.51), channel_id=1, source_target_pairs={{0,1},{1,0},{2,3},{3,2},{4,5},{5,4},{6,7},{7,6},{8,9},{9,8},{10,11... | collective-permute-start | bytes 294920 | tf_op jit(solution)/shard_map/ppermute | solution.py:64
  24.3 47.0 %copy-start = (bf16[768,1536]{1,0:T(8,128)(2,1)S(1)}, bf16[768,1536]{1,0:T(8,128)(2,1)}, u32[]{:S(2)}) copy-start(bf16[768,1536]{1,0:T(8,128)(2,1)} %wo.1) | copy-start | bytes 7077892
  24.3 47.0 %copy-start.1 = (bf16[2,64,1536]{2,1,0:T(8,128)(2,1)S(1)}, bf16[2,64,1536]{2,1,0:T(8,128)(2,1)}, u32[]{:S(2)}) copy-start(bf16[2,64,1536]{2,1,0:T(8,128)(2,1)} %param.11) | copy-start | bytes 1179652
  24.3 18.1 %collective-permute-start.4 = (bf16[512,256]{1,0:T(8,128)(2,1)S(1)}, bf16[512,256]{1,0:T(8,128)(2,1)S(1)}, u32[]{:S(2)}, u32[]{:S(2)}) collective-permute-start(bf16[512,256]{1,0:T(8,128)(2,1)S(1)} %bitcast.17), channel_id=1, source_target_pairs={{0,4},{1,5},{2,6},{3,7},{4,8},{5,9},{6,10},{7,11},{8,12},{9,13},{1... | collective-permute-start | bytes 786440 | tf_op jit(solution)/shard_map/ppermute | solution.py:64
  33.8 18.8 %collective-permute-start.14 = (bf16[544,384]{1,0:T(8,128)(2,1)S(1)}, bf16[544,384]{1,0:T(8,128)(2,1)S(1)}, u32[]{:S(2)}, u32[]{:S(2)}) collective-permute-start(bf16[544,384]{1,0:T(8,128)(2,1)S(1)} %collective-permute-done.8.refs_7_), channel_id=1, source_target_pairs={{0,4},{1,5},{2,6},{3,7},{4,8},{5,9},{6,10},{7,11},{8,12},{9,13},{1... | collective-permute-start | bytes 1253384 | tf_op jit(solution)/shard_map/ppermute | solution.py:64
  33.8 18.8 %collective-permute-start.16 = (bf16[544,384]{1,0:T(8,128)(2,1)S(1)}, bf16[544,384]{1,0:T(8,128)(2,1)S(1)}, u32[]{:S(2)}, u32[]{:S(2)}) collective-permute-start(bf16[544,384]{1,0:T(8,128)(2,1)S(1)} %collective-permute-done.8.refs_7_), channel_id=1, source_target_pairs={{0,16},{16,0},{1,17},{17,1},{2,18},{18,2},{3,19},{19,3},{4,20},{20... | collective-permute-start | bytes 1253384 | tf_op jit(solution)/shard_map/ppermute | solution.py:72
  35.3 18.6 %collective-permute-start.10 = (bf16[544,384]{1,0:T(8,128)(2,1)S(1)}, bf16[544,384]{1,0:T(8,128)(2,1)S(1)}, u32[]{:S(2)}, u32[]{:S(2)}) collective-permute-start(bf16[544,384]{1,0:T(8,128)(2,1)S(1)} %collective-permute-done.8.refs_7_), channel_id=1, source_target_pairs={{0,2},{1,3},{2,0},{3,1},{4,6},{5,7},{6,4},{7,5},{8,10},{9,11},{10,... | collective-permute-start | bytes 1253384 | tf_op jit(solution)/shard_map/ppermute | solution.py:64
  41.0 13.0 %collective-permute-start.23 = (bf16[544,384]{1,0:T(8,128)(2,1)S(1)}, bf16[544,384]{1,0:T(8,128)(2,1)S(1)}, u32[]{:S(2)}, u32[]{:S(2)}) collective-permute-start(bf16[544,384]{1,0:T(8,128)(2,1)S(1)} %collective-permute-done.22.refs_4_), channel_id=1, source_target_pairs={{0,16},{16,0},{1,17},{17,1},{2,18},{18,2},{3,19},{19,3},{4,20},{20... | collective-permute-start | bytes 1253384 | tf_op jit(solution)/shard_map/ppermute | solution.py:72
  42.5 10.1 %collective-permute-start.5 = (bf16[512,256]{1,0:T(8,128)(2,1)S(1)}, bf16[512,256]{1,0:T(8,128)(2,1)S(1)}, u32[]{:S(2)}, u32[]{:S(2)}) collective-permute-start(bf16[512,256]{1,0:T(8,128)(2,1)S(1)} %collective-permute-done.4.refs_5_), channel_id=1, source_target_pairs={{0,4},{1,5},{2,6},{3,7},{4,8},{5,9},{6,10},{7,11},{8,12},{9,13},{1... | collective-permute-start | bytes 786440 | tf_op jit(solution)/shard_map/ppermute | solution.py:64
  52.6 8.7 %collective-permute-start.6 = (bf16[512,256]{1,0:T(8,128)(2,1)S(1)}, bf16[512,256]{1,0:T(8,128)(2,1)S(1)}, u32[]{:S(2)}, u32[]{:S(2)}) collective-permute-start(bf16[512,256]{1,0:T(8,128)(2,1)S(1)} %collective-permute-done.5.refs_6_), channel_id=1, source_target_pairs={{0,4},{1,5},{2,6},{3,7},{4,8},{5,9},{6,10},{7,11},{8,12},{9,13},{1... | collective-permute-start | bytes 786440 | tf_op jit(solution)/shard_map/ppermute | solution.py:64
  52.6 15.0 %collective-permute-start.17 = (bf16[544,384]{1,0:T(8,128)(2,1)S(1)}, bf16[544,384]{1,0:T(8,128)(2,1)S(1)}, u32[]{:S(2)}, u32[]{:S(2)}) collective-permute-start(bf16[544,384]{1,0:T(8,128)(2,1)S(1)} %collective-permute-done.14.refs_11_), channel_id=1, source_target_pairs={{0,2},{1,3},{2,0},{3,1},{4,6},{5,7},{6,4},{7,5},{8,10},{9,11},{10,... | collective-permute-start | bytes 1253384 | tf_op jit(solution)/shard_map/ppermute | solution.py:64
  54.0 13.7 %collective-permute-start.24 = (bf16[544,384]{1,0:T(8,128)(2,1)S(1)}, bf16[544,384]{1,0:T(8,128)(2,1)S(1)}, u32[]{:S(2)}, u32[]{:S(2)}) collective-permute-start(bf16[544,384]{1,0:T(8,128)(2,1)S(1)} %collective-permute-done.10.refs_8_), channel_id=1, source_target_pairs={{0,16},{16,0},{1,17},{17,1},{2,18},{18,2},{3,19},{19,3},{4,20},{20... | collective-permute-start | bytes 1253384 | tf_op jit(solution)/shard_map/ppermute | solution.py:72
  55.9 16.8 %collective-permute-start.19 = (bf16[256,1280]{1,0:T(8,128)(2,1)S(1)}, bf16[256,1280]{1,0:T(8,128)(2,1)S(1)}, u32[]{:S(2)}, u32[]{:S(2)}) collective-permute-start(bf16[256,1280]{1,0:T(8,128)(2,1)S(1)} %bitcast.12), channel_id=1, source_target_pairs={{0,1},{1,0},{2,3},{3,2},{4,5},{5,4},{6,7},{7,6},{8,9},{9,8},{10,11... | collective-permute-start | bytes 1966088 | tf_op jit(solution)/shard_map/ppermute | solution.py:64
  62.6 4.0 %collective-permute-start.15 = (bf16[128,256]{1,0:T(8,128)(2,1)S(1)}, bf16[128,256]{1,0:T(8,128)(2,1)S(1)}, u32[]{:S(2)}, u32[]{:S(2)}) collective-permute-start(bf16[128,256]{1,0:T(8,128)(2,1)S(1)} %get-tuple-element.67), channel_id=1, source_target_pairs={{0,3},{1,2},{2,1},{3,0},{4,7},{5,6},{6,5},{7,4},{8,11},{9,10},{10,... | collective-permute-start | bytes 196616 | tf_op jit(solution)/shard_map/ppermute | solution.py:64
  62.7 6.2 %collective-permute-start.11 = (bf16[128,256]{1,0:T(8,128)(2,1)S(1)}, bf16[128,256]{1,0:T(8,128)(2,1)S(1)}, u32[]{:S(2)}, u32[]{:S(2)}) collective-permute-start(bf16[128,256]{1,0:T(8,128)(2,1)S(1)} %get-tuple-element.61), channel_id=1, source_target_pairs={{0,1},{1,0},{2,3},{3,2},{4,5},{5,4},{6,7},{7,6},{8,9},{9,8},{10,11... | collective-permute-start | bytes 196616 | tf_op jit(solution)/shard_map/ppermute | solution.py:64
  66.6 4.7 %collective-permute-start.12 = (bf16[128,256]{1,0:T(8,128)(2,1)S(1)}, bf16[128,256]{1,0:T(8,128)(2,1)S(1)}, u32[]{:S(2)}, u32[]{:S(2)}) collective-permute-start(bf16[128,256]{1,0:T(8,128)(2,1)S(1)} %get-tuple-element.63), channel_id=1, source_target_pairs={{0,2},{1,3},{2,0},{3,1},{4,6},{5,7},{6,4},{7,5},{8,10},{9,11},{10,... | collective-permute-start | bytes 196616 | tf_op jit(solution)/shard_map/ppermute | solution.py:64
  67.7 13.2 %collective-permute-start.26 = (bf16[544,384]{1,0:T(8,128)(2,1)S(1)}, bf16[544,384]{1,0:T(8,128)(2,1)S(1)}, u32[]{:S(2)}, u32[]{:S(2)}) collective-permute-start(bf16[544,384]{1,0:T(8,128)(2,1)S(1)} %collective-permute-done.16.refs_9_), channel_id=1, source_target_pairs={{0,4},{1,5},{2,6},{3,7},{4,8},{5,9},{6,10},{7,11},{8,12},{9,13},{1... | collective-permute-start | bytes 1253384 | tf_op jit(solution)/shard_map/ppermute | solution.py:64
  67.7 14.6 %collective-permute-start.27 = (bf16[544,384]{1,0:T(8,128)(2,1)S(1)}, bf16[544,384]{1,0:T(8,128)(2,1)S(1)}, u32[]{:S(2)}, u32[]{:S(2)}) collective-permute-start(bf16[544,384]{1,0:T(8,128)(2,1)S(1)} %collective-permute-done.17.refs_12_), channel_id=1, source_target_pairs={{0,16},{16,0},{1,17},{17,1},{2,18},{18,2},{3,19},{19,3},{4,20},{20... | collective-permute-start | bytes 1253384 | tf_op jit(solution)/shard_map/ppermute | solution.py:72
  68.9 13.3 %collective-permute-start.25 = (bf16[544,384]{1,0:T(8,128)(2,1)S(1)}, bf16[544,384]{1,0:T(8,128)(2,1)S(1)}, u32[]{:S(2)}, u32[]{:S(2)}) collective-permute-start(bf16[544,384]{1,0:T(8,128)(2,1)S(1)} %get-tuple-element.80), channel_id=1, source_target_pairs={{0,2},{1,3},{2,0},{3,1},{4,6},{5,7},{6,4},{7,5},{8,10},{9,11},{10,... | collective-permute-start | bytes 1253384 | tf_op jit(solution)/shard_map/ppermute | solution.py:64
  72.7 1.8 %collective-permute-start.18 = (bf16[128,1536]{1,0:T(8,128)(2,1)S(1)}, bf16[128,1536]{1,0:T(8,128)(2,1)S(1)}, u32[]{:S(2)}, u32[]{:S(2)}) collective-permute-start(bf16[128,1536]{1,0:T(8,128)(2,1)S(1)} %output.1.act_own), channel_id=1, source_target_pairs={{0,1},{1,0},{2,3},{3,2},{4,5},{5,4},{6,7},{7,6},{8,9},{9,8},{10,11... | collective-permute-start | bytes 1179656 | tf_op jit(solution)/shard_map/ppermute | solution.py:64
  75.0 5.9 %collective-permute-start.21 = (bf16[2,2816]{1,0:T(2,128)(2,1)S(1)}, bf16[2,2816]{1,0:T(2,128)(2,1)S(1)}, u32[]{:S(2)}, u32[]{:S(2)}) collective-permute-start(bf16[2,2816]{1,0:T(2,128)(2,1)S(1)} %get-tuple-element.75), channel_id=1, source_target_pairs={{2,0},{3,1},{4,2},{5,3},{6,4},{7,5},{8,6},{9,7},{10,8},{11,9},{12,... | collective-permute-start | bytes 33800 | tf_op jit(solution)/shard_map/ppermute | solution.py:64
  76.3 5.9 %collective-permute-start.20 = (bf16[2,2816]{1,0:T(2,128)(2,1)S(1)}, bf16[2,2816]{1,0:T(2,128)(2,1)S(1)}, u32[]{:S(2)}, u32[]{:S(2)}) collective-permute-start(bf16[2,2816]{1,0:T(2,128)(2,1)S(1)} %get-tuple-element.73), channel_id=1, source_target_pairs={{0,2},{1,3},{2,4},{3,5},{4,6},{5,7},{6,8},{7,9},{8,10},{9,11},{10,... | collective-permute-start | bytes 33800 | tf_op jit(solution)/shard_map/ppermute | solution.py:64
  82.3 3.1 %copy-start.2 = (f32[3,1536]{1,0:T(4,128)S(1)}, f32[3,1536]{1,0:T(4,128)}, u32[]{:S(2)}) copy-start(f32[3,1536]{1,0:T(4,128)} %depth.1) | copy-start | bytes 55300
  88.6 2.4 %collective-permute-start.28 = (bf16[2,128,1536]{2,1,0:T(8,128)(2,1)S(1)}, bf16[2,128,1536]{2,1,0:T(8,128)(2,1)S(1)}, u32[]{:S(2)}, u32[]{:S(2)}) collective-permute-start(bf16[2,128,1536]{2,1,0:T(8,128)(2,1)S(1)} %get-tuple-element.86), channel_id=1, source_target_pairs={{0,1},{1,0},{2,3},{3,2},{4,5},{5,4},{6,7},{7,6},{8,9},{9,8},{10,11... | collective-permute-start | bytes 2359304 | tf_op jit(solution)/shard_map/ppermute | solution.py:64

commit v3 on v2

--- a/solution.py
+++ b/solution.py
@@ -19,35 +19,35 @@
 LIMIT = pltpu.CompilerParams(vmem_limit_bytes=20 * 1024 * 1024)
 
 WIDTH = 5
-CUMULATIVE = False
+CUMULATIVE = True
 SENDS = (
     ("u1", "z", "u0"),
+    ("b0", "y", "u0"),
     ("qy", "y", "py"),
-    ("qcy", "cy", "pcy"),
-    ("qc", "c", "pc"),
-    ("k1", "z", "k0"),
-    ("b1", "y", "u1"),
     ("u2", "z", "u1"),
     ("c1", "x", "u1"),
-    ("b0", "y", "u0"),
-    ("skipc", "c", "skip"),
-    ("k2", "z", "k1"),
-    ("d1", "x", "b1"),
+    ("qcy", "cy", "pcy"),
+    ("b1", "y", "u1"),
+    ("k1", "z", "k0"),
     ("c2", "x", "u2"),
     ("b2", "y", "u2"),
     ("u3", "z", "u2"),
+    ("qc", "c", "pc"),
+    ("k2", "z", "k1"),
+    ("skipc", "c", "skip"),
+    ("d2", "y", "c2"),
+    ("d0", "x", "b0"),
     ("k3", "z", "k2"),
-    ("d2", "x", "b2"),
     ("b3", "y", "u3"),
+    ("d1", "x", "b1"),
+    ("my", "y", "oy"),
     ("mc", "c", "oc"),
-    ("my", "y", "oy"),
     ("mcy", "cy", "ocy"),
-    ("c3", "z", "c2"),
-    ("d0", "y", "c0"),
+    ("c3", "x", "u3"),
+    ("d3", "z", "d2"),
+    ("far", "beyond", "edge"),
     ("actc", "c", "act"),
-    ("before", "up", "high"),
-    ("after", "down", "low"),
-    ("d3", "x", "b3"),
+    ("farc", "beyond c", "edge"),
 )
 
 POS = 16
@@ -55,8 +55,8 @@
 Y_SWAP = [(i, i ^ 2) for i in range(POS)]
 CY_SWAP = [(i, i ^ 3) for i in range(POS)]
 Z_RING = [(i, (i + 4) % POS) for i in range(POS)]
-CHIP_UP = [(i, i + 2) for i in range(POS - 2)]
-CHIP_DOWN = [(i + 2, i) for i in range(POS - 2)]
+BEYOND = [(i, i + 1 if i % 2 else i - 1) for i in range(1, POS - 1)]
+BEYOND_C = [(i, j ^ 1) for i, j in BEYOND]
 X_SWAP = [(0, 1), (1, 0)]
 
 
@@ -189,9 +189,6 @@
     )(idx, acts, wo, *mixed)
 
 
-ALL = slice(None)
-
-
 def quarter(x):
     return pl.ds(pl.multiple_of(x * 384, 384), 384)
 
@@ -203,135 +200,175 @@
 A_ROWS = 352
 
 
-def merge_kernel(idx, act_own, act_oth, skip_own, skip_oth, before, after, *refs):
-    pieces, (merged, ends), (wl, ws, act, skip) = refs[:15], refs[15:17], refs[17:]
+def place(ref, zz, yy, c, col, wl, ws, wp):
+    for n, cc in ((0, c), (1, 1 - c)):
+        p = 4 * zz + 2 * yy + cc
+        base = 176 * n
+        wl[rows_of(p, 96), col] = ref[base : base + 96, :]
+        ws[rows_of(p, 80), col] = ref[base + 96 : base + 176, :]
+        base = A_ROWS + 96 * n
+        wp[rows_of(p, 96), col] = ref[base : base + 96, :]
+
+
+def early_kernel(idx, skip_own, skip_oth, *refs):
+    pieces, (wl, ws, wp, part, late), (skip,) = refs[:12], refs[12:17], refs[17:]
     x, y, z, c = idx[0], idx[1], idx[2], idx[3]
-
-    def add(ref, zz, yy, col):
-        for n, cc in ((0, c), (176, 1 - c)):
-            p = 4 * zz + 2 * yy + cc
-            wl[rows_of(p, 96), col] = ref[n : n + 96, :]
-            ws[rows_of(p, 80), col] = ref[n + 96 : n + 176, :]
-
-    own, b0, xb0 = pieces[:3]
-    add(own, z, y, ALL)
-    add(b0, z, 1 - y, quarter(x))
-    add(xb0, z, 1 - y, quarter(1 - x))
-    for k in range(1, 4):
-        zz = lax.rem(z + 4 - k, 4)
-        a, b, xa, xb = pieces[4 * k - 1 : 4 * k + 3]
-        add(a, zz, y, quarter(x))
-        add(b, zz, 1 - y, quarter(x))
-        add(xa, zz, y, quarter(1 - x))
-        add(xb, zz, 1 - y, quarter(1 - x))
+    last = lax.rem(z + 1, 4)
+    ws[rows_of(last, 320), :] = jnp.zeros((320, 768), BF16)
+    keep, got, b0, d0 = pieces[:4]
+    for ref, cc in ((keep, c), (got, 1 - c)):
+        p = 4 * z + 2 * y + cc
+        wl[rows_of(p, 96), :] = ref[:96, :]
+        ws[rows_of(p, 80), :] = ref[96:176, :]
+        wp[rows_of(p, 96), :] = ref[176:, :]
+    place(b0, z, 1 - y, c, quarter(x), wl, ws, wp)
+    place(d0, z, 1 - y, c, quarter(1 - x), wl, ws, wp)
+    for k in (1, 2):
+        place_plane(pieces[4 * k : 4 * k + 4], lax.rem(z + 4 - k, 4), x, y, c, wl, ws, wp)
     for s in range(2):
-        for src_a, src_s, cc in ((act_own, skip_own, c), (act_oth, skip_oth, 1 - c)):
-            act[pl.ds(pl.multiple_of(128 * s + 64 * cc, 64), 64), :] = src_a[
+        for src, cc in ((skip_own, c), (skip_oth, 1 - c)):
+            skip[pl.ds(pl.multiple_of(256 * s + 128 * cc, 128), 128), :] = src[
+                pl.ds(128 * s, 128), :
+            ]
+    for zz in range(4):
+
+        @pl.when(last == zz)
+        def _():
+            late[...] = skip[:, 320 * zz : 320 * (zz + 1)]
+
+    part[...] = jnp.dot(skip[...], ws[...], preferred_element_type=F32)
+
+
+def place_plane(pieces, zz, x, y, c, wl, ws, wp):
+    a, b, xa, xb = pieces
+    place(a, zz, y, c, quarter(x), wl, ws, wp)
+    place(b, zz, 1 - y, c, quarter(x), wl, ws, wp)
+    place(xa, zz, y, c, quarter(1 - x), wl, ws, wp)
+    place(xb, zz, 1 - y, c, quarter(1 - x), wl, ws, wp)
+
+
+WEIGHTS = [
+    jax.ShapeDtypeStruct((1536, 768), BF16),
+    jax.ShapeDtypeStruct((1280, 768), BF16),
+    jax.ShapeDtypeStruct((1536, 768), BF16),
+]
+
+
+def early(idx, skip_own, skip_oth, pieces):
+    return pl.pallas_call(
+        early_kernel,
+        out_shape=WEIGHTS
+        + [jax.ShapeDtypeStruct((512, 768), F32), jax.ShapeDtypeStruct((512, 320), BF16)],
+        in_specs=[SMEM] + [VMEM] * (2 + len(pieces)),
+        out_specs=[VMEM] * 5,
+        scratch_shapes=[pltpu.VMEM((512, 1280), BF16)],
+        compiler_params=LIMIT,
+        name="early",
+    )(idx, skip_own, skip_oth, *pieces)
+
+
+def merge_kernel(idx, act_own, act_oth, wl_in, ws_in, wp_in, part, late, *refs):
+    del wl_in, ws_in, wp_in
+    pieces, (merged, wl, ws, wp), (act,) = refs[:4], refs[4:8], refs[8:]
+    x, y, z, c = idx[0], idx[1], idx[2], idx[3]
+    last = lax.rem(z + 1, 4)
+    place_plane(pieces, last, x, y, c, wl, ws, wp)
+    for s in range(2):
+        for src, cc in ((act_own, c), (act_oth, 1 - c)):
+            act[pl.ds(pl.multiple_of(128 * s + 64 * cc, 64), 64), :] = src[
                 pl.ds(64 * s, 64), :
             ]
-            skip[pl.ds(pl.multiple_of(256 * s + 128 * cc, 128), 128), :] = src_s[
-                pl.ds(128 * s, 128), :
-            ]
-    act[256:272, :] = jnp.concatenate(
-        [before[:, :1536], after[:, :1536], jnp.zeros((12, 1536), BF16)], axis=0
-    )
-    skip[512:528, :] = jnp.concatenate(
-        [before[:, 1536:], after[:, 1536:], jnp.zeros((12, 1280), BF16)], axis=0
-    )
     twice = (
         lax.broadcasted_iota(jnp.int32, (256, 128), 0) // 2
         == lax.broadcasted_iota(jnp.int32, (256, 128), 1)
     ).astype(BF16)
     lifted = jnp.dot(act[...], wl[...], preferred_element_type=F32).astype(BF16)
-    terms = jnp.dot(skip[...], ws[...], preferred_element_type=F32)
+    terms = part[...] + jnp.dot(
+        late[...], ws[rows_of(last, 320), :], preferred_element_type=F32
+    )
     for s in range(2):
-        term = terms[256 * s : 256 * (s + 1)]
         raised = jnp.dot(twice, lifted[128 * s : 128 * (s + 1)], preferred_element_type=F32)
-        total = (raised + term).astype(BF16)
-        merged[s, :, :] = total
-    ends[...] = (lifted[256:272].astype(F32) + terms[512:528]).astype(BF16)
-
-
-def merge(idx, act_own, act_oth, skip_own, skip_oth, before, after, pieces):
+        merged[s, :, :] = (raised + terms[256 * s : 256 * (s + 1)]).astype(BF16)
+
+
+def merge(idx, act_own, act_oth, weights, part, late, pieces):
     return pl.pallas_call(
         merge_kernel,
-        out_shape=[
-            jax.ShapeDtypeStruct((2, 256, 768), BF16),
-            jax.ShapeDtypeStruct((16, 768), BF16),
-        ],
-        in_specs=[SMEM] + [VMEM] * (6 + len(pieces)),
-        out_specs=[VMEM] * 2,
-        scratch_shapes=[
-            pltpu.VMEM((1536, 768), BF16),
-            pltpu.VMEM((1280, 768), BF16),
-            pltpu.VMEM((272, 1536), BF16),
-            pltpu.VMEM((528, 1280), BF16),
-        ],
+        out_shape=[jax.ShapeDtypeStruct((2, 256, 768), BF16)] + WEIGHTS,
+        in_specs=[SMEM] + [VMEM] * (7 + len(pieces)),
+        out_specs=[VMEM] * 4,
+        scratch_shapes=[pltpu.VMEM((256, 1536), BF16)],
+        input_output_aliases={3: 1, 4: 2, 5: 3},
         compiler_params=LIMIT,
         name="merge",
-    )(idx, act_own, act_oth, skip_own, skip_oth, before, after, *pieces)
-
-
-def point_kernel(idx, depth, merged, ends, *refs):
-    pieces, (own, oth), (wp, spread) = refs[:15], refs[15:17], refs[17:]
-    x, y, z, c = idx[0], idx[1], idx[2], idx[3]
-
-    def add(ref, zz, yy, col):
-        base = A_ROWS
-        for n, cc in ((base, c), (base + 96, 1 - c)):
-            wp[rows_of(4 * zz + 2 * yy + cc, 96), col] = ref[n : n + 96, :]
-
-    full, b0, xb0 = pieces[:3]
-    add(full, z, y, ALL)
-    add(b0, z, 1 - y, quarter(x))
-    add(xb0, z, 1 - y, quarter(1 - x))
-    for k in range(1, 4):
-        zz = lax.rem(z + 4 - k, 4)
-        a, b, xa, xb = pieces[4 * k - 1 : 4 * k + 3]
-        add(a, zz, y, quarter(x))
-        add(b, zz, 1 - y, quarter(x))
-        add(xa, zz, y, quarter(1 - x))
-        add(xb, zz, 1 - y, quarter(1 - x))
+    )(idx, act_own, act_oth, *weights, part, late, *pieces)
+
+
+def point_kernel(idx, depth, merged, wl, ws, wp, far, far_oth, oth, rest, spread):
+    c = idx[3]
+    ends = jnp.where(
+        c == 0,
+        jnp.concatenate([far[...], far_oth[...]], axis=0),
+        jnp.concatenate([far_oth[...], far[...]], axis=0),
+    )
+    lifted = jnp.dot(ends[:, :1536], wl[...], preferred_element_type=F32).astype(BF16)
+    ends = lifted.astype(F32) + jnp.dot(ends[:, 1536:], ws[...], preferred_element_type=F32)
+    ends = ends.astype(BF16).astype(F32)
     taps = depth[:, pl.ds(pl.multiple_of(c * 768, 768), 768)]
     row = lax.broadcasted_iota(jnp.int32, (256, 768), 0)
     for s in range(2):
         here = merged[s, :, :].astype(F32)
-        up = jnp.where(row == 0, ends[s : s + 1, :].astype(F32), pltpu.roll(here, 1, 0))
-        down = jnp.where(row == 255, ends[s + 2 : s + 3, :].astype(F32), pltpu.roll(here, 255, 0))
+        up = jnp.where(row == 0, ends[s : s + 1, :], pltpu.roll(here, 1, 0))
+        down = jnp.where(row == 255, ends[s + 16 : s + 17, :], pltpu.roll(here, 255, 0))
         spread[pl.ds(256 * s, 256), :] = (
             taps[0:1] * up + taps[1:2] * here + taps[2:3] * down
         ).astype(BF16)
-    for out, cc in ((oth, 1 - c), (own, c)):
-        part = jnp.concatenate(
-            [
-                spread[pl.ds(pl.multiple_of(256 * s + 128 * cc, 128), 128), :]
-                for s in range(2)
-            ],
-            axis=0,
-        )
-        out[...] = (
-            lax.dot_general(part, wp[...], (((1,), (1,)), ((), ())), preferred_element_type=F32)
-            .astype(out.dtype)
-            .reshape(out.shape)
-        )
-
-
-def point(idx, depth, merged, ends, pieces):
+    for s in range(2):
+        rest[pl.ds(128 * s, 128), :] = spread[
+            pl.ds(pl.multiple_of(256 * s + 128 * c, 128), 128), :
+        ]
+    part = jnp.concatenate(
+        [
+            spread[pl.ds(pl.multiple_of(256 * s + 128 * (1 - c), 128), 128), :]
+            for s in range(2)
+        ],
+        axis=0,
+    )
+    oth[...] = across(part, wp[...]).astype(BF16).reshape(oth.shape)
+
+
+def across(rows, w):
+    return lax.dot_general(rows, w, (((1,), (1,)), ((), ())), preferred_element_type=F32)
+
+
+def point(idx, depth, merged, weights, far, far_oth):
     return pl.pallas_call(
         point_kernel,
         out_shape=[
-            jax.ShapeDtypeStruct((2, 128, 1536), F32),
             jax.ShapeDtypeStruct((2, 128, 1536), BF16),
+            jax.ShapeDtypeStruct((256, 768), BF16),
         ],
-        in_specs=[SMEM] + [VMEM] * (3 + len(pieces)),
+        in_specs=[SMEM] + [VMEM] * 7,
         out_specs=[VMEM] * 2,
-        scratch_shapes=[
-            pltpu.VMEM((1536, 768), BF16),
-            pltpu.VMEM((512, 768), BF16),
-        ],
+        scratch_shapes=[pltpu.VMEM((512, 768), BF16)],
         compiler_params=LIMIT,
         name="point",
-    )(idx, depth, merged, ends, *pieces)
+    )(idx, depth, merged, *weights, far, far_oth)
+
+
+def rest_kernel(rest, wp, own):
+    own[...] = across(rest[...], wp[...]).reshape(own.shape)
+
+
+def point_rest(rest, wp):
+    return pl.pallas_call(
+        rest_kernel,
+        out_shape=jax.ShapeDtypeStruct((2, 128, 1536), F32),
+        in_specs=[VMEM] * 2,
+        out_specs=VMEM,
+        compiler_params=LIMIT,
+        name="point_rest",
+    )(rest, wp)
 
 
 def behind(v, *tokens):
@@ -391,56 +428,45 @@
     )(idx, wl, ws, wp)
 
 
-def join_kernel(idx, keep, got, full, quart, rest):
+def take_kernel(idx, keep, got, out, *, other):
     x = idx[0]
+    cols = quarter(1 - x if other else x)
     for n, ref in enumerate((keep, got)):
-        for dst, src in (
-            (slice(176 * n, 176 * (n + 1)), slice(0, 176)),
-            (slice(352 + 96 * n, 352 + 96 * (n + 1)), slice(176, 272)),
-        ):
-            full[dst, :] = ref[src, :]
-            quart[dst, :] = ref[src, quarter(x)]
-            rest[dst, :] = ref[src, quarter(1 - x)]
-
-
-def join(idx, keep, got):
-    return pl.pallas_call(
-        join_kernel,
-        out_shape=[
-            jax.ShapeDtypeStruct(shape, BF16) for shape in ((544, 768), (544, 384), (544, 384))
-        ],
+        out[176 * n : 176 * (n + 1), :] = ref[:176, cols]
+        out[A_ROWS + 96 * n : A_ROWS + 96 * (n + 1), :] = ref[176:, cols]
+
+
+def take(idx, keep, got, other):
+    return pl.pallas_call(
+        functools.partial(take_kernel, other=other),
+        out_shape=jax.ShapeDtypeStruct((544, 384), BF16),
         in_specs=[SMEM] + [VMEM] * 2,
-        out_specs=[VMEM] * 3,
-        compiler_params=LIMIT,
-        name="join",
+        out_specs=VMEM,
+        compiler_params=LIMIT,
+        name="take",
     )(idx, keep, got)
 
 
-def edges_kernel(idx, act_own, act_oth, skip_own, skip_oth, low, high):
+def give_kernel(idx, act, skip, out):
     c = idx[3]
-    for first, last, mine in (
-        ((act_own, skip_own), (act_oth, skip_oth), 0),
-        ((act_oth, skip_oth), (act_own, skip_own), 1),
-    ):
-
-        @pl.when(c == mine)
-        def _():
-            for s in range(2):
-                for cols, n, rows in ((slice(0, 1536), 0, 64), (slice(1536, 2816), 1, 128)):
-                    low[s : s + 1, cols] = first[n][rows * s : rows * s + 1, :]
-                    end = rows * (s + 1)
-                    high[s : s + 1, cols] = last[n][end - 1 : end, :]
-
-
-def edges(idx, act_own, act_oth, skip_own, skip_oth):
-    return pl.pallas_call(
-        edges_kernel,
-        out_shape=[jax.ShapeDtypeStruct((2, 2816), BF16)] * 2,
-        in_specs=[SMEM] + [VMEM] * 4,
-        out_specs=[VMEM] * 2,
-        compiler_params=LIMIT,
-        name="edges",
-    )(idx, act_own, act_oth, skip_own, skip_oth)
+    out[2:16, :] = jnp.zeros((14, 2816), BF16)
+    for s in range(2):
+        for src, height, cols in ((act, 64, slice(0, 1536)), (skip, 128, slice(1536, 2816))):
+            low, high = height * s, height * (s + 1) - 1
+            out[s : s + 1, cols] = jnp.where(
+                c == 0, src[low : low + 1, :], src[high : high + 1, :]
+            )
+
+
+def give(idx, act, skip):
+    return pl.pallas_call(
+        give_kernel,
+        out_shape=jax.ShapeDtypeStruct((16, 2816), BF16),
+        in_specs=[SMEM, VMEM, VMEM],
+        out_specs=VMEM,
+        compiler_params=LIMIT,
+        name="give",
+    )(idx, act, skip)
 
 
 def on_device(
@@ -451,7 +477,8 @@
     idx = jnp.stack([x, y, z, c]).astype(jnp.int32)
     flat = acts.reshape(128, 1536)
     keep, send = split(idx, *map(in_hbm, (w_lift, w_skip, w_point.T)))
-    full, u0, c0 = join(idx, keep, c_swap(send))
+    got = c_swap(send)
+    u0 = take(idx, keep, got, False)
 
     def projected():
         return project(
@@ -475,22 +502,20 @@
 
     makers = {
         "u0": lambda: u0,
-        "c0": lambda: c0,
+        "c0": lambda: take(idx, keep, got, True),
         "packs": projected,
         "k0": joined,
         "mixes": attended,
         "act": lambda: output(idx, flat, w_out, [plan[n] for n in ("m0", "mc", "my", "mcy")]),
         "skip": lambda: jax.nn.gelu(skips.astype(F32)).astype(BF16).reshape(256, 1280),
-        "edges": lambda: edges(idx, *(plan[n] for n in ("act", "actc", "skip", "skipc"))),
-        "low": lambda: plan["edges"][0],
-        "high": lambda: plan["edges"][1],
+        "edge": lambda: give(idx, plan["act"], plan["skip"]),
     }
     for n, way in enumerate(("0", "c", "y", "cy")):
         makers["p" + way] = lambda n=n: plan["packs"][n]
         makers["o" + way] = lambda n=n: plan["mixes"][n]
     makers["q0"], makers["m0"] = makers["p0"], makers["o0"]
     swaps = {"c": c_swap, "y": y_swap, "cy": cy_swap, "x": x_swap, "z": z_ring}
-    swaps |= {"up": over_pos(CHIP_UP), "down": over_pos(CHIP_DOWN)}
+    swaps["beyond"], swaps["beyond c"] = over_pos(BEYOND), over_pos(BEYOND_C)
 
     def sender(how, src):
         return lambda: plan.send(swaps[how], src)
@@ -500,15 +525,17 @@
     plan = Plan(WIDTH, makers)
     for name, _, _ in SENDS:
         plan[name]
-    pieces = [full, plan["b0"], plan["d0"]] + [
-        plan[part + str(k)] for k in (1, 2, 3) for part in "ubcd"
+    pieces = [keep, got, plan["b0"], plan["d0"]] + [
+        plan[part + str(k)] for k in (1, 2) for part in "ubcd"
     ]
-    merged, ends = merge(
-        idx, plan["act"], plan["actc"], plan["skip"], plan["skipc"], plan["before"],
-        plan["after"], pieces,
-    )
-    own, oth = point(idx, depth_kernel, merged, ends, pieces)
-    return (own + c_swap(oth).astype(F32)).astype(BF16)
+    *weights, part, late = early(idx, plan["skip"], plan["skipc"], pieces)
+    merged, *weights = merge(
+        idx, plan["act"], plan["actc"], weights, part, late,
+        [plan[part + "3"] for part in "ubcd"],
+    )
+    oth, rest = point(idx, depth_kernel, merged, weights, plan["far"], plan["farc"])
+    got = c_swap(oth)
+    return (point_rest(rest, weights[2]) + got.astype(F32)).astype(BF16)
 
 
 def extended(cells, sides, width):

time: 93 us -> 87.2 us (0.938)
  starting transfers between devices: 29.4 us -> 25.8 us
  waiting for transfers between devices: 45.1 us -> 41.7 us
  Pallas kernels: 15.7 us -> 17.7 us
    ppermute x24, waiting for transfers between devices: 45.1 us -> 37.5 us  [over_pos(): return lambda v: lax.ppermute(v, 'pos', pairs)]
    ppermute x5, waiting for transfers between devices: 0.01 us -> 4.16 us  [x_swap(): return lax.ppermute(v, 'group', X_SWAP)]
    ppermute x24, starting transfers between devices: 22.1 us -> 18.6 us  [over_pos(): return lambda v: lax.ppermute(v, 'pos', pairs)]
    pallas_call x2 -> x4, Pallas kernels: 1.25 us -> 4.47 us  [the longest x1 2.52 us: early(): pl.pallas_call(early_kernel, out_shape=WEIGHTS + [jax.ShapeDtypeStruct((5...]
    pallas_call x1, Pallas kernels: 3.07 us -> 2.1 us  [merge(): pl.pallas_call(merge_kernel, out_shape=[jax.ShapeDtypeStruct((2, 256, 768...]
  transfers between devices with their start and end apart: 29 -> 29, of which waited for: 13 -> 12; matrix products, arithmetic and copies ran while one was open for 1% -> 1% of each run, Pallas kernels for 7% -> 14%
where the time goes in v3:
time: 87.2 us; the launch traced here: 87.1 us
  waiting for transfers between devices  41.7 us (48%)
  starting transfers between devices  25.8 us (30%)
  Pallas kernels  17.7 us (20%)
  other arithmetic  1.61 us (2%)
    ppermute x24, waiting for transfers between devices, over_pos(): return lambda v: lax.ppermute(v, 'pos', pairs)  37.5 us
    ppermute x24, starting transfers between devices, over_pos(): return lambda v: lax.ppermute(v, 'pos', pairs)  18.6 us
    ppermute x5, starting transfers between devices, x_swap(): return lax.ppermute(v, 'group', X_SWAP)  7.2 us
    ppermute x5, waiting for transfers between devices, x_swap(): return lax.ppermute(v, 'group', X_SWAP)  4.16 us
    pallas_call x1, Pallas kernels, project(): pl.pallas_call(project_kernel, out_shape=[jax.ShapeDtypeStruct((rows, 384...  3.71 us
    pallas_call x1, Pallas kernels, point(): pl.pallas_call(point_kernel, out_shape=[jax.ShapeDtypeStruct((2, 128, 153...  2.93 us
    pallas_call x1, Pallas kernels, early(): pl.pallas_call(early_kernel, out_shape=WEIGHTS + [jax.ShapeDtypeStruct((5...  2.52 us
    pallas_call x1, Pallas kernels, merge(): pl.pallas_call(merge_kernel, out_shape=[jax.ShapeDtypeStruct((2, 256, 768...  2.1 us
  transfers between devices with their start and end apart: 29, of which 12 were waited for; matrix products, arithmetic and copies ran while one was open for 1% of the time, Pallas kernels for 14%

profile of v3, /device:TPU:0, one launch (start us, length us, event | category | flops | bytes accessed | tf_op | source)
XLA Modules:
  0.0 87.1 jit_solution(13872474692965376952)
XLA Ops:
  0.0 0.1 pad_add_fusion.idx
  0.1 1.8 %split.1 = (bf16[272,768]{1,0:T(8,128)(2,1)S(1)}, bf16[272,768]{1,0:T(8,128)(2,1)S(1)}) custom-call(s32[4]{0:T(128)S(1)} %pad_add_fusion.idx, bf16[96,1536]{1,0:T(8,128)(2,1)} %wl.1, bf16[80,1536]{1,0:T(8,128)(2,1)} %ws.1, bf16[96,1536]{1,0:T(8,128)(2,1)} %bitcast.19), custom_call_target="tpu_custom_call" | custom-call | tf_op jit(solution)/shard_map/split/pallas_call | solution.py:418
  1.9 0.5 collective-permute-start
  2.4 1.4 %collective-permute-done.got.refs_1_ = bf16[272,768]{1,0:T(8,128)(2,1)S(1)} collective-permute-done((bf16[272,768]{1,0:T(8,128)(2,1)S(1)}, bf16[272,768]{1,0:T(8,128)(2,1)S(1)}, u32[]{:S(2)}, u32[]{:S(2)}) %collective-permute-start) | collective-permute-done | bytes 417824 | tf_op jit(solution)/shard_map/ppermute | solution.py:64
  3.8 0.6 take.1
  4.4 3.0 %collective-permute-start.1 = (bf16[544,384]{1,0:T(8,128)(2,1)S(1)}, bf16[544,384]{1,0:T(8,128)(2,1)S(1)}, u32[]{:S(2)}, u32[]{:S(2)}) collective-permute-start(bf16[544,384]{1,0:T(8,128)(2,1)S(1)} %take.1), channel_id=1, source_target_pairs={{0,4},{1,5},{2,6},{3,7},{4,8},{5,9},{6,10},{7,11},{8,12},{9,13},{1... | collective-permute-start | bytes 1253384 | tf_op jit(solution)/shard_map/ppermute | solution.py:64
  7.4 1.5 %collective-permute-start.2 = (bf16[544,384]{1,0:T(8,128)(2,1)S(1)}, bf16[544,384]{1,0:T(8,128)(2,1)S(1)}, u32[]{:S(2)}, u32[]{:S(2)}) collective-permute-start(bf16[544,384]{1,0:T(8,128)(2,1)S(1)} %take.1), channel_id=1, source_target_pairs={{0,2},{1,3},{2,0},{3,1},{4,6},{5,7},{6,4},{7,5},{8,10},{9,11},{10,... | collective-permute-start | bytes 1253384 | tf_op jit(solution)/shard_map/ppermute | solution.py:64
  8.9 3.7 %project.1 = (bf16[128,384]{1,0:T(8,128)(2,1)S(1)}, bf16[128,384]{1,0:T(8,128)(2,1)S(1)}, bf16[128,384]{1,0:T(8,128)(2,1)S(1)}, bf16[128,384]{1,0:T(8,128)(2,1)S(1)}) custom-call(s32[4]{0:T(128)S(1)} %pad_add_fusion.idx, bf16[128,1536]{1,0:T(8,128)(2,1)} %bitcast.15, f32[1,1536]{1,0:T(1,128)S(1)} %reshape.25.gain, bf16[1536,256]{1,0:T(8,128)(2,1)} %wq_hbm.1, ...), custom_call_target="tpu_custom_call" | custom-call | tf_op jit(solution)/shard_map/project/pallas_call | solution.py:121
  12.6 0.0 copy-start.3
  12.7 0.6 collective-permute-start.3
  13.2 6.1 %collective-permute-done.1.refs_4_ = bf16[544,384]{1,0:T(8,128)(2,1)S(1)} collective-permute-done((bf16[544,384]{1,0:T(8,128)(2,1)S(1)}, bf16[544,384]{1,0:T(8,128)(2,1)S(1)}, u32[]{:S(2)}, u32[]{:S(2)}) %collective-permute-start.1) | collective-permute-done | bytes 417824 | tf_op jit(solution)/shard_map/ppermute | solution.py:64
  19.4 1.5 %collective-permute-start.8 = (bf16[544,384]{1,0:T(8,128)(2,1)S(1)}, bf16[544,384]{1,0:T(8,128)(2,1)S(1)}, u32[]{:S(2)}, u32[]{:S(2)}) collective-permute-start(bf16[544,384]{1,0:T(8,128)(2,1)S(1)} %collective-permute-done.1.refs_4_), channel_id=1, source_target_pairs={{0,16},{16,0},{1,17},{17,1},{2,18},{18,2},{3,19},{19,3},{4,20},{20... | collective-permute-start | bytes 1253384 | tf_op jit(solution)/shard_map/ppermute | solution.py:72
  20.9 0.0 collective-permute-done.3.refs_2_
  20.9 1.6 %collective-permute-start.5 = (bf16[128,384]{1,0:T(8,128)(2,1)S(1)}, bf16[128,384]{1,0:T(8,128)(2,1)S(1)}, u32[]{:S(2)}, u32[]{:S(2)}) collective-permute-start(bf16[128,384]{1,0:T(8,128)(2,1)S(1)} %get-tuple-element.57), channel_id=1, source_target_pairs={{0,3},{1,2},{2,1},{3,0},{4,7},{5,6},{6,5},{7,4},{8,11},{9,10},{10,... | collective-permute-start | bytes 294920 | tf_op jit(solution)/shard_map/ppermute | solution.py:64
  22.6 0.5 collective-permute-start.9
  23.1 0.0 collective-permute-done.4.refs_1_
  23.1 2.6 %collective-permute-done.5.refs_3_ = bf16[128,384]{1,0:T(8,128)(2,1)S(1)} collective-permute-done((bf16[128,384]{1,0:T(8,128)(2,1)S(1)}, bf16[128,384]{1,0:T(8,128)(2,1)S(1)}, u32[]{:S(2)}, u32[]{:S(2)}) %collective-permute-start.5) | collective-permute-done | bytes 98336 | tf_op jit(solution)/shard_map/ppermute | solution.py:64
  25.7 0.0 copy-start
  25.7 0.0 copy-start.1
  25.7 1.6 %collective-permute-start.6 = (bf16[512,256]{1,0:T(8,128)(2,1)S(1)}, bf16[512,256]{1,0:T(8,128)(2,1)S(1)}, u32[]{:S(2)}, u32[]{:S(2)}) collective-permute-start(bf16[512,256]{1,0:T(8,128)(2,1)S(1)} %bitcast.17), channel_id=1, source_target_pairs={{0,4},{1,5},{2,6},{3,7},{4,8},{5,9},{6,10},{7,11},{8,12},{9,13},{1... | collective-permute-start | bytes 786440 | tf_op jit(solution)/shard_map/ppermute | solution.py:64
  27.4 5.7 %collective-permute-done.7.refs_8_ = bf16[544,384]{1,0:T(8,128)(2,1)S(1)} collective-permute-done((bf16[544,384]{1,0:T(8,128)(2,1)S(1)}, bf16[544,384]{1,0:T(8,128)(2,1)S(1)}, u32[]{:S(2)}, u32[]{:S(2)}) %collective-permute-start.7) | collective-permute-done | bytes 417824 | tf_op jit(solution)/shard_map/ppermute | solution.py:64
  33.1 1.2 %collective-permute-start.11 = (bf16[544,384]{1,0:T(8,128)(2,1)S(1)}, bf16[544,384]{1,0:T(8,128)(2,1)S(1)}, u32[]{:S(2)}, u32[]{:S(2)}) collective-permute-start(bf16[544,384]{1,0:T(8,128)(2,1)S(1)} %collective-permute-done.7.refs_8_), channel_id=1, source_target_pairs={{0,16},{16,0},{1,17},{17,1},{2,18},{18,2},{3,19},{19,3},{4,20},{20... | collective-permute-start | bytes 1253384 | tf_op jit(solution)/shard_map/ppermute | solution.py:72
  34.3 0.0 collective-permute-done.8.refs_6_
  34.3 1.5 %collective-permute-start.12 = (bf16[544,384]{1,0:T(8,128)(2,1)S(1)}, bf16[544,384]{1,0:T(8,128)(2,1)S(1)}, u32[]{:S(2)}, u32[]{:S(2)}) collective-permute-start(bf16[544,384]{1,0:T(8,128)(2,1)S(1)} %collective-permute-done.7.refs_8_), channel_id=1, source_target_pairs={{0,2},{1,3},{2,0},{3,1},{4,6},{5,7},{6,4},{7,5},{8,10},{9,11},{10,... | collective-permute-start | bytes 1253384 | tf_op jit(solution)/shard_map/ppermute | solution.py:64
  35.9 0.0 collective-permute-start.14
  35.9 2.6 %collective-permute-done.6.refs_5_ = bf16[512,256]{1,0:T(8,128)(2,1)S(1)} collective-permute-done((bf16[512,256]{1,0:T(8,128)(2,1)S(1)}, bf16[512,256]{1,0:T(8,128)(2,1)S(1)}, u32[]{:S(2)}, u32[]{:S(2)}) %collective-permute-start.6) | collective-permute-done | bytes 262176 | tf_op jit(solution)/shard_map/ppermute | solution.py:64
  38.5 0.0 collective-permute-done.9.refs_5_
  38.5 0.0 collective-permute-start.10
  38.5 4.2 %collective-permute-done.11.refs_10_ = bf16[544,384]{1,0:T(8,128)(2,1)S(1)} collective-permute-done((bf16[544,384]{1,0:T(8,128)(2,1)S(1)}, bf16[544,384]{1,0:T(8,128)(2,1)S(1)}, u32[]{:S(2)}, u32[]{:S(2)}) %collective-permute-start.11) | collective-permute-done | bytes 417824 | tf_op jit(solution)/shard_map/ppermute | solution.py:72
  42.6 1.0 %collective-permute-start.15 = (bf16[544,384]{1,0:T(8,128)(2,1)S(1)}, bf16[544,384]{1,0:T(8,128)(2,1)S(1)}, u32[]{:S(2)}, u32[]{:S(2)}) collective-permute-start(bf16[544,384]{1,0:T(8,128)(2,1)S(1)} %collective-permute-done.11.refs_10_), channel_id=1, source_target_pairs={{0,2},{1,3},{2,0},{3,1},{4,6},{5,7},{6,4},{7,5},{8,10},{9,11},{10,... | collective-permute-start | bytes 1253384 | tf_op jit(solution)/shard_map/ppermute | solution.py:64
  43.6 1.8 %collective-permute-start.16 = (bf16[544,384]{1,0:T(8,128)(2,1)S(1)}, bf16[544,384]{1,0:T(8,128)(2,1)S(1)}, u32[]{:S(2)}, u32[]{:S(2)}) collective-permute-start(bf16[544,384]{1,0:T(8,128)(2,1)S(1)} %collective-permute-done.2.refs_2_), channel_id=1, source_target_pairs={{0,16},{16,0},{1,17},{17,1},{2,18},{18,2},{3,19},{19,3},{4,20},{20... | collective-permute-start | bytes 1253384 | tf_op jit(solution)/shard_map/ppermute | solution.py:72
  45.4 7.1 %collective-permute-done.10.refs_6_ = bf16[512,256]{1,0:T(8,128)(2,1)S(1)} collective-permute-done((bf16[512,256]{1,0:T(8,128)(2,1)S(1)}, bf16[512,256]{1,0:T(8,128)(2,1)S(1)}, u32[]{:S(2)}, u32[]{:S(2)}) %collective-permute-start.10) | collective-permute-done | bytes 262176 | tf_op jit(solution)/shard_map/ppermute | solution.py:64
  52.5 0.0 collective-permute-done.12.refs_9_
  52.5 1.3 %collective-permute-start.20 = (bf16[544,384]{1,0:T(8,128)(2,1)S(1)}, bf16[544,384]{1,0:T(8,128)(2,1)S(1)}, u32[]{:S(2)}, u32[]{:S(2)}) collective-permute-start(bf16[544,384]{1,0:T(8,128)(2,1)S(1)} %collective-permute-done.14.refs_0_), channel_id=1, source_target_pairs={{0,2},{1,3},{2,0},{3,1},{4,6},{5,7},{6,4},{7,5},{8,10},{9,11},{10,... | collective-permute-start | bytes 1253384 | tf_op jit(solution)/shard_map/ppermute | solution.py:64
  53.9 1.5 %collective-permute-start.21 = (bf16[544,384]{1,0:T(8,128)(2,1)S(1)}, bf16[544,384]{1,0:T(8,128)(2,1)S(1)}, u32[]{:S(2)}, u32[]{:S(2)}) collective-permute-start(bf16[544,384]{1,0:T(8,128)(2,1)S(1)} %collective-permute-done.9.refs_5_), channel_id=1, source_target_pairs={{0,16},{16,0},{1,17},{17,1},{2,18},{18,2},{3,19},{19,3},{4,20},{20... | collective-permute-start | bytes 1253384 | tf_op jit(solution)/shard_map/ppermute | solution.py:72
  55.4 0.4 fusion.5
  55.8 4.9 %collective-permute-done.13.refs_7_ = bf16[512,256]{1,0:T(8,128)(2,1)S(1)} collective-permute-done((bf16[512,256]{1,0:T(8,128)(2,1)S(1)}, bf16[512,256]{1,0:T(8,128)(2,1)S(1)}, u32[]{:S(2)}, u32[]{:S(2)}) %collective-permute-start.13) | collective-permute-done | bytes 262176 | tf_op jit(solution)/shard_map/ppermute | solution.py:64
  60.7 1.3 %attend.1 = (bf16[128,256]{1,0:T(8,128)(2,1)S(1)}, bf16[128,256]{1,0:T(8,128)(2,1)S(1)}, bf16[128,256]{1,0:T(8,128)(2,1)S(1)}, bf16[128,256]{1,0:T(8,128)(2,1)S(1)}) custom-call(bf16[128,384]{1,0:T(8,128)(2,1)S(1)} %get-tuple-element.52.refs_0_, bf16[128,384]{1,0:T(8,128)(2,1)S(1)} %collective-permute-done.4.refs_1_, ...), custom_call_target="tpu_custom_call" | custom-call | tf_op jit(solution)/shard_map/attend/pallas_call | solution.py:158
  62.0 0.0 collective-permute-done.16.refs_3_
  62.0 0.6 collective-permute-start.17
  62.6 1.3 %collective-permute-start.18 = (bf16[128,256]{1,0:T(8,128)(2,1)S(1)}, bf16[128,256]{1,0:T(8,128)(2,1)S(1)}, u32[]{:S(2)}, u32[]{:S(2)}) collective-permute-start(bf16[128,256]{1,0:T(8,128)(2,1)S(1)} %get-tuple-element.71), channel_id=1, source_target_pairs={{0,2},{1,3},{2,0},{3,1},{4,6},{5,7},{6,4},{7,5},{8,10},{9,11},{10,... | collective-permute-start | bytes 196616 | tf_op jit(solution)/shard_map/ppermute | solution.py:64
  63.9 0.0 collective-permute-done.20.refs_1_
  63.9 0.2 collective-permute-start.19
  64.0 0.0 collective-permute-done.17.refs_1_
  64.0 0.5 collective-permute-start.25
  64.6 2.3 %collective-permute-done.18.refs_2_ = bf16[128,256]{1,0:T(8,128)(2,1)S(1)} collective-permute-done((bf16[128,256]{1,0:T(8,128)(2,1)S(1)}, bf16[128,256]{1,0:T(8,128)(2,1)S(1)}, u32[]{:S(2)}, u32[]{:S(2)}) %collective-permute-start.18) | collective-permute-done | bytes 65568 | tf_op jit(solution)/shard_map/ppermute | solution.py:64
  66.9 1.2 %collective-permute-start.24 = (bf16[544,384]{1,0:T(8,128)(2,1)S(1)}, bf16[544,384]{1,0:T(8,128)(2,1)S(1)}, u32[]{:S(2)}, u32[]{:S(2)}) collective-permute-start(bf16[544,384]{1,0:T(8,128)(2,1)S(1)} %collective-permute-done.14.refs_0_), channel_id=1, source_target_pairs={{0,16},{16,0},{1,17},{17,1},{2,18},{18,2},{3,19},{19,3},{4,20},{20... | collective-permute-start | bytes 1253384 | tf_op jit(solution)/shard_map/ppermute | solution.py:72
  68.1 0.1 collective-permute-done.19.refs_3_
  68.2 1.3 %output.1.act_own.act = bf16[128,1536]{1,0:T(8,128)(2,1)S(1)} custom-call(s32[4]{0:T(128)S(1)} %pad_add_fusion.idx, bf16[128,1536]{1,0:T(8,128)(2,1)S(1)} %bitcast.16, bf16[768,1536]{1,0:T(8,128)(2,1)S(1)} %copy-done, bf16[128,256]{1,0:T(8,128)(2,1)S(1)} %get-tuple-element.64.refs_0_, bf16[128,256]{1,0:T(8,128)(2,1)S(1)} %collective-permute-done.17.refs_1_, ...), custom_call_target="tpu_custom_call" | custom-call | tf_op jit(solution)/shard_map/output/pallas_call | solution.py:182
  69.6 0.0 collective-permute-done.21.refs_7_
  69.6 0.2 collective-permute-start.22
  69.8 0.6 give.1
  70.3 0.7 collective-permute-start.26
  71.0 1.3 %collective-permute-start.27 = (bf16[16,2816]{1,0:T(8,128)(2,1)S(1)}, bf16[16,2816]{1,0:T(8,128)(2,1)S(1)}, u32[]{:S(2)}, u32[]{:S(2)}) collective-permute-start(bf16[16,2816]{1,0:T(8,128)(2,1)S(1)} %give.1), channel_id=1, source_target_pairs={{1,3},{2,0},{3,5},{4,2},{5,7},{6,4},{7,9},{8,6},{9,11},{10,8},{11,... | collective-permute-start | bytes 270344 | tf_op jit(solution)/shard_map/ppermute | solution.py:64
  72.3 2.5 %early.1 = (bf16[1536,768]{1,0:T(8,128)(2,1)S(1)}, bf16[1280,768]{1,0:T(8,128)(2,1)S(1)}, bf16[1536,768]{1,0:T(8,128)(2,1)S(1)}, f32[512,768]{1,0:T(8,128)S(1)}, bf16[512,320]{1,0:T(8,128)(2,1)S(1)}) custom-call(s32[4]{0:T(128)S(1)} %pad_add_fusion.idx, bf16[256,1280]{1,0:T(8,128)(2,1)S(1)} %bitcast.14, ...), custom_call_target="tpu_custom_call" | custom-call | tf_op jit(solution)/shard_map/early/pallas_call | solution.py:258
  74.9 3.4 %collective-permute-done.25.refs_3_ = bf16[544,384]{1,0:T(8,128)(2,1)S(1)} collective-permute-done((bf16[544,384]{1,0:T(8,128)(2,1)S(1)}, bf16[544,384]{1,0:T(8,128)(2,1)S(1)}, u32[]{:S(2)}, u32[]{:S(2)}) %collective-permute-start.25) | collective-permute-done | bytes 417824 | tf_op jit(solution)/shard_map/ppermute | solution.py:64
  78.3 0.0 collective-permute-done.24.refs_2_
  78.3 0.0 collective-permute-done.22.act_oth
  78.3 2.1 %merge.1 = (bf16[2,256,768]{2,1,0:T(8,128)(2,1)S(1)}, bf16[1536,768]{1,0:T(8,128)(2,1)S(1)}, bf16[1280,768]{1,0:T(8,128)(2,1)S(1)}, bf16[1536,768]{1,0:T(8,128)(2,1)S(1)}) custom-call(s32[4]{0:T(128)S(1)} %pad_add_fusion.idx, bf16[128,1536]{1,0:T(8,128)(2,1)S(1)} %output.1.act_own.act, ...), custom_call_target="tpu_custom_call", output_to_operand_aliasing={{1}: (3, {}), {2}: (4, {}), {3}: (5, {})} | custom-call | tf_op jit(solution)/shard_map/merge/pallas_call | solution.py:295
  80.4 2.9 %point.1 = (bf16[2,128,1536]{2,1,0:T(8,128)(2,1)S(1)}, bf16[256,768]{1,0:T(8,128)(2,1)S(1)}) custom-call(s32[4]{0:T(128)S(1)} %pad_add_fusion.idx, f32[3,1536]{1,0:T(4,128)S(1)} %copy-done.2, bf16[2,256,768]{2,1,0:T(8,128)(2,1)S(1)} %get-tuple-element.85.merged, bf16[1536,768]{1,0:T(8,128)(2,1)S(1)} %get-tuple-element.86.wl, ...), custom_call_target="tpu_custom_call" | custom-call | tf_op jit(solution)/shard_map/point/pallas_call | solution.py:345
  83.4 0.7 collective-permute-start.28
  84.1 0.8 point_rest.1
  84.9 1.1 %collective-permute-done.28 = bf16[2,128,1536]{2,1,0:T(8,128)(2,1)S(1)} collective-permute-done((bf16[2,128,1536]{2,1,0:T(8,128)(2,1)S(1)}, bf16[2,128,1536]{2,1,0:T(8,128)(2,1)S(1)}, u32[]{:S(2)}, u32[]{:S(2)}) %collective-permute-start.28) | collective-permute-done | bytes 786464 | tf_op jit(solution)/shard_map/ppermute | solution.py:64
  86.0 1.1 %add_convert_fusion = bf16[2,128,1536]{2,1,0:T(8,128)(2,1)} fusion(f32[2,128,1536]{2,1,0:T(8,128)S(1)} %point_rest.1, bf16[2,128,1536]{2,1,0:T(8,128)(2,1)S(1)} %collective-permute-done.28), kind=kLoop, calls=%fused_computation.4 | loop fusion | flops 1179648 | bytes 3145728 | tf_op jit(solution)/shard_map/convert_element_type | solution.py:538
  (23 shorter events, 0.1 us)
Async XLA Ops:
  0.0 8.9 %copy-start.4 = (f32[1536]{0:T(1024)S(1)}, f32[1536]{0:T(1024)}, u32[]{:S(2)}) copy-start(f32[1536]{0:T(1024)} %param.13) | copy-start | bytes 18436
  1.9 1.9 %collective-permute-start = (bf16[272,768]{1,0:T(8,128)(2,1)S(1)}, bf16[272,768]{1,0:T(8,128)(2,1)S(1)}, u32[]{:S(2)}, u32[]{:S(2)}) collective-permute-start(bf16[272,768]{1,0:T(8,128)(2,1)S(1)} %get-tuple-element.50), channel_id=1, source_target_pairs={{0,1},{1,0},{2,3},{3,2},{4,5},{5,4},{6,7},{7,6},{8,9},{9,8},{10,11... | collective-permute-start | bytes 1253384 | tf_op jit(solution)/shard_map/ppermute | solution.py:64
  4.4 15.0 %collective-permute-start.1 = (bf16[544,384]{1,0:T(8,128)(2,1)S(1)}, bf16[544,384]{1,0:T(8,128)(2,1)S(1)}, u32[]{:S(2)}, u32[]{:S(2)}) collective-permute-start(bf16[544,384]{1,0:T(8,128)(2,1)S(1)} %take.1), channel_id=1, source_target_pairs={{0,4},{1,5},{2,6},{3,7},{4,8},{5,9},{6,10},{7,11},{8,12},{9,13},{1... | collective-permute-start | bytes 1253384 | tf_op jit(solution)/shard_map/ppermute | solution.py:64
  7.4 13.5 %collective-permute-start.2 = (bf16[544,384]{1,0:T(8,128)(2,1)S(1)}, bf16[544,384]{1,0:T(8,128)(2,1)S(1)}, u32[]{:S(2)}, u32[]{:S(2)}) collective-permute-start(bf16[544,384]{1,0:T(8,128)(2,1)S(1)} %take.1), channel_id=1, source_target_pairs={{0,2},{1,3},{2,0},{3,1},{4,6},{5,7},{6,4},{7,5},{8,10},{9,11},{10,... | collective-permute-start | bytes 1253384 | tf_op jit(solution)/shard_map/ppermute | solution.py:64
  12.6 42.7 %copy-start.3 = (bf16[2,128,1280]{2,1,0:T(8,128)(2,1)S(1)}, bf16[2,128,1280]{2,1,0:T(8,128)(2,1)}, u32[]{:S(2)}) copy-start(bf16[2,128,1280]{2,1,0:T(8,128)(2,1)} %param.12) | copy-start | bytes 1966084
  12.7 8.3 %collective-permute-start.3 = (bf16[128,384]{1,0:T(8,128)(2,1)S(1)}, bf16[128,384]{1,0:T(8,128)(2,1)S(1)}, u32[]{:S(2)}, u32[]{:S(2)}) collective-permute-start(bf16[128,384]{1,0:T(8,128)(2,1)S(1)} %get-tuple-element.54), channel_id=1, source_target_pairs={{0,2},{1,3},{2,0},{3,1},{4,6},{5,7},{6,4},{7,5},{8,10},{9,11},{10,... | collective-permute-start | bytes 294920 | tf_op jit(solution)/shard_map/ppermute | solution.py:64
  19.4 13.8 %collective-permute-start.7 = (bf16[544,384]{1,0:T(8,128)(2,1)S(1)}, bf16[544,384]{1,0:T(8,128)(2,1)S(1)}, u32[]{:S(2)}, u32[]{:S(2)}) collective-permute-start(bf16[544,384]{1,0:T(8,128)(2,1)S(1)} %collective-permute-done.1.refs_4_), channel_id=1, source_target_pairs={{0,4},{1,5},{2,6},{3,7},{4,8},{5,9},{6,10},{7,11},{8,12},{9,13},{1... | collective-permute-start | bytes 1253384 | tf_op jit(solution)/shard_map/ppermute | solution.py:64
  19.4 15.0 %collective-permute-start.8 = (bf16[544,384]{1,0:T(8,128)(2,1)S(1)}, bf16[544,384]{1,0:T(8,128)(2,1)S(1)}, u32[]{:S(2)}, u32[]{:S(2)}) collective-permute-start(bf16[544,384]{1,0:T(8,128)(2,1)S(1)} %collective-permute-done.1.refs_4_), channel_id=1, source_target_pairs={{0,16},{16,0},{1,17},{17,1},{2,18},{18,2},{3,19},{19,3},{4,20},{20... | collective-permute-start | bytes 1253384 | tf_op jit(solution)/shard_map/ppermute | solution.py:72
  20.9 2.2 %collective-permute-start.4 = (bf16[128,384]{1,0:T(8,128)(2,1)S(1)}, bf16[128,384]{1,0:T(8,128)(2,1)S(1)}, u32[]{:S(2)}, u32[]{:S(2)}) collective-permute-start(bf16[128,384]{1,0:T(8,128)(2,1)S(1)} %get-tuple-element.55), channel_id=1, source_target_pairs={{0,1},{1,0},{2,3},{3,2},{4,5},{5,4},{6,7},{7,6},{8,9},{9,8},{10,11... | collective-permute-start | bytes 294920 | tf_op jit(solution)/shard_map/ppermute | solution.py:64
  20.9 4.8 %collective-permute-start.5 = (bf16[128,384]{1,0:T(8,128)(2,1)S(1)}, bf16[128,384]{1,0:T(8,128)(2,1)S(1)}, u32[]{:S(2)}, u32[]{:S(2)}) collective-permute-start(bf16[128,384]{1,0:T(8,128)(2,1)S(1)} %get-tuple-element.57), channel_id=1, source_target_pairs={{0,3},{1,2},{2,1},{3,0},{4,7},{5,6},{6,5},{7,4},{8,11},{9,10},{10,... | collective-permute-start | bytes 294920 | tf_op jit(solution)/shard_map/ppermute | solution.py:64
  22.6 15.9 %collective-permute-start.9 = (bf16[544,384]{1,0:T(8,128)(2,1)S(1)}, bf16[544,384]{1,0:T(8,128)(2,1)S(1)}, u32[]{:S(2)}, u32[]{:S(2)}) collective-permute-start(bf16[544,384]{1,0:T(8,128)(2,1)S(1)} %collective-permute-done.1.refs_4_), channel_id=1, source_target_pairs={{0,2},{1,3},{2,0},{3,1},{4,6},{5,7},{6,4},{7,5},{8,10},{9,11},{10,... | collective-permute-start | bytes 1253384 | tf_op jit(solution)/shard_map/ppermute | solution.py:64
  25.7 42.5 %copy-start = (bf16[768,1536]{1,0:T(8,128)(2,1)S(1)}, bf16[768,1536]{1,0:T(8,128)(2,1)}, u32[]{:S(2)}) copy-start(bf16[768,1536]{1,0:T(8,128)(2,1)} %wo.1) | copy-start | bytes 7077892
  25.7 42.5 %copy-start.1 = (bf16[2,64,1536]{2,1,0:T(8,128)(2,1)S(1)}, bf16[2,64,1536]{2,1,0:T(8,128)(2,1)}, u32[]{:S(2)}) copy-start(bf16[2,64,1536]{2,1,0:T(8,128)(2,1)} %param.11) | copy-start | bytes 1179652
  25.7 12.7 %collective-permute-start.6 = (bf16[512,256]{1,0:T(8,128)(2,1)S(1)}, bf16[512,256]{1,0:T(8,128)(2,1)S(1)}, u32[]{:S(2)}, u32[]{:S(2)}) collective-permute-start(bf16[512,256]{1,0:T(8,128)(2,1)S(1)} %bitcast.17), channel_id=1, source_target_pairs={{0,4},{1,5},{2,6},{3,7},{4,8},{5,9},{6,10},{7,11},{8,12},{9,13},{1... | collective-permute-start | bytes 786440 | tf_op jit(solution)/shard_map/ppermute | solution.py:64
  33.1 9.5 %collective-permute-start.11 = (bf16[544,384]{1,0:T(8,128)(2,1)S(1)}, bf16[544,384]{1,0:T(8,128)(2,1)S(1)}, u32[]{:S(2)}, u32[]{:S(2)}) collective-permute-start(bf16[544,384]{1,0:T(8,128)(2,1)S(1)} %collective-permute-done.7.refs_8_), channel_id=1, source_target_pairs={{0,16},{16,0},{1,17},{17,1},{2,18},{18,2},{3,19},{19,3},{4,20},{20... | collective-permute-start | bytes 1253384 | tf_op jit(solution)/shard_map/ppermute | solution.py:72
  34.3 18.2 %collective-permute-start.12 = (bf16[544,384]{1,0:T(8,128)(2,1)S(1)}, bf16[544,384]{1,0:T(8,128)(2,1)S(1)}, u32[]{:S(2)}, u32[]{:S(2)}) collective-permute-start(bf16[544,384]{1,0:T(8,128)(2,1)S(1)} %collective-permute-done.7.refs_8_), channel_id=1, source_target_pairs={{0,2},{1,3},{2,0},{3,1},{4,6},{5,7},{6,4},{7,5},{8,10},{9,11},{10,... | collective-permute-start | bytes 1253384 | tf_op jit(solution)/shard_map/ppermute | solution.py:64
  35.9 16.7 %collective-permute-start.14 = (bf16[544,384]{1,0:T(8,128)(2,1)S(1)}, bf16[544,384]{1,0:T(8,128)(2,1)S(1)}, u32[]{:S(2)}, u32[]{:S(2)}) collective-permute-start(bf16[544,384]{1,0:T(8,128)(2,1)S(1)} %collective-permute-done.7.refs_8_), channel_id=1, source_target_pairs={{0,4},{1,5},{2,6},{3,7},{4,8},{5,9},{6,10},{7,11},{8,12},{9,13},{1... | collective-permute-start | bytes 1253384 | tf_op jit(solution)/shard_map/ppermute | solution.py:64
  38.5 14.1 %collective-permute-start.10 = (bf16[512,256]{1,0:T(8,128)(2,1)S(1)}, bf16[512,256]{1,0:T(8,128)(2,1)S(1)}, u32[]{:S(2)}, u32[]{:S(2)}) collective-permute-start(bf16[512,256]{1,0:T(8,128)(2,1)S(1)} %collective-permute-done.6.refs_5_), channel_id=1, source_target_pairs={{0,4},{1,5},{2,6},{3,7},{4,8},{5,9},{6,10},{7,11},{8,12},{9,13},{1... | collective-permute-start | bytes 786440 | tf_op jit(solution)/shard_map/ppermute | solution.py:64
  42.6 19.4 %collective-permute-start.15 = (bf16[544,384]{1,0:T(8,128)(2,1)S(1)}, bf16[544,384]{1,0:T(8,128)(2,1)S(1)}, u32[]{:S(2)}, u32[]{:S(2)}) collective-permute-start(bf16[544,384]{1,0:T(8,128)(2,1)S(1)} %collective-permute-done.11.refs_10_), channel_id=1, source_target_pairs={{0,2},{1,3},{2,0},{3,1},{4,6},{5,7},{6,4},{7,5},{8,10},{9,11},{10,... | collective-permute-start | bytes 1253384 | tf_op jit(solution)/shard_map/ppermute | solution.py:64
  43.6 18.4 %collective-permute-start.16 = (bf16[544,384]{1,0:T(8,128)(2,1)S(1)}, bf16[544,384]{1,0:T(8,128)(2,1)S(1)}, u32[]{:S(2)}, u32[]{:S(2)}) collective-permute-start(bf16[544,384]{1,0:T(8,128)(2,1)S(1)} %collective-permute-done.2.refs_2_), channel_id=1, source_target_pairs={{0,16},{16,0},{1,17},{17,1},{2,18},{18,2},{3,19},{19,3},{4,20},{20... | collective-permute-start | bytes 1253384 | tf_op jit(solution)/shard_map/ppermute | solution.py:72
  52.5 8.2 %collective-permute-start.13 = (bf16[512,256]{1,0:T(8,128)(2,1)S(1)}, bf16[512,256]{1,0:T(8,128)(2,1)S(1)}, u32[]{:S(2)}, u32[]{:S(2)}) collective-permute-start(bf16[512,256]{1,0:T(8,128)(2,1)S(1)} %collective-permute-done.10.refs_6_), channel_id=1, source_target_pairs={{0,4},{1,5},{2,6},{3,7},{4,8},{5,9},{6,10},{7,11},{8,12},{9,13},{1... | collective-permute-start | bytes 786440 | tf_op jit(solution)/shard_map/ppermute | solution.py:64
  52.5 11.3 %collective-permute-start.20 = (bf16[544,384]{1,0:T(8,128)(2,1)S(1)}, bf16[544,384]{1,0:T(8,128)(2,1)S(1)}, u32[]{:S(2)}, u32[]{:S(2)}) collective-permute-start(bf16[544,384]{1,0:T(8,128)(2,1)S(1)} %collective-permute-done.14.refs_0_), channel_id=1, source_target_pairs={{0,2},{1,3},{2,0},{3,1},{4,6},{5,7},{6,4},{7,5},{8,10},{9,11},{10,... | collective-permute-start | bytes 1253384 | tf_op jit(solution)/shard_map/ppermute | solution.py:64
  53.9 15.7 %collective-permute-start.21 = (bf16[544,384]{1,0:T(8,128)(2,1)S(1)}, bf16[544,384]{1,0:T(8,128)(2,1)S(1)}, u32[]{:S(2)}, u32[]{:S(2)}) collective-permute-start(bf16[544,384]{1,0:T(8,128)(2,1)S(1)} %collective-permute-done.9.refs_5_), channel_id=1, source_target_pairs={{0,16},{16,0},{1,17},{17,1},{2,18},{18,2},{3,19},{19,3},{4,20},{20... | collective-permute-start | bytes 1253384 | tf_op jit(solution)/shard_map/ppermute | solution.py:72
  60.7 10.3 %collective-permute-start.23 = (bf16[256,1280]{1,0:T(8,128)(2,1)S(1)}, bf16[256,1280]{1,0:T(8,128)(2,1)S(1)}, u32[]{:S(2)}, u32[]{:S(2)}) collective-permute-start(bf16[256,1280]{1,0:T(8,128)(2,1)S(1)} %bitcast.12), channel_id=1, source_target_pairs={{0,1},{1,0},{2,3},{3,2},{4,5},{5,4},{6,7},{7,6},{8,9},{9,8},{10,11... | collective-permute-start | bytes 1966088 | tf_op jit(solution)/shard_map/ppermute | solution.py:64
  62.0 2.0 %collective-permute-start.17 = (bf16[128,256]{1,0:T(8,128)(2,1)S(1)}, bf16[128,256]{1,0:T(8,128)(2,1)S(1)}, u32[]{:S(2)}, u32[]{:S(2)}) collective-permute-start(bf16[128,256]{1,0:T(8,128)(2,1)S(1)} %get-tuple-element.69), channel_id=1, source_target_pairs={{0,1},{1,0},{2,3},{3,2},{4,5},{5,4},{6,7},{7,6},{8,9},{9,8},{10,11... | collective-permute-start | bytes 196616 | tf_op jit(solution)/shard_map/ppermute | solution.py:64
  62.6 4.3 %collective-permute-start.18 = (bf16[128,256]{1,0:T(8,128)(2,1)S(1)}, bf16[128,256]{1,0:T(8,128)(2,1)S(1)}, u32[]{:S(2)}, u32[]{:S(2)}) collective-permute-start(bf16[128,256]{1,0:T(8,128)(2,1)S(1)} %get-tuple-element.71), channel_id=1, source_target_pairs={{0,2},{1,3},{2,0},{3,1},{4,6},{5,7},{6,4},{7,5},{8,10},{9,11},{10,... | collective-permute-start | bytes 196616 | tf_op jit(solution)/shard_map/ppermute | solution.py:64
  63.9 4.3 %collective-permute-start.19 = (bf16[128,256]{1,0:T(8,128)(2,1)S(1)}, bf16[128,256]{1,0:T(8,128)(2,1)S(1)}, u32[]{:S(2)}, u32[]{:S(2)}) collective-permute-start(bf16[128,256]{1,0:T(8,128)(2,1)S(1)} %get-tuple-element.73), channel_id=1, source_target_pairs={{0,3},{1,2},{2,1},{3,0},{4,7},{5,6},{6,5},{7,4},{8,11},{9,10},{10,... | collective-permute-start | bytes 196616 | tf_op jit(solution)/shard_map/ppermute | solution.py:64
  64.0 14.3 %collective-permute-start.25 = (bf16[544,384]{1,0:T(8,128)(2,1)S(1)}, bf16[544,384]{1,0:T(8,128)(2,1)S(1)}, u32[]{:S(2)}, u32[]{:S(2)}) collective-permute-start(bf16[544,384]{1,0:T(8,128)(2,1)S(1)} %collective-permute-done.15.refs_11_), channel_id=1, source_target_pairs={{0,4},{1,5},{2,6},{3,7},{4,8},{5,9},{6,10},{7,11},{8,12},{9,13},{1... | collective-permute-start | bytes 1253384 | tf_op jit(solution)/shard_map/ppermute | solution.py:64
  66.9 11.4 %collective-permute-start.24 = (bf16[544,384]{1,0:T(8,128)(2,1)S(1)}, bf16[544,384]{1,0:T(8,128)(2,1)S(1)}, u32[]{:S(2)}, u32[]{:S(2)}) collective-permute-start(bf16[544,384]{1,0:T(8,128)(2,1)S(1)} %collective-permute-done.14.refs_0_), channel_id=1, source_target_pairs={{0,16},{16,0},{1,17},{17,1},{2,18},{18,2},{3,19},{19,3},{4,20},{20... | collective-permute-start | bytes 1253384 | tf_op jit(solution)/shard_map/ppermute | solution.py:72
  69.6 8.7 %collective-permute-start.22 = (bf16[128,1536]{1,0:T(8,128)(2,1)S(1)}, bf16[128,1536]{1,0:T(8,128)(2,1)S(1)}, u32[]{:S(2)}, u32[]{:S(2)}) collective-permute-start(bf16[128,1536]{1,0:T(8,128)(2,1)S(1)} %output.1.act_own.act), channel_id=1, source_target_pairs={{0,1},{1,0},{2,3},{3,2},{4,5},{5,4},{6,7},{7,6},{8,9},{9,8},{10,11... | collective-permute-start | bytes 1179656 | tf_op jit(solution)/shard_map/ppermute | solution.py:64
  70.3 10.1 %collective-permute-start.26 = (bf16[16,2816]{1,0:T(8,128)(2,1)S(1)}, bf16[16,2816]{1,0:T(8,128)(2,1)S(1)}, u32[]{:S(2)}, u32[]{:S(2)}) collective-permute-start(bf16[16,2816]{1,0:T(8,128)(2,1)S(1)} %give.1), channel_id=1, source_target_pairs={{1,2},{2,1},{3,4},{4,3},{5,6},{6,5},{7,8},{8,7},{9,10},{10,9},{11,... | collective-permute-start | bytes 270344 | tf_op jit(solution)/shard_map/ppermute | solution.py:64
  71.0 9.4 %collective-permute-start.27 = (bf16[16,2816]{1,0:T(8,128)(2,1)S(1)}, bf16[16,2816]{1,0:T(8,128)(2,1)S(1)}, u32[]{:S(2)}, u32[]{:S(2)}) collective-permute-start(bf16[16,2816]{1,0:T(8,128)(2,1)S(1)} %give.1), channel_id=1, source_target_pairs={{1,3},{2,0},{3,5},{4,2},{5,7},{6,4},{7,9},{8,6},{9,11},{10,8},{11,... | collective-permute-start | bytes 270344 | tf_op jit(solution)/shard_map/ppermute | solution.py:64
  78.3 2.1 %copy-start.2 = (f32[3,1536]{1,0:T(4,128)S(1)}, f32[3,1536]{1,0:T(4,128)}, u32[]{:S(2)}) copy-start(f32[3,1536]{1,0:T(4,128)} %depth.1) | copy-start | bytes 55300
  83.4 2.6 %collective-permute-start.28 = (bf16[2,128,1536]{2,1,0:T(8,128)(2,1)S(1)}, bf16[2,128,1536]{2,1,0:T(8,128)(2,1)S(1)}, u32[]{:S(2)}, u32[]{:S(2)}) collective-permute-start(bf16[2,128,1536]{2,1,0:T(8,128)(2,1)S(1)} %get-tuple-element.92), channel_id=1, source_target_pairs={{0,1},{1,0},{2,3},{3,2},{4,5},{5,4},{6,7},{7,6},{8,9},{9,8},{10,11... | collective-permute-start | bytes 2359304 | tf_op jit(solution)/shard_map/ppermute | solution.py:64

commit v4 on v3

--- a/solution.py
+++ b/solution.py
@@ -20,6 +20,7 @@
 
 WIDTH = 5
 CUMULATIVE = True
+FREE = ()
 SENDS = (
     ("u1", "z", "u0"),
     ("b0", "y", "u0"),
@@ -254,6 +255,12 @@
 ]
 
 
+def ordered(c, own, other):
+    return jnp.where(
+        c == 0, jnp.concatenate([own, other], axis=0), jnp.concatenate([other, own], axis=0)
+    )
+
+
 def early(idx, skip_own, skip_oth, pieces):
     return pl.pallas_call(
         early_kernel,
@@ -267,9 +274,9 @@
     )(idx, skip_own, skip_oth, *pieces)
 
 
-def merge_kernel(idx, act_own, act_oth, wl_in, ws_in, wp_in, part, late, *refs):
+def decode_kernel(idx, depth, act_own, act_oth, far, far_oth, wl_in, ws_in, wp_in, part, late, *refs):
     del wl_in, ws_in, wp_in
-    pieces, (merged, wl, ws, wp), (act,) = refs[:4], refs[4:8], refs[8:]
+    pieces, (oth, rest, wl, ws, wp), (act, spread) = refs[:4], refs[4:9], refs[9:]
     x, y, z, c = idx[0], idx[1], idx[2], idx[3]
     last = lax.rem(z + 1, 4)
     place_plane(pieces, last, x, y, c, wl, ws, wp)
@@ -278,6 +285,8 @@
             act[pl.ds(pl.multiple_of(128 * s + 64 * cc, 64), 64), :] = src[
                 pl.ds(64 * s, 64), :
             ]
+    beyond = ordered(c, far[...], far_oth[...])
+    act[256:288, :] = beyond[:, :1536]
     twice = (
         lax.broadcasted_iota(jnp.int32, (256, 128), 0) // 2
         == lax.broadcasted_iota(jnp.int32, (256, 128), 1)
@@ -286,38 +295,15 @@
     terms = part[...] + jnp.dot(
         late[...], ws[rows_of(last, 320), :], preferred_element_type=F32
     )
-    for s in range(2):
-        raised = jnp.dot(twice, lifted[128 * s : 128 * (s + 1)], preferred_element_type=F32)
-        merged[s, :, :] = (raised + terms[256 * s : 256 * (s + 1)]).astype(BF16)
-
-
-def merge(idx, act_own, act_oth, weights, part, late, pieces):
-    return pl.pallas_call(
-        merge_kernel,
-        out_shape=[jax.ShapeDtypeStruct((2, 256, 768), BF16)] + WEIGHTS,
-        in_specs=[SMEM] + [VMEM] * (7 + len(pieces)),
-        out_specs=[VMEM] * 4,
-        scratch_shapes=[pltpu.VMEM((256, 1536), BF16)],
-        input_output_aliases={3: 1, 4: 2, 5: 3},
-        compiler_params=LIMIT,
-        name="merge",
-    )(idx, act_own, act_oth, *weights, part, late, *pieces)
-
-
-def point_kernel(idx, depth, merged, wl, ws, wp, far, far_oth, oth, rest, spread):
-    c = idx[3]
-    ends = jnp.where(
-        c == 0,
-        jnp.concatenate([far[...], far_oth[...]], axis=0),
-        jnp.concatenate([far_oth[...], far[...]], axis=0),
-    )
-    lifted = jnp.dot(ends[:, :1536], wl[...], preferred_element_type=F32).astype(BF16)
-    ends = lifted.astype(F32) + jnp.dot(ends[:, 1536:], ws[...], preferred_element_type=F32)
+    ends = lifted[256:].astype(F32) + jnp.dot(
+        beyond[:, 1536:], ws[...], preferred_element_type=F32
+    )
     ends = ends.astype(BF16).astype(F32)
     taps = depth[:, pl.ds(pl.multiple_of(c * 768, 768), 768)]
     row = lax.broadcasted_iota(jnp.int32, (256, 768), 0)
     for s in range(2):
-        here = merged[s, :, :].astype(F32)
+        raised = jnp.dot(twice, lifted[128 * s : 128 * (s + 1)], preferred_element_type=F32)
+        here = (raised + terms[256 * s : 256 * (s + 1)]).astype(BF16).astype(F32)
         up = jnp.where(row == 0, ends[s : s + 1, :], pltpu.roll(here, 1, 0))
         down = jnp.where(row == 255, ends[s + 16 : s + 17, :], pltpu.roll(here, 255, 0))
         spread[pl.ds(256 * s, 256), :] = (
@@ -327,33 +313,35 @@
         rest[pl.ds(128 * s, 128), :] = spread[
             pl.ds(pl.multiple_of(256 * s + 128 * c, 128), 128), :
         ]
-    part = jnp.concatenate(
+    rows = jnp.concatenate(
         [
             spread[pl.ds(pl.multiple_of(256 * s + 128 * (1 - c), 128), 128), :]
             for s in range(2)
         ],
         axis=0,
     )
-    oth[...] = across(part, wp[...]).astype(BF16).reshape(oth.shape)
-
-
-def across(rows, w):
-    return lax.dot_general(rows, w, (((1,), (1,)), ((), ())), preferred_element_type=F32)
-
-
-def point(idx, depth, merged, weights, far, far_oth):
-    return pl.pallas_call(
-        point_kernel,
+    oth[...] = across(rows, wp[...]).astype(BF16).reshape(oth.shape)
+
+
+def decode(idx, depth, act_own, act_oth, far, far_oth, weights, part, late, pieces):
+    return pl.pallas_call(
+        decode_kernel,
         out_shape=[
             jax.ShapeDtypeStruct((2, 128, 1536), BF16),
             jax.ShapeDtypeStruct((256, 768), BF16),
-        ],
-        in_specs=[SMEM] + [VMEM] * 7,
-        out_specs=[VMEM] * 2,
-        scratch_shapes=[pltpu.VMEM((512, 768), BF16)],
-        compiler_params=LIMIT,
-        name="point",
-    )(idx, depth, merged, *weights, far, far_oth)
+        ]
+        + WEIGHTS,
+        in_specs=[SMEM] + [VMEM] * (10 + len(pieces)),
+        out_specs=[VMEM] * 5,
+        scratch_shapes=[pltpu.VMEM((288, 1536), BF16), pltpu.VMEM((512, 768), BF16)],
+        input_output_aliases={6: 2, 7: 3, 8: 4},
+        compiler_params=LIMIT,
+        name="decode",
+    )(idx, depth, act_own, act_oth, far, far_oth, *weights, part, late, *pieces)
+
+
+def across(rows, w):
+    return lax.dot_general(rows, w, (((1,), (1,)), ((), ())), preferred_element_type=F32)
 
 
 def rest_kernel(rest, wp, own):
@@ -384,13 +372,13 @@
             self.made[name] = self.makers[name]()
         return self.made[name]
 
-    def send(self, how, name):
+    def send(self, how, name, free):
         v = self[name]
-        if len(self.done) >= self.width:
+        if not free and len(self.done) >= self.width:
             late = self.done[: len(self.done) - self.width + 1]
             v = behind(v, *(late if CUMULATIVE else late[-1:]))
         got = how(v)
-        if how is not c_swap:
+        if not free and how is not c_swap:
             self.done.append(got)
         return got
 
@@ -517,23 +505,22 @@
     swaps = {"c": c_swap, "y": y_swap, "cy": cy_swap, "x": x_swap, "z": z_ring}
     swaps["beyond"], swaps["beyond c"] = over_pos(BEYOND), over_pos(BEYOND_C)
 
-    def sender(how, src):
-        return lambda: plan.send(swaps[how], src)
+    def sender(name, how, src):
+        return lambda: plan.send(swaps[how], src, name in FREE)
 
     for name, how, src in SENDS:
-        makers[name] = sender(how, src)
+        makers[name] = sender(name, how, src)
     plan = Plan(WIDTH, makers)
     for name, _, _ in SENDS:
         plan[name]
     pieces = [keep, got, plan["b0"], plan["d0"]] + [
-        plan[part + str(k)] for k in (1, 2) for part in "ubcd"
+        plan[kind + str(k)] for k in (1, 2) for kind in "ubcd"
     ]
     *weights, part, late = early(idx, plan["skip"], plan["skipc"], pieces)
-    merged, *weights = merge(
-        idx, plan["act"], plan["actc"], weights, part, late,
-        [plan[part + "3"] for part in "ubcd"],
-    )
-    oth, rest = point(idx, depth_kernel, merged, weights, plan["far"], plan["farc"])
+    oth, rest, *weights = decode(
+        idx, depth_kernel, *(plan[n] for n in ("act", "actc", "far", "farc")), weights, part, late,
+        [plan[kind + "3"] for kind in "ubcd"],
+    )
     got = c_swap(oth)
     return (point_rest(rest, weights[2]) + got.astype(F32)).astype(BF16)
 

time: 87.2 us -> 86.9 us (level)
  Pallas kernels: 17.7 us -> 16.3 us
    pallas_call x2 -> x1, Pallas kernels: 5.03 us -> 3.7 us  [decode(): pl.pallas_call(decode_kernel, out_shape=[jax.ShapeDtypeStruct((2, 128, 15...]
  transfers between devices with their start and end apart: 29 -> 29, of which waited for: 12 -> 12; matrix products, arithmetic and copies ran while one was open for 1% -> 1% of each run, Pallas kernels for 14% -> 12%
where the time goes in v4:
time: 86.9 us; the launch traced here: 86.5 us
  waiting for transfers between devices  42 us (48%)
  starting transfers between devices  26.3 us (30%)
  Pallas kernels  16.3 us (19%)
  other arithmetic  1.64 us (2%)
    ppermute x24, waiting for transfers between devices, over_pos(): return lambda v: lax.ppermute(v, 'pos', pairs)  37.8 us
    ppermute x24, starting transfers between devices, over_pos(): return lambda v: lax.ppermute(v, 'pos', pairs)  19.1 us
    ppermute x5, starting transfers between devices, x_swap(): return lax.ppermute(v, 'group', X_SWAP)  7.2 us
    ppermute x5, waiting for transfers between devices, x_swap(): return lax.ppermute(v, 'group', X_SWAP)  4.16 us
    pallas_call x1, Pallas kernels, project(): pl.pallas_call(project_kernel, out_shape=[jax.ShapeDtypeStruct((rows, 384...  3.71 us
    pallas_call x1, Pallas kernels, decode(): pl.pallas_call(decode_kernel, out_shape=[jax.ShapeDtypeStruct((2, 128, 15...  3.7 us
    pallas_call x1, Pallas kernels, early(): pl.pallas_call(early_kernel, out_shape=WEIGHTS + [jax.ShapeDtypeStruct((5...  2.52 us
    pallas_call x1, Pallas kernels, split(): pl.pallas_call(split_kernel, out_shape=[jax.ShapeDtypeStruct((272, 768),...  1.82 us
  transfers between devices with their start and end apart: 29, of which 12 were waited for; matrix products, arithmetic and copies ran while one was open for 1% of the time, Pallas kernels for 12%

profile of v4, /device:TPU:0, one launch (start us, length us, event | category | flops | bytes accessed | tf_op | source)
XLA Modules:
  0.0 86.5 jit_solution(9835759462686882563)
XLA Ops:
  0.0 0.1 pad_add_fusion.idx
  0.1 1.8 %split.1 = (bf16[272,768]{1,0:T(8,128)(2,1)S(1)}, bf16[272,768]{1,0:T(8,128)(2,1)S(1)}) custom-call(s32[4]{0:T(128)S(1)} %pad_add_fusion.idx, bf16[96,1536]{1,0:T(8,128)(2,1)} %wl.1, bf16[80,1536]{1,0:T(8,128)(2,1)} %ws.1, bf16[96,1536]{1,0:T(8,128)(2,1)} %bitcast.19), custom_call_target="tpu_custom_call" | custom-call | tf_op jit(solution)/shard_map/split/pallas_call | solution.py:406
  1.9 0.5 collective-permute-start
  2.4 1.4 %collective-permute-done.got.refs_1_ = bf16[272,768]{1,0:T(8,128)(2,1)S(1)} collective-permute-done((bf16[272,768]{1,0:T(8,128)(2,1)S(1)}, bf16[272,768]{1,0:T(8,128)(2,1)S(1)}, u32[]{:S(2)}, u32[]{:S(2)}) %collective-permute-start) | collective-permute-done | bytes 417824 | tf_op jit(solution)/shard_map/ppermute | solution.py:65
  3.8 0.6 take.1
  4.4 3.0 %collective-permute-start.1 = (bf16[544,384]{1,0:T(8,128)(2,1)S(1)}, bf16[544,384]{1,0:T(8,128)(2,1)S(1)}, u32[]{:S(2)}, u32[]{:S(2)}) collective-permute-start(bf16[544,384]{1,0:T(8,128)(2,1)S(1)} %take.1), channel_id=1, source_target_pairs={{0,4},{1,5},{2,6},{3,7},{4,8},{5,9},{6,10},{7,11},{8,12},{9,13},{1... | collective-permute-start | bytes 1253384 | tf_op jit(solution)/shard_map/ppermute | solution.py:65
  7.4 1.5 %collective-permute-start.2 = (bf16[544,384]{1,0:T(8,128)(2,1)S(1)}, bf16[544,384]{1,0:T(8,128)(2,1)S(1)}, u32[]{:S(2)}, u32[]{:S(2)}) collective-permute-start(bf16[544,384]{1,0:T(8,128)(2,1)S(1)} %take.1), channel_id=1, source_target_pairs={{0,2},{1,3},{2,0},{3,1},{4,6},{5,7},{6,4},{7,5},{8,10},{9,11},{10,... | collective-permute-start | bytes 1253384 | tf_op jit(solution)/shard_map/ppermute | solution.py:65
  8.9 3.7 %project.1 = (bf16[128,384]{1,0:T(8,128)(2,1)S(1)}, bf16[128,384]{1,0:T(8,128)(2,1)S(1)}, bf16[128,384]{1,0:T(8,128)(2,1)S(1)}, bf16[128,384]{1,0:T(8,128)(2,1)S(1)}) custom-call(s32[4]{0:T(128)S(1)} %pad_add_fusion.idx, bf16[128,1536]{1,0:T(8,128)(2,1)} %bitcast.15, f32[1,1536]{1,0:T(1,128)S(1)} %reshape.25.gain, bf16[1536,256]{1,0:T(8,128)(2,1)} %wq_hbm.1, ...), custom_call_target="tpu_custom_call" | custom-call | tf_op jit(solution)/shard_map/project/pallas_call | solution.py:122
  12.6 0.0 copy-start.3
  12.7 0.6 collective-permute-start.3
  13.2 6.1 %collective-permute-done.1.refs_4_ = bf16[544,384]{1,0:T(8,128)(2,1)S(1)} collective-permute-done((bf16[544,384]{1,0:T(8,128)(2,1)S(1)}, bf16[544,384]{1,0:T(8,128)(2,1)S(1)}, u32[]{:S(2)}, u32[]{:S(2)}) %collective-permute-start.1) | collective-permute-done | bytes 417824 | tf_op jit(solution)/shard_map/ppermute | solution.py:65
  19.4 0.0 collective-permute-start.7
  19.4 1.5 %collective-permute-start.8 = (bf16[544,384]{1,0:T(8,128)(2,1)S(1)}, bf16[544,384]{1,0:T(8,128)(2,1)S(1)}, u32[]{:S(2)}, u32[]{:S(2)}) collective-permute-start(bf16[544,384]{1,0:T(8,128)(2,1)S(1)} %collective-permute-done.1.refs_4_), channel_id=1, source_target_pairs={{0,16},{16,0},{1,17},{17,1},{2,18},{18,2},{3,19},{19,3},{4,20},{20... | collective-permute-start | bytes 1253384 | tf_op jit(solution)/shard_map/ppermute | solution.py:73
  20.9 0.0 collective-permute-done.3.refs_2_
  20.9 0.0 collective-permute-done.2.refs_2_
  20.9 0.0 collective-permute-start.4
  20.9 1.6 %collective-permute-start.5 = (bf16[128,384]{1,0:T(8,128)(2,1)S(1)}, bf16[128,384]{1,0:T(8,128)(2,1)S(1)}, u32[]{:S(2)}, u32[]{:S(2)}) collective-permute-start(bf16[128,384]{1,0:T(8,128)(2,1)S(1)} %get-tuple-element.54), channel_id=1, source_target_pairs={{0,3},{1,2},{2,1},{3,0},{4,7},{5,6},{6,5},{7,4},{8,11},{9,10},{10,... | collective-permute-start | bytes 294920 | tf_op jit(solution)/shard_map/ppermute | solution.py:65
  22.6 0.5 collective-permute-start.9
  23.1 0.0 collective-permute-done.4.refs_1_
  23.1 2.6 %collective-permute-done.5.refs_3_ = bf16[128,384]{1,0:T(8,128)(2,1)S(1)} collective-permute-done((bf16[128,384]{1,0:T(8,128)(2,1)S(1)}, bf16[128,384]{1,0:T(8,128)(2,1)S(1)}, u32[]{:S(2)}, u32[]{:S(2)}) %collective-permute-start.5) | collective-permute-done | bytes 98336 | tf_op jit(solution)/shard_map/ppermute | solution.py:65
  25.7 0.0 copy-start
  25.7 0.0 copy-start.1
  25.7 1.6 %collective-permute-start.6 = (bf16[512,256]{1,0:T(8,128)(2,1)S(1)}, bf16[512,256]{1,0:T(8,128)(2,1)S(1)}, u32[]{:S(2)}, u32[]{:S(2)}) collective-permute-start(bf16[512,256]{1,0:T(8,128)(2,1)S(1)} %bitcast.17), channel_id=1, source_target_pairs={{0,4},{1,5},{2,6},{3,7},{4,8},{5,9},{6,10},{7,11},{8,12},{9,13},{1... | collective-permute-start | bytes 786440 | tf_op jit(solution)/shard_map/ppermute | solution.py:65
  27.4 5.7 %collective-permute-done.7.refs_8_ = bf16[544,384]{1,0:T(8,128)(2,1)S(1)} collective-permute-done((bf16[544,384]{1,0:T(8,128)(2,1)S(1)}, bf16[544,384]{1,0:T(8,128)(2,1)S(1)}, u32[]{:S(2)}, u32[]{:S(2)}) %collective-permute-start.7) | collective-permute-done | bytes 417824 | tf_op jit(solution)/shard_map/ppermute | solution.py:65
  33.1 1.2 %collective-permute-start.11 = (bf16[544,384]{1,0:T(8,128)(2,1)S(1)}, bf16[544,384]{1,0:T(8,128)(2,1)S(1)}, u32[]{:S(2)}, u32[]{:S(2)}) collective-permute-start(bf16[544,384]{1,0:T(8,128)(2,1)S(1)} %collective-permute-done.7.refs_8_), channel_id=1, source_target_pairs={{0,16},{16,0},{1,17},{17,1},{2,18},{18,2},{3,19},{19,3},{4,20},{20... | collective-permute-start | bytes 1253384 | tf_op jit(solution)/shard_map/ppermute | solution.py:73
  34.3 1.5 %collective-permute-start.12 = (bf16[544,384]{1,0:T(8,128)(2,1)S(1)}, bf16[544,384]{1,0:T(8,128)(2,1)S(1)}, u32[]{:S(2)}, u32[]{:S(2)}) collective-permute-start(bf16[544,384]{1,0:T(8,128)(2,1)S(1)} %collective-permute-done.7.refs_8_), channel_id=1, source_target_pairs={{0,2},{1,3},{2,0},{3,1},{4,6},{5,7},{6,4},{7,5},{8,10},{9,11},{10,... | collective-permute-start | bytes 1253384 | tf_op jit(solution)/shard_map/ppermute | solution.py:65
  35.9 0.0 collective-permute-start.14
  35.9 2.6 %collective-permute-done.6.refs_5_ = bf16[512,256]{1,0:T(8,128)(2,1)S(1)} collective-permute-done((bf16[512,256]{1,0:T(8,128)(2,1)S(1)}, bf16[512,256]{1,0:T(8,128)(2,1)S(1)}, u32[]{:S(2)}, u32[]{:S(2)}) %collective-permute-start.6) | collective-permute-done | bytes 262176 | tf_op jit(solution)/shard_map/ppermute | solution.py:65
  38.5 0.0 collective-permute-start.10
  38.5 4.2 %collective-permute-done.11.refs_10_ = bf16[544,384]{1,0:T(8,128)(2,1)S(1)} collective-permute-done((bf16[544,384]{1,0:T(8,128)(2,1)S(1)}, bf16[544,384]{1,0:T(8,128)(2,1)S(1)}, u32[]{:S(2)}, u32[]{:S(2)}) %collective-permute-start.11) | collective-permute-done | bytes 417824 | tf_op jit(solution)/shard_map/ppermute | solution.py:73
  42.6 1.0 %collective-permute-start.15 = (bf16[544,384]{1,0:T(8,128)(2,1)S(1)}, bf16[544,384]{1,0:T(8,128)(2,1)S(1)}, u32[]{:S(2)}, u32[]{:S(2)}) collective-permute-start(bf16[544,384]{1,0:T(8,128)(2,1)S(1)} %collective-permute-done.11.refs_10_), channel_id=1, source_target_pairs={{0,2},{1,3},{2,0},{3,1},{4,6},{5,7},{6,4},{7,5},{8,10},{9,11},{10,... | collective-permute-start | bytes 1253384 | tf_op jit(solution)/shard_map/ppermute | solution.py:65
  43.6 1.8 %collective-permute-start.16 = (bf16[544,384]{1,0:T(8,128)(2,1)S(1)}, bf16[544,384]{1,0:T(8,128)(2,1)S(1)}, u32[]{:S(2)}, u32[]{:S(2)}) collective-permute-start(bf16[544,384]{1,0:T(8,128)(2,1)S(1)} %collective-permute-done.2.refs_2_), channel_id=1, source_target_pairs={{0,16},{16,0},{1,17},{17,1},{2,18},{18,2},{3,19},{19,3},{4,20},{20... | collective-permute-start | bytes 1253384 | tf_op jit(solution)/shard_map/ppermute | solution.py:73
  45.4 7.1 %collective-permute-done.10.refs_6_ = bf16[512,256]{1,0:T(8,128)(2,1)S(1)} collective-permute-done((bf16[512,256]{1,0:T(8,128)(2,1)S(1)}, bf16[512,256]{1,0:T(8,128)(2,1)S(1)}, u32[]{:S(2)}, u32[]{:S(2)}) %collective-permute-start.10) | collective-permute-done | bytes 262176 | tf_op jit(solution)/shard_map/ppermute | solution.py:65
  52.5 0.0 collective-permute-done.12.refs_9_
  52.5 0.0 collective-permute-start.13
  52.5 0.0 collective-permute-done.14.refs_0_
  52.5 1.3 %collective-permute-start.20 = (bf16[544,384]{1,0:T(8,128)(2,1)S(1)}, bf16[544,384]{1,0:T(8,128)(2,1)S(1)}, u32[]{:S(2)}, u32[]{:S(2)}) collective-permute-start(bf16[544,384]{1,0:T(8,128)(2,1)S(1)} %collective-permute-done.14.refs_0_), channel_id=1, source_target_pairs={{0,2},{1,3},{2,0},{3,1},{4,6},{5,7},{6,4},{7,5},{8,10},{9,11},{10,... | collective-permute-start | bytes 1253384 | tf_op jit(solution)/shard_map/ppermute | solution.py:65
  53.9 1.5 %collective-permute-start.21 = (bf16[544,384]{1,0:T(8,128)(2,1)S(1)}, bf16[544,384]{1,0:T(8,128)(2,1)S(1)}, u32[]{:S(2)}, u32[]{:S(2)}) collective-permute-start(bf16[544,384]{1,0:T(8,128)(2,1)S(1)} %collective-permute-done.9.refs_5_), channel_id=1, source_target_pairs={{0,16},{16,0},{1,17},{17,1},{2,18},{18,2},{3,19},{19,3},{4,20},{20... | collective-permute-start | bytes 1253384 | tf_op jit(solution)/shard_map/ppermute | solution.py:73
  55.4 0.4 fusion.5
  55.8 4.9 %collective-permute-done.13.refs_7_ = bf16[512,256]{1,0:T(8,128)(2,1)S(1)} collective-permute-done((bf16[512,256]{1,0:T(8,128)(2,1)S(1)}, bf16[512,256]{1,0:T(8,128)(2,1)S(1)}, u32[]{:S(2)}, u32[]{:S(2)}) %collective-permute-start.13) | collective-permute-done | bytes 262176 | tf_op jit(solution)/shard_map/ppermute | solution.py:65
  60.7 0.0 collective-permute-start.25
  60.7 1.3 %attend.1 = (bf16[128,256]{1,0:T(8,128)(2,1)S(1)}, bf16[128,256]{1,0:T(8,128)(2,1)S(1)}, bf16[128,256]{1,0:T(8,128)(2,1)S(1)}, bf16[128,256]{1,0:T(8,128)(2,1)S(1)}) custom-call(bf16[128,384]{1,0:T(8,128)(2,1)S(1)} %get-tuple-element.49.refs_0_, bf16[128,384]{1,0:T(8,128)(2,1)S(1)} %collective-permute-done.4.refs_1_, ...), custom_call_target="tpu_custom_call" | custom-call | tf_op jit(solution)/shard_map/attend/pallas_call | solution.py:159
  62.0 0.0 collective-permute-done.15.refs_11_
  62.0 0.0 collective-permute-done.16.refs_3_
  62.0 0.6 collective-permute-start.17
  62.6 1.3 %collective-permute-start.18 = (bf16[128,256]{1,0:T(8,128)(2,1)S(1)}, bf16[128,256]{1,0:T(8,128)(2,1)S(1)}, u32[]{:S(2)}, u32[]{:S(2)}) collective-permute-start(bf16[128,256]{1,0:T(8,128)(2,1)S(1)} %get-tuple-element.68), channel_id=1, source_target_pairs={{0,2},{1,3},{2,0},{3,1},{4,6},{5,7},{6,4},{7,5},{8,10},{9,11},{10,... | collective-permute-start | bytes 196616 | tf_op jit(solution)/shard_map/ppermute | solution.py:65
  63.8 0.2 collective-permute-start.19
  64.0 0.6 collective-permute-start.27
  64.6 2.3 %collective-permute-done.18.refs_2_ = bf16[128,256]{1,0:T(8,128)(2,1)S(1)} collective-permute-done((bf16[128,256]{1,0:T(8,128)(2,1)S(1)}, bf16[128,256]{1,0:T(8,128)(2,1)S(1)}, u32[]{:S(2)}, u32[]{:S(2)}) %collective-permute-start.18) | collective-permute-done | bytes 65568 | tf_op jit(solution)/shard_map/ppermute | solution.py:65
  66.9 1.2 %collective-permute-start.26 = (bf16[544,384]{1,0:T(8,128)(2,1)S(1)}, bf16[544,384]{1,0:T(8,128)(2,1)S(1)}, u32[]{:S(2)}, u32[]{:S(2)}) collective-permute-start(bf16[544,384]{1,0:T(8,128)(2,1)S(1)} %collective-permute-done.14.refs_0_), channel_id=1, source_target_pairs={{0,16},{16,0},{1,17},{17,1},{2,18},{18,2},{3,19},{19,3},{4,20},{20... | collective-permute-start | bytes 1253384 | tf_op jit(solution)/shard_map/ppermute | solution.py:73
  68.1 0.1 collective-permute-done.19.refs_3_
  68.2 1.3 %output.1.act.act_own = bf16[128,1536]{1,0:T(8,128)(2,1)S(1)} custom-call(s32[4]{0:T(128)S(1)} %pad_add_fusion.idx, bf16[128,1536]{1,0:T(8,128)(2,1)S(1)} %bitcast.16, bf16[768,1536]{1,0:T(8,128)(2,1)S(1)} %copy-done, bf16[128,256]{1,0:T(8,128)(2,1)S(1)} %get-tuple-element.61.refs_0_, bf16[128,256]{1,0:T(8,128)(2,1)S(1)} %collective-permute-done.17.refs_1_, ...), custom_call_target="tpu_custom_call" | custom-call | tf_op jit(solution)/shard_map/output/pallas_call | solution.py:183
  69.5 0.2 collective-permute-start.22
  69.7 0.6 give.1
  70.3 0.0 copy-start.2
  70.3 0.7 collective-permute-start.23
  71.0 1.3 %collective-permute-start.24 = (bf16[16,2816]{1,0:T(8,128)(2,1)S(1)}, bf16[16,2816]{1,0:T(8,128)(2,1)S(1)}, u32[]{:S(2)}, u32[]{:S(2)}) collective-permute-start(bf16[16,2816]{1,0:T(8,128)(2,1)S(1)} %give.1), channel_id=1, source_target_pairs={{1,3},{2,0},{3,5},{4,2},{5,7},{6,4},{7,9},{8,6},{9,11},{10,8},{11,... | collective-permute-start | bytes 270344 | tf_op jit(solution)/shard_map/ppermute | solution.py:65
  72.3 2.5 %early.1 = (bf16[1536,768]{1,0:T(8,128)(2,1)S(1)}, bf16[1280,768]{1,0:T(8,128)(2,1)S(1)}, bf16[1536,768]{1,0:T(8,128)(2,1)S(1)}, f32[512,768]{1,0:T(8,128)S(1)}, bf16[512,320]{1,0:T(8,128)(2,1)S(1)}) custom-call(s32[4]{0:T(128)S(1)} %pad_add_fusion.idx, bf16[256,1280]{1,0:T(8,128)(2,1)S(1)} %bitcast.14, ...), custom_call_target="tpu_custom_call" | custom-call | tf_op jit(solution)/shard_map/early/pallas_call | solution.py:265
  74.8 3.8 %collective-permute-done.24.far_oth = bf16[16,2816]{1,0:T(8,128)(2,1)S(1)} collective-permute-done((bf16[16,2816]{1,0:T(8,128)(2,1)S(1)}, bf16[16,2816]{1,0:T(8,128)(2,1)S(1)}, u32[]{:S(2)}, u32[]{:S(2)}) %collective-permute-start.24) | collective-permute-done | bytes 90144 | tf_op jit(solution)/shard_map/ppermute | solution.py:65
  78.7 3.7 %decode.1 = (bf16[2,128,1536]{2,1,0:T(8,128)(2,1)S(1)}, bf16[256,768]{1,0:T(8,128)(2,1)S(1)}, bf16[1536,768]{1,0:T(8,128)(2,1)S(1)}, bf16[1280,768]{1,0:T(8,128)(2,1)S(1)}, bf16[1536,768]{1,0:T(8,128)(2,1)S(1)}) custom-call(s32[4]{0:T(128)S(1)} %pad_add_fusion.idx, ...), custom_call_target="tpu_custom_call", output_to_operand_aliasing={{2}: (6, {}), {3}: (7, {}), {4}: (8, {})} | custom-call | tf_op jit(solution)/shard_map/decode/pallas_call | solution.py:327
  82.4 1.1 %collective-permute-start.28 = (bf16[2,128,1536]{2,1,0:T(8,128)(2,1)S(1)}, bf16[2,128,1536]{2,1,0:T(8,128)(2,1)S(1)}, u32[]{:S(2)}, u32[]{:S(2)}) collective-permute-start(bf16[2,128,1536]{2,1,0:T(8,128)(2,1)S(1)} %get-tuple-element.86), channel_id=1, source_target_pairs={{0,1},{1,0},{2,3},{3,2},{4,5},{5,4},{6,7},{7,6},{8,9},{9,8},{10,11... | collective-permute-start | bytes 2359304 | tf_op jit(solution)/shard_map/ppermute | solution.py:65
  83.5 0.8 point_rest.1
  84.3 1.1 %collective-permute-done.28 = bf16[2,128,1536]{2,1,0:T(8,128)(2,1)S(1)} collective-permute-done((bf16[2,128,1536]{2,1,0:T(8,128)(2,1)S(1)}, bf16[2,128,1536]{2,1,0:T(8,128)(2,1)S(1)}, u32[]{:S(2)}, u32[]{:S(2)}) %collective-permute-start.28) | collective-permute-done | bytes 786464 | tf_op jit(solution)/shard_map/ppermute | solution.py:65
  85.4 1.1 %add_convert_fusion = bf16[2,128,1536]{2,1,0:T(8,128)(2,1)} fusion(f32[2,128,1536]{2,1,0:T(8,128)S(1)} %point_rest.1, bf16[2,128,1536]{2,1,0:T(8,128)(2,1)S(1)} %collective-permute-done.28), kind=kLoop, calls=%fused_computation.4 | loop fusion | flops 1179648 | bytes 3145728 | tf_op jit(solution)/shard_map/convert_element_type | solution.py:525
  (22 shorter events, 0.1 us)
Async XLA Ops:
  0.0 8.9 %copy-start.4 = (f32[1536]{0:T(1024)S(1)}, f32[1536]{0:T(1024)}, u32[]{:S(2)}) copy-start(f32[1536]{0:T(1024)} %param.13) | copy-start | bytes 18436
  1.9 1.9 %collective-permute-start = (bf16[272,768]{1,0:T(8,128)(2,1)S(1)}, bf16[272,768]{1,0:T(8,128)(2,1)S(1)}, u32[]{:S(2)}, u32[]{:S(2)}) collective-permute-start(bf16[272,768]{1,0:T(8,128)(2,1)S(1)} %get-tuple-element.47), channel_id=1, source_target_pairs={{0,1},{1,0},{2,3},{3,2},{4,5},{5,4},{6,7},{7,6},{8,9},{9,8},{10,11... | collective-permute-start | bytes 1253384 | tf_op jit(solution)/shard_map/ppermute | solution.py:65
  4.4 15.0 %collective-permute-start.1 = (bf16[544,384]{1,0:T(8,128)(2,1)S(1)}, bf16[544,384]{1,0:T(8,128)(2,1)S(1)}, u32[]{:S(2)}, u32[]{:S(2)}) collective-permute-start(bf16[544,384]{1,0:T(8,128)(2,1)S(1)} %take.1), channel_id=1, source_target_pairs={{0,4},{1,5},{2,6},{3,7},{4,8},{5,9},{6,10},{7,11},{8,12},{9,13},{1... | collective-permute-start | bytes 1253384 | tf_op jit(solution)/shard_map/ppermute | solution.py:65
  7.4 13.5 %collective-permute-start.2 = (bf16[544,384]{1,0:T(8,128)(2,1)S(1)}, bf16[544,384]{1,0:T(8,128)(2,1)S(1)}, u32[]{:S(2)}, u32[]{:S(2)}) collective-permute-start(bf16[544,384]{1,0:T(8,128)(2,1)S(1)} %take.1), channel_id=1, source_target_pairs={{0,2},{1,3},{2,0},{3,1},{4,6},{5,7},{6,4},{7,5},{8,10},{9,11},{10,... | collective-permute-start | bytes 1253384 | tf_op jit(solution)/shard_map/ppermute | solution.py:65
  12.6 42.7 %copy-start.3 = (bf16[2,128,1280]{2,1,0:T(8,128)(2,1)S(1)}, bf16[2,128,1280]{2,1,0:T(8,128)(2,1)}, u32[]{:S(2)}) copy-start(bf16[2,128,1280]{2,1,0:T(8,128)(2,1)} %param.12) | copy-start | bytes 1966084
  12.7 8.3 %collective-permute-start.3 = (bf16[128,384]{1,0:T(8,128)(2,1)S(1)}, bf16[128,384]{1,0:T(8,128)(2,1)S(1)}, u32[]{:S(2)}, u32[]{:S(2)}) collective-permute-start(bf16[128,384]{1,0:T(8,128)(2,1)S(1)} %get-tuple-element.51), channel_id=1, source_target_pairs={{0,2},{1,3},{2,0},{3,1},{4,6},{5,7},{6,4},{7,5},{8,10},{9,11},{10,... | collective-permute-start | bytes 294920 | tf_op jit(solution)/shard_map/ppermute | solution.py:65
  19.4 13.8 %collective-permute-start.7 = (bf16[544,384]{1,0:T(8,128)(2,1)S(1)}, bf16[544,384]{1,0:T(8,128)(2,1)S(1)}, u32[]{:S(2)}, u32[]{:S(2)}) collective-permute-start(bf16[544,384]{1,0:T(8,128)(2,1)S(1)} %collective-permute-done.1.refs_4_), channel_id=1, source_target_pairs={{0,4},{1,5},{2,6},{3,7},{4,8},{5,9},{6,10},{7,11},{8,12},{9,13},{1... | collective-permute-start | bytes 1253384 | tf_op jit(solution)/shard_map/ppermute | solution.py:65
  19.4 15.0 %collective-permute-start.8 = (bf16[544,384]{1,0:T(8,128)(2,1)S(1)}, bf16[544,384]{1,0:T(8,128)(2,1)S(1)}, u32[]{:S(2)}, u32[]{:S(2)}) collective-permute-start(bf16[544,384]{1,0:T(8,128)(2,1)S(1)} %collective-permute-done.1.refs_4_), channel_id=1, source_target_pairs={{0,16},{16,0},{1,17},{17,1},{2,18},{18,2},{3,19},{19,3},{4,20},{20... | collective-permute-start | bytes 1253384 | tf_op jit(solution)/shard_map/ppermute | solution.py:73
  20.9 2.2 %collective-permute-start.4 = (bf16[128,384]{1,0:T(8,128)(2,1)S(1)}, bf16[128,384]{1,0:T(8,128)(2,1)S(1)}, u32[]{:S(2)}, u32[]{:S(2)}) collective-permute-start(bf16[128,384]{1,0:T(8,128)(2,1)S(1)} %get-tuple-element.52), channel_id=1, source_target_pairs={{0,1},{1,0},{2,3},{3,2},{4,5},{5,4},{6,7},{7,6},{8,9},{9,8},{10,11... | collective-permute-start | bytes 294920 | tf_op jit(solution)/shard_map/ppermute | solution.py:65
  20.9 4.8 %collective-permute-start.5 = (bf16[128,384]{1,0:T(8,128)(2,1)S(1)}, bf16[128,384]{1,0:T(8,128)(2,1)S(1)}, u32[]{:S(2)}, u32[]{:S(2)}) collective-permute-start(bf16[128,384]{1,0:T(8,128)(2,1)S(1)} %get-tuple-element.54), channel_id=1, source_target_pairs={{0,3},{1,2},{2,1},{3,0},{4,7},{5,6},{6,5},{7,4},{8,11},{9,10},{10,... | collective-permute-start | bytes 294920 | tf_op jit(solution)/shard_map/ppermute | solution.py:65
  22.6 15.9 %collective-permute-start.9 = (bf16[544,384]{1,0:T(8,128)(2,1)S(1)}, bf16[544,384]{1,0:T(8,128)(2,1)S(1)}, u32[]{:S(2)}, u32[]{:S(2)}) collective-permute-start(bf16[544,384]{1,0:T(8,128)(2,1)S(1)} %collective-permute-done.1.refs_4_), channel_id=1, source_target_pairs={{0,2},{1,3},{2,0},{3,1},{4,6},{5,7},{6,4},{7,5},{8,10},{9,11},{10,... | collective-permute-start | bytes 1253384 | tf_op jit(solution)/shard_map/ppermute | solution.py:65
  25.7 42.5 %copy-start = (bf16[768,1536]{1,0:T(8,128)(2,1)S(1)}, bf16[768,1536]{1,0:T(8,128)(2,1)}, u32[]{:S(2)}) copy-start(bf16[768,1536]{1,0:T(8,128)(2,1)} %wo.1) | copy-start | bytes 7077892
  25.7 42.5 %copy-start.1 = (bf16[2,64,1536]{2,1,0:T(8,128)(2,1)S(1)}, bf16[2,64,1536]{2,1,0:T(8,128)(2,1)}, u32[]{:S(2)}) copy-start(bf16[2,64,1536]{2,1,0:T(8,128)(2,1)} %param.11) | copy-start | bytes 1179652
  25.7 12.7 %collective-permute-start.6 = (bf16[512,256]{1,0:T(8,128)(2,1)S(1)}, bf16[512,256]{1,0:T(8,128)(2,1)S(1)}, u32[]{:S(2)}, u32[]{:S(2)}) collective-permute-start(bf16[512,256]{1,0:T(8,128)(2,1)S(1)} %bitcast.17), channel_id=1, source_target_pairs={{0,4},{1,5},{2,6},{3,7},{4,8},{5,9},{6,10},{7,11},{8,12},{9,13},{1... | collective-permute-start | bytes 786440 | tf_op jit(solution)/shard_map/ppermute | solution.py:65
  33.1 9.5 %collective-permute-start.11 = (bf16[544,384]{1,0:T(8,128)(2,1)S(1)}, bf16[544,384]{1,0:T(8,128)(2,1)S(1)}, u32[]{:S(2)}, u32[]{:S(2)}) collective-permute-start(bf16[544,384]{1,0:T(8,128)(2,1)S(1)} %collective-permute-done.7.refs_8_), channel_id=1, source_target_pairs={{0,16},{16,0},{1,17},{17,1},{2,18},{18,2},{3,19},{19,3},{4,20},{20... | collective-permute-start | bytes 1253384 | tf_op jit(solution)/shard_map/ppermute | solution.py:73
  34.3 18.2 %collective-permute-start.12 = (bf16[544,384]{1,0:T(8,128)(2,1)S(1)}, bf16[544,384]{1,0:T(8,128)(2,1)S(1)}, u32[]{:S(2)}, u32[]{:S(2)}) collective-permute-start(bf16[544,384]{1,0:T(8,128)(2,1)S(1)} %collective-permute-done.7.refs_8_), channel_id=1, source_target_pairs={{0,2},{1,3},{2,0},{3,1},{4,6},{5,7},{6,4},{7,5},{8,10},{9,11},{10,... | collective-permute-start | bytes 1253384 | tf_op jit(solution)/shard_map/ppermute | solution.py:65
  35.9 16.7 %collective-permute-start.14 = (bf16[544,384]{1,0:T(8,128)(2,1)S(1)}, bf16[544,384]{1,0:T(8,128)(2,1)S(1)}, u32[]{:S(2)}, u32[]{:S(2)}) collective-permute-start(bf16[544,384]{1,0:T(8,128)(2,1)S(1)} %collective-permute-done.7.refs_8_), channel_id=1, source_target_pairs={{0,4},{1,5},{2,6},{3,7},{4,8},{5,9},{6,10},{7,11},{8,12},{9,13},{1... | collective-permute-start | bytes 1253384 | tf_op jit(solution)/shard_map/ppermute | solution.py:65
  38.5 14.1 %collective-permute-start.10 = (bf16[512,256]{1,0:T(8,128)(2,1)S(1)}, bf16[512,256]{1,0:T(8,128)(2,1)S(1)}, u32[]{:S(2)}, u32[]{:S(2)}) collective-permute-start(bf16[512,256]{1,0:T(8,128)(2,1)S(1)} %collective-permute-done.6.refs_5_), channel_id=1, source_target_pairs={{0,4},{1,5},{2,6},{3,7},{4,8},{5,9},{6,10},{7,11},{8,12},{9,13},{1... | collective-permute-start | bytes 786440 | tf_op jit(solution)/shard_map/ppermute | solution.py:65
  42.6 19.4 %collective-permute-start.15 = (bf16[544,384]{1,0:T(8,128)(2,1)S(1)}, bf16[544,384]{1,0:T(8,128)(2,1)S(1)}, u32[]{:S(2)}, u32[]{:S(2)}) collective-permute-start(bf16[544,384]{1,0:T(8,128)(2,1)S(1)} %collective-permute-done.11.refs_10_), channel_id=1, source_target_pairs={{0,2},{1,3},{2,0},{3,1},{4,6},{5,7},{6,4},{7,5},{8,10},{9,11},{10,... | collective-permute-start | bytes 1253384 | tf_op jit(solution)/shard_map/ppermute | solution.py:65
  43.6 18.4 %collective-permute-start.16 = (bf16[544,384]{1,0:T(8,128)(2,1)S(1)}, bf16[544,384]{1,0:T(8,128)(2,1)S(1)}, u32[]{:S(2)}, u32[]{:S(2)}) collective-permute-start(bf16[544,384]{1,0:T(8,128)(2,1)S(1)} %collective-permute-done.2.refs_2_), channel_id=1, source_target_pairs={{0,16},{16,0},{1,17},{17,1},{2,18},{18,2},{3,19},{19,3},{4,20},{20... | collective-permute-start | bytes 1253384 | tf_op jit(solution)/shard_map/ppermute | solution.py:73
  52.5 8.2 %collective-permute-start.13 = (bf16[512,256]{1,0:T(8,128)(2,1)S(1)}, bf16[512,256]{1,0:T(8,128)(2,1)S(1)}, u32[]{:S(2)}, u32[]{:S(2)}) collective-permute-start(bf16[512,256]{1,0:T(8,128)(2,1)S(1)} %collective-permute-done.10.refs_6_), channel_id=1, source_target_pairs={{0,4},{1,5},{2,6},{3,7},{4,8},{5,9},{6,10},{7,11},{8,12},{9,13},{1... | collective-permute-start | bytes 786440 | tf_op jit(solution)/shard_map/ppermute | solution.py:65
  52.5 11.3 %collective-permute-start.20 = (bf16[544,384]{1,0:T(8,128)(2,1)S(1)}, bf16[544,384]{1,0:T(8,128)(2,1)S(1)}, u32[]{:S(2)}, u32[]{:S(2)}) collective-permute-start(bf16[544,384]{1,0:T(8,128)(2,1)S(1)} %collective-permute-done.14.refs_0_), channel_id=1, source_target_pairs={{0,2},{1,3},{2,0},{3,1},{4,6},{5,7},{6,4},{7,5},{8,10},{9,11},{10,... | collective-permute-start | bytes 1253384 | tf_op jit(solution)/shard_map/ppermute | solution.py:65
  53.9 15.7 %collective-permute-start.21 = (bf16[544,384]{1,0:T(8,128)(2,1)S(1)}, bf16[544,384]{1,0:T(8,128)(2,1)S(1)}, u32[]{:S(2)}, u32[]{:S(2)}) collective-permute-start(bf16[544,384]{1,0:T(8,128)(2,1)S(1)} %collective-permute-done.9.refs_5_), channel_id=1, source_target_pairs={{0,16},{16,0},{1,17},{17,1},{2,18},{18,2},{3,19},{19,3},{4,20},{20... | collective-permute-start | bytes 1253384 | tf_op jit(solution)/shard_map/ppermute | solution.py:73
  60.7 10.3 %collective-permute-start.25 = (bf16[256,1280]{1,0:T(8,128)(2,1)S(1)}, bf16[256,1280]{1,0:T(8,128)(2,1)S(1)}, u32[]{:S(2)}, u32[]{:S(2)}) collective-permute-start(bf16[256,1280]{1,0:T(8,128)(2,1)S(1)} %bitcast.12), channel_id=1, source_target_pairs={{0,1},{1,0},{2,3},{3,2},{4,5},{5,4},{6,7},{7,6},{8,9},{9,8},{10,11... | collective-permute-start | bytes 1966088 | tf_op jit(solution)/shard_map/ppermute | solution.py:65
  62.0 2.0 %collective-permute-start.17 = (bf16[128,256]{1,0:T(8,128)(2,1)S(1)}, bf16[128,256]{1,0:T(8,128)(2,1)S(1)}, u32[]{:S(2)}, u32[]{:S(2)}) collective-permute-start(bf16[128,256]{1,0:T(8,128)(2,1)S(1)} %get-tuple-element.66), channel_id=1, source_target_pairs={{0,1},{1,0},{2,3},{3,2},{4,5},{5,4},{6,7},{7,6},{8,9},{9,8},{10,11... | collective-permute-start | bytes 196616 | tf_op jit(solution)/shard_map/ppermute | solution.py:65
  62.6 4.3 %collective-permute-start.18 = (bf16[128,256]{1,0:T(8,128)(2,1)S(1)}, bf16[128,256]{1,0:T(8,128)(2,1)S(1)}, u32[]{:S(2)}, u32[]{:S(2)}) collective-permute-start(bf16[128,256]{1,0:T(8,128)(2,1)S(1)} %get-tuple-element.68), channel_id=1, source_target_pairs={{0,2},{1,3},{2,0},{3,1},{4,6},{5,7},{6,4},{7,5},{8,10},{9,11},{10,... | collective-permute-start | bytes 196616 | tf_op jit(solution)/shard_map/ppermute | solution.py:65
  63.8 4.3 %collective-permute-start.19 = (bf16[128,256]{1,0:T(8,128)(2,1)S(1)}, bf16[128,256]{1,0:T(8,128)(2,1)S(1)}, u32[]{:S(2)}, u32[]{:S(2)}) collective-permute-start(bf16[128,256]{1,0:T(8,128)(2,1)S(1)} %get-tuple-element.70), channel_id=1, source_target_pairs={{0,3},{1,2},{2,1},{3,0},{4,7},{5,6},{6,5},{7,4},{8,11},{9,10},{10,... | collective-permute-start | bytes 196616 | tf_op jit(solution)/shard_map/ppermute | solution.py:65
  64.0 14.7 %collective-permute-start.27 = (bf16[544,384]{1,0:T(8,128)(2,1)S(1)}, bf16[544,384]{1,0:T(8,128)(2,1)S(1)}, u32[]{:S(2)}, u32[]{:S(2)}) collective-permute-start(bf16[544,384]{1,0:T(8,128)(2,1)S(1)} %collective-permute-done.15.refs_11_), channel_id=1, source_target_pairs={{0,4},{1,5},{2,6},{3,7},{4,8},{5,9},{6,10},{7,11},{8,12},{9,13},{1... | collective-permute-start | bytes 1253384 | tf_op jit(solution)/shard_map/ppermute | solution.py:65
  66.9 11.8 %collective-permute-start.26 = (bf16[544,384]{1,0:T(8,128)(2,1)S(1)}, bf16[544,384]{1,0:T(8,128)(2,1)S(1)}, u32[]{:S(2)}, u32[]{:S(2)}) collective-permute-start(bf16[544,384]{1,0:T(8,128)(2,1)S(1)} %collective-permute-done.14.refs_0_), channel_id=1, source_target_pairs={{0,16},{16,0},{1,17},{17,1},{2,18},{18,2},{3,19},{19,3},{4,20},{20... | collective-permute-start | bytes 1253384 | tf_op jit(solution)/shard_map/ppermute | solution.py:73
  69.5 9.1 %collective-permute-start.22 = (bf16[128,1536]{1,0:T(8,128)(2,1)S(1)}, bf16[128,1536]{1,0:T(8,128)(2,1)S(1)}, u32[]{:S(2)}, u32[]{:S(2)}) collective-permute-start(bf16[128,1536]{1,0:T(8,128)(2,1)S(1)} %output.1.act.act_own), channel_id=1, source_target_pairs={{0,1},{1,0},{2,3},{3,2},{4,5},{5,4},{6,7},{7,6},{8,9},{9,8},{10,11... | collective-permute-start | bytes 1179656 | tf_op jit(solution)/shard_map/ppermute | solution.py:65
  70.3 8.4 %copy-start.2 = (f32[3,1536]{1,0:T(4,128)S(1)}, f32[3,1536]{1,0:T(4,128)}, u32[]{:S(2)}) copy-start(f32[3,1536]{1,0:T(4,128)} %depth.1) | copy-start | bytes 55300
  70.3 4.5 %collective-permute-start.23 = (bf16[16,2816]{1,0:T(8,128)(2,1)S(1)}, bf16[16,2816]{1,0:T(8,128)(2,1)S(1)}, u32[]{:S(2)}, u32[]{:S(2)}) collective-permute-start(bf16[16,2816]{1,0:T(8,128)(2,1)S(1)} %give.1), channel_id=1, source_target_pairs={{1,2},{2,1},{3,4},{4,3},{5,6},{6,5},{7,8},{8,7},{9,10},{10,9},{11,... | collective-permute-start | bytes 270344 | tf_op jit(solution)/shard_map/ppermute | solution.py:65
  71.0 7.7 %collective-permute-start.24 = (bf16[16,2816]{1,0:T(8,128)(2,1)S(1)}, bf16[16,2816]{1,0:T(8,128)(2,1)S(1)}, u32[]{:S(2)}, u32[]{:S(2)}) collective-permute-start(bf16[16,2816]{1,0:T(8,128)(2,1)S(1)} %give.1), channel_id=1, source_target_pairs={{1,3},{2,0},{3,5},{4,2},{5,7},{6,4},{7,9},{8,6},{9,11},{10,8},{11,... | collective-permute-start | bytes 270344 | tf_op jit(solution)/shard_map/ppermute | solution.py:65
  82.4 3.0 %collective-permute-start.28 = (bf16[2,128,1536]{2,1,0:T(8,128)(2,1)S(1)}, bf16[2,128,1536]{2,1,0:T(8,128)(2,1)S(1)}, u32[]{:S(2)}, u32[]{:S(2)}) collective-permute-start(bf16[2,128,1536]{2,1,0:T(8,128)(2,1)S(1)} %get-tuple-element.86), channel_id=1, source_target_pairs={{0,1},{1,0},{2,3},{3,2},{4,5},{5,4},{6,7},{7,6},{8,9},{9,8},{10,11... | collective-permute-start | bytes 2359304 | tf_op jit(solution)/shard_map/ppermute | solution.py:65

commit v5 on v4

--- a/solution.py
+++ b/solution.py
@@ -20,14 +20,14 @@
 
 WIDTH = 5
 CUMULATIVE = True
-FREE = ()
+FREE = ("far", "farc",)
 SENDS = (
     ("u1", "z", "u0"),
+    ("qy", "y", "py"),
+    ("qcy", "cy", "pcy"),
     ("b0", "y", "u0"),
-    ("qy", "y", "py"),
     ("u2", "z", "u1"),
     ("c1", "x", "u1"),
-    ("qcy", "cy", "pcy"),
     ("b1", "y", "u1"),
     ("k1", "z", "k0"),
     ("c2", "x", "u2"),
@@ -41,13 +41,13 @@
     ("k3", "z", "k2"),
     ("b3", "y", "u3"),
     ("d1", "x", "b1"),
+    ("d3", "z", "d2"),
     ("my", "y", "oy"),
     ("mc", "c", "oc"),
+    ("c3", "x", "u3"),
     ("mcy", "cy", "ocy"),
-    ("c3", "x", "u3"),
-    ("d3", "z", "d2"),
+    ("actc", "c", "act"),
     ("far", "beyond", "edge"),
-    ("actc", "c", "act"),
     ("farc", "beyond c", "edge"),
 )
 
@@ -387,19 +387,18 @@
     return pltpu.with_memory_space_constraint(v, pltpu.HBM)
 
 
-def split_kernel(idx, wl, ws, wp, keep, send, sems):
+def split_kernel(idx, wl, ws, wp, keep, send, whole, sems):
     c = idx[3]
-    copies = []
-    for out, cc in ((send, 1 - c), (keep, c)):
-        cols = pl.ds(pl.multiple_of(768 * cc, 768), 768)
-        for src, lo, hi in ((wl, 0, 96), (ws, 96, 176), (wp, 176, 272)):
-            copies.append(
-                pltpu.make_async_copy(src.at[:, cols], out.at[lo:hi], sems.at[len(copies)])
-            )
+    copies = [
+        pltpu.make_async_copy(src, whole.at[lo:hi], sems.at[n])
+        for n, (src, lo, hi) in enumerate(((wl, 0, 96), (ws, 96, 176), (wp, 176, 272)))
+    ]
     for copy in copies:
         copy.start()
-    for copy in copies:
+    for copy, (lo, hi) in zip(copies, ((0, 96), (96, 176), (176, 272))):
         copy.wait()
+        for out, cc in ((send, 1 - c), (keep, c)):
+            out[lo:hi, :] = whole[lo:hi, pl.ds(pl.multiple_of(768 * cc, 768), 768)]
 
 
 def split(idx, wl, ws, wp):
@@ -409,7 +408,8 @@
         in_specs=[SMEM] + [HBM] * 3,
         out_specs=[VMEM] * 2,
         scratch_shapes=[
-            pltpu.SemaphoreType.DMA((6,)),
+            pltpu.VMEM((272, 1536), BF16),
+            pltpu.SemaphoreType.DMA((3,)),
         ],
         compiler_params=LIMIT,
         name="split",

time: 86.9 us -> 86.8 us (level)
  starting transfers between devices: 26.3 us -> 25.3 us
    ppermute x24, starting transfers between devices: 19.1 us -> 16.9 us  [over_pos(): return lambda v: lax.ppermute(v, 'pos', pairs)]
    ppermute x5, starting transfers between devices: 7.2 us -> 8.37 us  [x_swap(): return lax.ppermute(v, 'group', X_SWAP)]
  transfers between devices with their start and end apart: 29 -> 29, of which waited for: 12 -> 13; matrix products, arithmetic and copies ran while one was open for 1% -> 1% of each run, Pallas kernels for 12% -> 12%
where the time goes in v5:
time: 86.8 us; the launch traced here: 86.3 us
  waiting for transfers between devices  42.8 us (49%)
  starting transfers between devices  25.3 us (29%)
  Pallas kernels  16.3 us (19%)
  other arithmetic  1.64 us (2%)
    ppermute x24, waiting for transfers between devices, over_pos(): return lambda v: lax.ppermute(v, 'pos', pairs)  37.9 us
    ppermute x24, starting transfers between devices, over_pos(): return lambda v: lax.ppermute(v, 'pos', pairs)  16.9 us
    ppermute x5, starting transfers between devices, x_swap(): return lax.ppermute(v, 'group', X_SWAP)  8.37 us
    ppermute x5, waiting for transfers between devices, x_swap(): return lax.ppermute(v, 'group', X_SWAP)  4.91 us
    pallas_call x1, Pallas kernels, project(): pl.pallas_call(project_kernel, out_shape=[jax.ShapeDtypeStruct((rows, 384...  3.7 us
    pallas_call x1, Pallas kernels, decode(): pl.pallas_call(decode_kernel, out_shape=[jax.ShapeDtypeStruct((2, 128, 15...  3.69 us
    pallas_call x1, Pallas kernels, early(): pl.pallas_call(early_kernel, out_shape=WEIGHTS + [jax.ShapeDtypeStruct((5...  2.52 us
    pallas_call x1, Pallas kernels, split(): pl.pallas_call(split_kernel, out_shape=[jax.ShapeDtypeStruct((272, 768),...  1.75 us
  transfers between devices with their start and end apart: 29, of which 13 were waited for; matrix products, arithmetic and copies ran while one was open for 1% of the time, Pallas kernels for 12%

profile of v5, /device:TPU:0, one launch (start us, length us, event | category | flops | bytes accessed | tf_op | source)
XLA Modules:
  0.0 86.3 jit_solution(7448948523250390044)
XLA Ops:
  0.0 0.1 pad_add_fusion.idx
  0.1 1.8 %split.1 = (bf16[272,768]{1,0:T(8,128)(2,1)S(1)}, bf16[272,768]{1,0:T(8,128)(2,1)S(1)}) custom-call(s32[4]{0:T(128)S(1)} %pad_add_fusion.idx, bf16[96,1536]{1,0:T(8,128)(2,1)} %wl.1, bf16[80,1536]{1,0:T(8,128)(2,1)} %ws.1, bf16[96,1536]{1,0:T(8,128)(2,1)} %bitcast.19), custom_call_target="tpu_custom_call" | custom-call | tf_op jit(solution)/shard_map/split/pallas_call | solution.py:405
  1.8 0.5 collective-permute-start
  2.4 1.4 %collective-permute-done.got.refs_1_ = bf16[272,768]{1,0:T(8,128)(2,1)S(1)} collective-permute-done((bf16[272,768]{1,0:T(8,128)(2,1)S(1)}, bf16[272,768]{1,0:T(8,128)(2,1)S(1)}, u32[]{:S(2)}, u32[]{:S(2)}) %collective-permute-start) | collective-permute-done | bytes 417824 | tf_op jit(solution)/shard_map/ppermute | solution.py:65
  3.7 0.6 take.1
  4.3 3.0 %collective-permute-start.1 = (bf16[544,384]{1,0:T(8,128)(2,1)S(1)}, bf16[544,384]{1,0:T(8,128)(2,1)S(1)}, u32[]{:S(2)}, u32[]{:S(2)}) collective-permute-start(bf16[544,384]{1,0:T(8,128)(2,1)S(1)} %take.1), channel_id=1, source_target_pairs={{0,4},{1,5},{2,6},{3,7},{4,8},{5,9},{6,10},{7,11},{8,12},{9,13},{1... | collective-permute-start | bytes 1253384 | tf_op jit(solution)/shard_map/ppermute | solution.py:65
  7.3 3.7 %project.1 = (bf16[128,384]{1,0:T(8,128)(2,1)S(1)}, bf16[128,384]{1,0:T(8,128)(2,1)S(1)}, bf16[128,384]{1,0:T(8,128)(2,1)S(1)}, bf16[128,384]{1,0:T(8,128)(2,1)S(1)}) custom-call(s32[4]{0:T(128)S(1)} %pad_add_fusion.idx, bf16[128,1536]{1,0:T(8,128)(2,1)} %bitcast.15, f32[1,1536]{1,0:T(1,128)S(1)} %reshape.25.gain, bf16[1536,256]{1,0:T(8,128)(2,1)} %wq_hbm.1, ...), custom_call_target="tpu_custom_call" | custom-call | tf_op jit(solution)/shard_map/project/pallas_call | solution.py:122
  11.1 0.0 copy-start.3
  11.1 1.6 %collective-permute-start.2 = (bf16[128,384]{1,0:T(8,128)(2,1)S(1)}, bf16[128,384]{1,0:T(8,128)(2,1)S(1)}, u32[]{:S(2)}, u32[]{:S(2)}) collective-permute-start(bf16[128,384]{1,0:T(8,128)(2,1)S(1)} %get-tuple-element.49), channel_id=1, source_target_pairs={{0,2},{1,3},{2,0},{3,1},{4,6},{5,7},{6,4},{7,5},{8,10},{9,11},{10,... | collective-permute-start | bytes 294920 | tf_op jit(solution)/shard_map/ppermute | solution.py:65
  12.7 0.0 collective-permute-start.3
  12.7 1.2 %collective-permute-start.6 = (bf16[544,384]{1,0:T(8,128)(2,1)S(1)}, bf16[544,384]{1,0:T(8,128)(2,1)S(1)}, u32[]{:S(2)}, u32[]{:S(2)}) collective-permute-start(bf16[544,384]{1,0:T(8,128)(2,1)S(1)} %take.1), channel_id=1, source_target_pairs={{0,2},{1,3},{2,0},{3,1},{4,6},{5,7},{6,4},{7,5},{8,10},{9,11},{10,... | collective-permute-start | bytes 1253384 | tf_op jit(solution)/shard_map/ppermute | solution.py:65
  13.9 5.4 %collective-permute-done.1.refs_4_ = bf16[544,384]{1,0:T(8,128)(2,1)S(1)} collective-permute-done((bf16[544,384]{1,0:T(8,128)(2,1)S(1)}, bf16[544,384]{1,0:T(8,128)(2,1)S(1)}, u32[]{:S(2)}, u32[]{:S(2)}) %collective-permute-start.1) | collective-permute-done | bytes 417824 | tf_op jit(solution)/shard_map/ppermute | solution.py:65
  19.3 0.0 collective-permute-start.7
  19.3 1.5 %collective-permute-start.8 = (bf16[544,384]{1,0:T(8,128)(2,1)S(1)}, bf16[544,384]{1,0:T(8,128)(2,1)S(1)}, u32[]{:S(2)}, u32[]{:S(2)}) collective-permute-start(bf16[544,384]{1,0:T(8,128)(2,1)S(1)} %collective-permute-done.1.refs_4_), channel_id=1, source_target_pairs={{0,16},{16,0},{1,17},{17,1},{2,18},{18,2},{3,19},{19,3},{4,20},{20... | collective-permute-start | bytes 1253384 | tf_op jit(solution)/shard_map/ppermute | solution.py:73
  20.8 0.0 collective-permute-done.2.refs_2_
  20.8 0.0 collective-permute-done.3.refs_3_
  20.8 0.0 collective-permute-start.4
  20.8 1.6 %collective-permute-start.9 = (bf16[544,384]{1,0:T(8,128)(2,1)S(1)}, bf16[544,384]{1,0:T(8,128)(2,1)S(1)}, u32[]{:S(2)}, u32[]{:S(2)}) collective-permute-start(bf16[544,384]{1,0:T(8,128)(2,1)S(1)} %collective-permute-done.1.refs_4_), channel_id=1, source_target_pairs={{0,2},{1,3},{2,0},{3,1},{4,6},{5,7},{6,4},{7,5},{8,10},{9,11},{10,... | collective-permute-start | bytes 1253384 | tf_op jit(solution)/shard_map/ppermute | solution.py:65
  22.5 0.0 copy-start
  22.5 0.0 copy-start.1
  22.5 1.3 %collective-permute-start.5 = (bf16[512,256]{1,0:T(8,128)(2,1)S(1)}, bf16[512,256]{1,0:T(8,128)(2,1)S(1)}, u32[]{:S(2)}, u32[]{:S(2)}) collective-permute-start(bf16[512,256]{1,0:T(8,128)(2,1)S(1)} %bitcast.17), channel_id=1, source_target_pairs={{0,4},{1,5},{2,6},{3,7},{4,8},{5,9},{6,10},{7,11},{8,12},{9,13},{1... | collective-permute-start | bytes 786440 | tf_op jit(solution)/shard_map/ppermute | solution.py:65
  23.8 3.1 %collective-permute-done.6.refs_2_ = bf16[544,384]{1,0:T(8,128)(2,1)S(1)} collective-permute-done((bf16[544,384]{1,0:T(8,128)(2,1)S(1)}, bf16[544,384]{1,0:T(8,128)(2,1)S(1)}, u32[]{:S(2)}, u32[]{:S(2)}) %collective-permute-start.6) | collective-permute-done | bytes 417824 | tf_op jit(solution)/shard_map/ppermute | solution.py:65
  26.9 6.7 %collective-permute-done.7.refs_8_ = bf16[544,384]{1,0:T(8,128)(2,1)S(1)} collective-permute-done((bf16[544,384]{1,0:T(8,128)(2,1)S(1)}, bf16[544,384]{1,0:T(8,128)(2,1)S(1)}, u32[]{:S(2)}, u32[]{:S(2)}) %collective-permute-start.7) | collective-permute-done | bytes 417824 | tf_op jit(solution)/shard_map/ppermute | solution.py:65
  33.7 1.5 %collective-permute-start.11 = (bf16[544,384]{1,0:T(8,128)(2,1)S(1)}, bf16[544,384]{1,0:T(8,128)(2,1)S(1)}, u32[]{:S(2)}, u32[]{:S(2)}) collective-permute-start(bf16[544,384]{1,0:T(8,128)(2,1)S(1)} %collective-permute-done.7.refs_8_), channel_id=1, source_target_pairs={{0,16},{16,0},{1,17},{17,1},{2,18},{18,2},{3,19},{19,3},{4,20},{20... | collective-permute-start | bytes 1253384 | tf_op jit(solution)/shard_map/ppermute | solution.py:73
  35.2 1.5 %collective-permute-start.12 = (bf16[544,384]{1,0:T(8,128)(2,1)S(1)}, bf16[544,384]{1,0:T(8,128)(2,1)S(1)}, u32[]{:S(2)}, u32[]{:S(2)}) collective-permute-start(bf16[544,384]{1,0:T(8,128)(2,1)S(1)} %collective-permute-done.7.refs_8_), channel_id=1, source_target_pairs={{0,2},{1,3},{2,0},{3,1},{4,6},{5,7},{6,4},{7,5},{8,10},{9,11},{10,... | collective-permute-start | bytes 1253384 | tf_op jit(solution)/shard_map/ppermute | solution.py:65
  36.7 1.7 %collective-permute-done.5.refs_5_ = bf16[512,256]{1,0:T(8,128)(2,1)S(1)} collective-permute-done((bf16[512,256]{1,0:T(8,128)(2,1)S(1)}, bf16[512,256]{1,0:T(8,128)(2,1)S(1)}, u32[]{:S(2)}, u32[]{:S(2)}) %collective-permute-start.5) | collective-permute-done | bytes 262176 | tf_op jit(solution)/shard_map/ppermute | solution.py:65
  38.4 0.0 collective-permute-start.10
  38.4 4.9 %collective-permute-done.11.refs_10_ = bf16[544,384]{1,0:T(8,128)(2,1)S(1)} collective-permute-done((bf16[544,384]{1,0:T(8,128)(2,1)S(1)}, bf16[544,384]{1,0:T(8,128)(2,1)S(1)}, u32[]{:S(2)}, u32[]{:S(2)}) %collective-permute-start.11) | collective-permute-done | bytes 417824 | tf_op jit(solution)/shard_map/ppermute | solution.py:73
  43.3 0.5 collective-permute-start.15
  43.8 2.5 %collective-permute-start.16 = (bf16[544,384]{1,0:T(8,128)(2,1)S(1)}, bf16[544,384]{1,0:T(8,128)(2,1)S(1)}, u32[]{:S(2)}, u32[]{:S(2)}) collective-permute-start(bf16[544,384]{1,0:T(8,128)(2,1)S(1)} %collective-permute-done.6.refs_2_), channel_id=1, source_target_pairs={{0,16},{16,0},{1,17},{17,1},{2,18},{18,2},{3,19},{19,3},{4,20},{20... | collective-permute-start | bytes 1253384 | tf_op jit(solution)/shard_map/ppermute | solution.py:73
  46.3 6.2 %collective-permute-done.10.refs_6_ = bf16[512,256]{1,0:T(8,128)(2,1)S(1)} collective-permute-done((bf16[512,256]{1,0:T(8,128)(2,1)S(1)}, bf16[512,256]{1,0:T(8,128)(2,1)S(1)}, u32[]{:S(2)}, u32[]{:S(2)}) %collective-permute-start.10) | collective-permute-done | bytes 262176 | tf_op jit(solution)/shard_map/ppermute | solution.py:65
  52.5 0.0 collective-permute-start.13
  52.5 0.0 collective-permute-done.14.refs_0_
  52.5 1.3 %collective-permute-start.19 = (bf16[544,384]{1,0:T(8,128)(2,1)S(1)}, bf16[544,384]{1,0:T(8,128)(2,1)S(1)}, u32[]{:S(2)}, u32[]{:S(2)}) collective-permute-start(bf16[544,384]{1,0:T(8,128)(2,1)S(1)} %collective-permute-done.14.refs_0_), channel_id=1, source_target_pairs={{0,2},{1,3},{2,0},{3,1},{4,6},{5,7},{6,4},{7,5},{8,10},{9,11},{10,... | collective-permute-start | bytes 1253384 | tf_op jit(solution)/shard_map/ppermute | solution.py:65
  53.8 1.5 %collective-permute-start.21 = (bf16[544,384]{1,0:T(8,128)(2,1)S(1)}, bf16[544,384]{1,0:T(8,128)(2,1)S(1)}, u32[]{:S(2)}, u32[]{:S(2)}) collective-permute-start(bf16[544,384]{1,0:T(8,128)(2,1)S(1)} %collective-permute-done.9.refs_5_), channel_id=1, source_target_pairs={{0,16},{16,0},{1,17},{17,1},{2,18},{18,2},{3,19},{19,3},{4,20},{20... | collective-permute-start | bytes 1253384 | tf_op jit(solution)/shard_map/ppermute | solution.py:73
  55.3 0.4 fusion.5
  55.8 4.9 %collective-permute-done.13.refs_7_ = bf16[512,256]{1,0:T(8,128)(2,1)S(1)} collective-permute-done((bf16[512,256]{1,0:T(8,128)(2,1)S(1)}, bf16[512,256]{1,0:T(8,128)(2,1)S(1)}, u32[]{:S(2)}, u32[]{:S(2)}) %collective-permute-start.13) | collective-permute-done | bytes 262176 | tf_op jit(solution)/shard_map/ppermute | solution.py:65
  60.6 0.0 collective-permute-start.25
  60.6 1.3 %attend.1 = (bf16[128,256]{1,0:T(8,128)(2,1)S(1)}, bf16[128,256]{1,0:T(8,128)(2,1)S(1)}, bf16[128,256]{1,0:T(8,128)(2,1)S(1)}, bf16[128,256]{1,0:T(8,128)(2,1)S(1)}) custom-call(bf16[128,384]{1,0:T(8,128)(2,1)S(1)} %get-tuple-element.47.refs_0_, bf16[128,384]{1,0:T(8,128)(2,1)S(1)} %collective-permute-done.4.refs_1_, ...), custom_call_target="tpu_custom_call" | custom-call | tf_op jit(solution)/shard_map/attend/pallas_call | solution.py:159
  61.9 0.0 collective-permute-done.15.refs_11_
  61.9 0.6 collective-permute-start.17
  62.5 1.3 %collective-permute-start.18 = (bf16[128,256]{1,0:T(8,128)(2,1)S(1)}, bf16[128,256]{1,0:T(8,128)(2,1)S(1)}, u32[]{:S(2)}, u32[]{:S(2)}) collective-permute-start(bf16[128,256]{1,0:T(8,128)(2,1)S(1)} %get-tuple-element.66), channel_id=1, source_target_pairs={{0,2},{1,3},{2,0},{3,1},{4,6},{5,7},{6,4},{7,5},{8,10},{9,11},{10,... | collective-permute-start | bytes 196616 | tf_op jit(solution)/shard_map/ppermute | solution.py:65
  63.8 0.2 collective-permute-start.20
  63.9 0.0 collective-permute-done.17.refs_1_
  63.9 1.4 %collective-permute-start.26 = (bf16[544,384]{1,0:T(8,128)(2,1)S(1)}, bf16[544,384]{1,0:T(8,128)(2,1)S(1)}, u32[]{:S(2)}, u32[]{:S(2)}) collective-permute-start(bf16[544,384]{1,0:T(8,128)(2,1)S(1)} %collective-permute-done.14.refs_0_), channel_id=1, source_target_pairs={{0,16},{16,0},{1,17},{17,1},{2,18},{18,2},{3,19},{19,3},{4,20},{20... | collective-permute-start | bytes 1253384 | tf_op jit(solution)/shard_map/ppermute | solution.py:73
  65.3 1.5 %collective-permute-done.18.refs_2_ = bf16[128,256]{1,0:T(8,128)(2,1)S(1)} collective-permute-done((bf16[128,256]{1,0:T(8,128)(2,1)S(1)}, bf16[128,256]{1,0:T(8,128)(2,1)S(1)}, u32[]{:S(2)}, u32[]{:S(2)}) %collective-permute-start.18) | collective-permute-done | bytes 65568 | tf_op jit(solution)/shard_map/ppermute | solution.py:65
  66.8 1.3 %collective-permute-done.20.refs_3_ = bf16[128,256]{1,0:T(8,128)(2,1)S(1)} collective-permute-done((bf16[128,256]{1,0:T(8,128)(2,1)S(1)}, bf16[128,256]{1,0:T(8,128)(2,1)S(1)}, u32[]{:S(2)}, u32[]{:S(2)}) %collective-permute-start.20) | collective-permute-done | bytes 65568 | tf_op jit(solution)/shard_map/ppermute | solution.py:65
  68.1 1.4 %output.1.act.act_own = bf16[128,1536]{1,0:T(8,128)(2,1)S(1)} custom-call(s32[4]{0:T(128)S(1)} %pad_add_fusion.idx, bf16[128,1536]{1,0:T(8,128)(2,1)S(1)} %bitcast.16, bf16[768,1536]{1,0:T(8,128)(2,1)S(1)} %copy-done, bf16[128,256]{1,0:T(8,128)(2,1)S(1)} %get-tuple-element.59.refs_0_, bf16[128,256]{1,0:T(8,128)(2,1)S(1)} %collective-permute-done.17.refs_1_, ...), custom_call_target="tpu_custom_call" | custom-call | tf_op jit(solution)/shard_map/output/pallas_call | solution.py:183
  69.5 0.0 collective-permute-done.21.refs_7_
  69.5 0.2 collective-permute-start.22
  69.7 0.6 give.1
  70.3 0.0 copy-start.2
  70.3 1.3 %collective-permute-start.24 = (bf16[16,2816]{1,0:T(8,128)(2,1)S(1)}, bf16[16,2816]{1,0:T(8,128)(2,1)S(1)}, u32[]{:S(2)}, u32[]{:S(2)}) collective-permute-start(bf16[16,2816]{1,0:T(8,128)(2,1)S(1)} %give.1), channel_id=1, source_target_pairs={{1,3},{2,0},{3,5},{4,2},{5,7},{6,4},{7,9},{8,6},{9,11},{10,8},{11,... | collective-permute-start | bytes 270344 | tf_op jit(solution)/shard_map/ppermute | solution.py:65
  71.6 0.0 collective-permute-done.25.skip_oth
  71.6 0.7 collective-permute-start.23
  72.3 2.5 %early.1 = (bf16[1536,768]{1,0:T(8,128)(2,1)S(1)}, bf16[1280,768]{1,0:T(8,128)(2,1)S(1)}, bf16[1536,768]{1,0:T(8,128)(2,1)S(1)}, f32[512,768]{1,0:T(8,128)S(1)}, bf16[512,320]{1,0:T(8,128)(2,1)S(1)}) custom-call(s32[4]{0:T(128)S(1)} %pad_add_fusion.idx, bf16[256,1280]{1,0:T(8,128)(2,1)S(1)} %bitcast.14, ...), custom_call_target="tpu_custom_call" | custom-call | tf_op jit(solution)/shard_map/early/pallas_call | solution.py:265
  74.8 1.9 %collective-permute-done.24.far_oth = bf16[16,2816]{1,0:T(8,128)(2,1)S(1)} collective-permute-done((bf16[16,2816]{1,0:T(8,128)(2,1)S(1)}, bf16[16,2816]{1,0:T(8,128)(2,1)S(1)}, u32[]{:S(2)}, u32[]{:S(2)}) %collective-permute-start.24) | collective-permute-done | bytes 90144 | tf_op jit(solution)/shard_map/ppermute | solution.py:65
  76.7 0.0 collective-permute-done.23.far
  76.7 2.4 %collective-permute-done.27.refs_3_ = bf16[544,384]{1,0:T(8,128)(2,1)S(1)} collective-permute-done((bf16[544,384]{1,0:T(8,128)(2,1)S(1)}, bf16[544,384]{1,0:T(8,128)(2,1)S(1)}, u32[]{:S(2)}, u32[]{:S(2)}) %collective-permute-start.27) | collective-permute-done | bytes 417824 | tf_op jit(solution)/shard_map/ppermute | solution.py:65
  79.1 3.7 %decode.1 = (bf16[2,128,1536]{2,1,0:T(8,128)(2,1)S(1)}, bf16[256,768]{1,0:T(8,128)(2,1)S(1)}, bf16[1536,768]{1,0:T(8,128)(2,1)S(1)}, bf16[1280,768]{1,0:T(8,128)(2,1)S(1)}, bf16[1536,768]{1,0:T(8,128)(2,1)S(1)}) custom-call(s32[4]{0:T(128)S(1)} %pad_add_fusion.idx, ...), custom_call_target="tpu_custom_call", output_to_operand_aliasing={{2}: (6, {}), {3}: (7, {}), {4}: (8, {})} | custom-call | tf_op jit(solution)/shard_map/decode/pallas_call | solution.py:327
  82.8 0.2 collective-permute-start.28
  83.0 0.8 point_rest.1
  83.8 1.4 %collective-permute-done.28 = bf16[2,128,1536]{2,1,0:T(8,128)(2,1)S(1)} collective-permute-done((bf16[2,128,1536]{2,1,0:T(8,128)(2,1)S(1)}, bf16[2,128,1536]{2,1,0:T(8,128)(2,1)S(1)}, u32[]{:S(2)}, u32[]{:S(2)}) %collective-permute-start.28) | collective-permute-done | bytes 786464 | tf_op jit(solution)/shard_map/ppermute | solution.py:65
  85.2 1.1 %add_convert_fusion = bf16[2,128,1536]{2,1,0:T(8,128)(2,1)} fusion(f32[2,128,1536]{2,1,0:T(8,128)S(1)} %point_rest.1, bf16[2,128,1536]{2,1,0:T(8,128)(2,1)S(1)} %collective-permute-done.28), kind=kLoop, calls=%fused_computation.4 | loop fusion | flops 1179648 | bytes 3145728 | tf_op jit(solution)/shard_map/convert_element_type | solution.py:525
  (22 shorter events, 0.1 us)
Async XLA Ops:
  0.0 7.3 %copy-start.4 = (f32[1536]{0:T(1024)S(1)}, f32[1536]{0:T(1024)}, u32[]{:S(2)}) copy-start(f32[1536]{0:T(1024)} %param.13) | copy-start | bytes 18436
  1.8 1.9 %collective-permute-start = (bf16[272,768]{1,0:T(8,128)(2,1)S(1)}, bf16[272,768]{1,0:T(8,128)(2,1)S(1)}, u32[]{:S(2)}, u32[]{:S(2)}) collective-permute-start(bf16[272,768]{1,0:T(8,128)(2,1)S(1)} %get-tuple-element.45), channel_id=1, source_target_pairs={{0,1},{1,0},{2,3},{3,2},{4,5},{5,4},{6,7},{7,6},{8,9},{9,8},{10,11... | collective-permute-start | bytes 1253384 | tf_op jit(solution)/shard_map/ppermute | solution.py:65
  4.3 15.0 %collective-permute-start.1 = (bf16[544,384]{1,0:T(8,128)(2,1)S(1)}, bf16[544,384]{1,0:T(8,128)(2,1)S(1)}, u32[]{:S(2)}, u32[]{:S(2)}) collective-permute-start(bf16[544,384]{1,0:T(8,128)(2,1)S(1)} %take.1), channel_id=1, source_target_pairs={{0,4},{1,5},{2,6},{3,7},{4,8},{5,9},{6,10},{7,11},{8,12},{9,13},{1... | collective-permute-start | bytes 1253384 | tf_op jit(solution)/shard_map/ppermute | solution.py:65
  11.1 44.2 %copy-start.3 = (bf16[2,128,1280]{2,1,0:T(8,128)(2,1)S(1)}, bf16[2,128,1280]{2,1,0:T(8,128)(2,1)}, u32[]{:S(2)}) copy-start(bf16[2,128,1280]{2,1,0:T(8,128)(2,1)} %param.12) | copy-start | bytes 1966084
  11.1 9.7 %collective-permute-start.2 = (bf16[128,384]{1,0:T(8,128)(2,1)S(1)}, bf16[128,384]{1,0:T(8,128)(2,1)S(1)}, u32[]{:S(2)}, u32[]{:S(2)}) collective-permute-start(bf16[128,384]{1,0:T(8,128)(2,1)S(1)} %get-tuple-element.49), channel_id=1, source_target_pairs={{0,2},{1,3},{2,0},{3,1},{4,6},{5,7},{6,4},{7,5},{8,10},{9,11},{10,... | collective-permute-start | bytes 294920 | tf_op jit(solution)/shard_map/ppermute | solution.py:65
  12.7 8.1 %collective-permute-start.3 = (bf16[128,384]{1,0:T(8,128)(2,1)S(1)}, bf16[128,384]{1,0:T(8,128)(2,1)S(1)}, u32[]{:S(2)}, u32[]{:S(2)}) collective-permute-start(bf16[128,384]{1,0:T(8,128)(2,1)S(1)} %get-tuple-element.50), channel_id=1, source_target_pairs={{0,3},{1,2},{2,1},{3,0},{4,7},{5,6},{6,5},{7,4},{8,11},{9,10},{10,... | collective-permute-start | bytes 294920 | tf_op jit(solution)/shard_map/ppermute | solution.py:65
  12.7 14.3 %collective-permute-start.6 = (bf16[544,384]{1,0:T(8,128)(2,1)S(1)}, bf16[544,384]{1,0:T(8,128)(2,1)S(1)}, u32[]{:S(2)}, u32[]{:S(2)}) collective-permute-start(bf16[544,384]{1,0:T(8,128)(2,1)S(1)} %take.1), channel_id=1, source_target_pairs={{0,2},{1,3},{2,0},{3,1},{4,6},{5,7},{6,4},{7,5},{8,10},{9,11},{10,... | collective-permute-start | bytes 1253384 | tf_op jit(solution)/shard_map/ppermute | solution.py:65
  19.3 14.4 %collective-permute-start.7 = (bf16[544,384]{1,0:T(8,128)(2,1)S(1)}, bf16[544,384]{1,0:T(8,128)(2,1)S(1)}, u32[]{:S(2)}, u32[]{:S(2)}) collective-permute-start(bf16[544,384]{1,0:T(8,128)(2,1)S(1)} %collective-permute-done.1.refs_4_), channel_id=1, source_target_pairs={{0,4},{1,5},{2,6},{3,7},{4,8},{5,9},{6,10},{7,11},{8,12},{9,13},{1... | collective-permute-start | bytes 1253384 | tf_op jit(solution)/shard_map/ppermute | solution.py:65
  19.3 17.4 %collective-permute-start.8 = (bf16[544,384]{1,0:T(8,128)(2,1)S(1)}, bf16[544,384]{1,0:T(8,128)(2,1)S(1)}, u32[]{:S(2)}, u32[]{:S(2)}) collective-permute-start(bf16[544,384]{1,0:T(8,128)(2,1)S(1)} %collective-permute-done.1.refs_4_), channel_id=1, source_target_pairs={{0,16},{16,0},{1,17},{17,1},{2,18},{18,2},{3,19},{19,3},{4,20},{20... | collective-permute-start | bytes 1253384 | tf_op jit(solution)/shard_map/ppermute | solution.py:73
  20.8 1.6 %collective-permute-start.4 = (bf16[128,384]{1,0:T(8,128)(2,1)S(1)}, bf16[128,384]{1,0:T(8,128)(2,1)S(1)}, u32[]{:S(2)}, u32[]{:S(2)}) collective-permute-start(bf16[128,384]{1,0:T(8,128)(2,1)S(1)} %get-tuple-element.51), channel_id=1, source_target_pairs={{0,1},{1,0},{2,3},{3,2},{4,5},{5,4},{6,7},{7,6},{8,9},{9,8},{10,11... | collective-permute-start | bytes 294920 | tf_op jit(solution)/shard_map/ppermute | solution.py:65
  20.8 17.6 %collective-permute-start.9 = (bf16[544,384]{1,0:T(8,128)(2,1)S(1)}, bf16[544,384]{1,0:T(8,128)(2,1)S(1)}, u32[]{:S(2)}, u32[]{:S(2)}) collective-permute-start(bf16[544,384]{1,0:T(8,128)(2,1)S(1)} %collective-permute-done.1.refs_4_), channel_id=1, source_target_pairs={{0,2},{1,3},{2,0},{3,1},{4,6},{5,7},{6,4},{7,5},{8,10},{9,11},{10,... | collective-permute-start | bytes 1253384 | tf_op jit(solution)/shard_map/ppermute | solution.py:65
  22.5 45.6 %copy-start = (bf16[768,1536]{1,0:T(8,128)(2,1)S(1)}, bf16[768,1536]{1,0:T(8,128)(2,1)}, u32[]{:S(2)}) copy-start(bf16[768,1536]{1,0:T(8,128)(2,1)} %wo.1) | copy-start | bytes 7077892
  22.5 45.6 %copy-start.1 = (bf16[2,64,1536]{2,1,0:T(8,128)(2,1)S(1)}, bf16[2,64,1536]{2,1,0:T(8,128)(2,1)}, u32[]{:S(2)}) copy-start(bf16[2,64,1536]{2,1,0:T(8,128)(2,1)} %param.11) | copy-start | bytes 1179652
  22.5 15.9 %collective-permute-start.5 = (bf16[512,256]{1,0:T(8,128)(2,1)S(1)}, bf16[512,256]{1,0:T(8,128)(2,1)S(1)}, u32[]{:S(2)}, u32[]{:S(2)}) collective-permute-start(bf16[512,256]{1,0:T(8,128)(2,1)S(1)} %bitcast.17), channel_id=1, source_target_pairs={{0,4},{1,5},{2,6},{3,7},{4,8},{5,9},{6,10},{7,11},{8,12},{9,13},{1... | collective-permute-start | bytes 786440 | tf_op jit(solution)/shard_map/ppermute | solution.py:65
  33.7 9.6 %collective-permute-start.11 = (bf16[544,384]{1,0:T(8,128)(2,1)S(1)}, bf16[544,384]{1,0:T(8,128)(2,1)S(1)}, u32[]{:S(2)}, u32[]{:S(2)}) collective-permute-start(bf16[544,384]{1,0:T(8,128)(2,1)S(1)} %collective-permute-done.7.refs_8_), channel_id=1, source_target_pairs={{0,16},{16,0},{1,17},{17,1},{2,18},{18,2},{3,19},{19,3},{4,20},{20... | collective-permute-start | bytes 1253384 | tf_op jit(solution)/shard_map/ppermute | solution.py:73
  35.2 17.3 %collective-permute-start.12 = (bf16[544,384]{1,0:T(8,128)(2,1)S(1)}, bf16[544,384]{1,0:T(8,128)(2,1)S(1)}, u32[]{:S(2)}, u32[]{:S(2)}) collective-permute-start(bf16[544,384]{1,0:T(8,128)(2,1)S(1)} %collective-permute-done.7.refs_8_), channel_id=1, source_target_pairs={{0,2},{1,3},{2,0},{3,1},{4,6},{5,7},{6,4},{7,5},{8,10},{9,11},{10,... | collective-permute-start | bytes 1253384 | tf_op jit(solution)/shard_map/ppermute | solution.py:65
  36.7 15.8 %collective-permute-start.14 = (bf16[544,384]{1,0:T(8,128)(2,1)S(1)}, bf16[544,384]{1,0:T(8,128)(2,1)S(1)}, u32[]{:S(2)}, u32[]{:S(2)}) collective-permute-start(bf16[544,384]{1,0:T(8,128)(2,1)S(1)} %collective-permute-done.7.refs_8_), channel_id=1, source_target_pairs={{0,4},{1,5},{2,6},{3,7},{4,8},{5,9},{6,10},{7,11},{8,12},{9,13},{1... | collective-permute-start | bytes 1253384 | tf_op jit(solution)/shard_map/ppermute | solution.py:65
  38.4 14.1 %collective-permute-start.10 = (bf16[512,256]{1,0:T(8,128)(2,1)S(1)}, bf16[512,256]{1,0:T(8,128)(2,1)S(1)}, u32[]{:S(2)}, u32[]{:S(2)}) collective-permute-start(bf16[512,256]{1,0:T(8,128)(2,1)S(1)} %collective-permute-done.5.refs_5_), channel_id=1, source_target_pairs={{0,4},{1,5},{2,6},{3,7},{4,8},{5,9},{6,10},{7,11},{8,12},{9,13},{1... | collective-permute-start | bytes 786440 | tf_op jit(solution)/shard_map/ppermute | solution.py:65
  43.3 18.6 %collective-permute-start.15 = (bf16[544,384]{1,0:T(8,128)(2,1)S(1)}, bf16[544,384]{1,0:T(8,128)(2,1)S(1)}, u32[]{:S(2)}, u32[]{:S(2)}) collective-permute-start(bf16[544,384]{1,0:T(8,128)(2,1)S(1)} %collective-permute-done.11.refs_10_), channel_id=1, source_target_pairs={{0,2},{1,3},{2,0},{3,1},{4,6},{5,7},{6,4},{7,5},{8,10},{9,11},{10,... | collective-permute-start | bytes 1253384 | tf_op jit(solution)/shard_map/ppermute | solution.py:65
  43.8 18.1 %collective-permute-start.16 = (bf16[544,384]{1,0:T(8,128)(2,1)S(1)}, bf16[544,384]{1,0:T(8,128)(2,1)S(1)}, u32[]{:S(2)}, u32[]{:S(2)}) collective-permute-start(bf16[544,384]{1,0:T(8,128)(2,1)S(1)} %collective-permute-done.6.refs_2_), channel_id=1, source_target_pairs={{0,16},{16,0},{1,17},{17,1},{2,18},{18,2},{3,19},{19,3},{4,20},{20... | collective-permute-start | bytes 1253384 | tf_op jit(solution)/shard_map/ppermute | solution.py:73
  52.5 8.2 %collective-permute-start.13 = (bf16[512,256]{1,0:T(8,128)(2,1)S(1)}, bf16[512,256]{1,0:T(8,128)(2,1)S(1)}, u32[]{:S(2)}, u32[]{:S(2)}) collective-permute-start(bf16[512,256]{1,0:T(8,128)(2,1)S(1)} %collective-permute-done.10.refs_6_), channel_id=1, source_target_pairs={{0,4},{1,5},{2,6},{3,7},{4,8},{5,9},{6,10},{7,11},{8,12},{9,13},{1... | collective-permute-start | bytes 786440 | tf_op jit(solution)/shard_map/ppermute | solution.py:65
  52.5 11.3 %collective-permute-start.19 = (bf16[544,384]{1,0:T(8,128)(2,1)S(1)}, bf16[544,384]{1,0:T(8,128)(2,1)S(1)}, u32[]{:S(2)}, u32[]{:S(2)}) collective-permute-start(bf16[544,384]{1,0:T(8,128)(2,1)S(1)} %collective-permute-done.14.refs_0_), channel_id=1, source_target_pairs={{0,2},{1,3},{2,0},{3,1},{4,6},{5,7},{6,4},{7,5},{8,10},{9,11},{10,... | collective-permute-start | bytes 1253384 | tf_op jit(solution)/shard_map/ppermute | solution.py:65
  53.8 15.7 %collective-permute-start.21 = (bf16[544,384]{1,0:T(8,128)(2,1)S(1)}, bf16[544,384]{1,0:T(8,128)(2,1)S(1)}, u32[]{:S(2)}, u32[]{:S(2)}) collective-permute-start(bf16[544,384]{1,0:T(8,128)(2,1)S(1)} %collective-permute-done.9.refs_5_), channel_id=1, source_target_pairs={{0,16},{16,0},{1,17},{17,1},{2,18},{18,2},{3,19},{19,3},{4,20},{20... | collective-permute-start | bytes 1253384 | tf_op jit(solution)/shard_map/ppermute | solution.py:73
  60.6 11.0 %collective-permute-start.25 = (bf16[256,1280]{1,0:T(8,128)(2,1)S(1)}, bf16[256,1280]{1,0:T(8,128)(2,1)S(1)}, u32[]{:S(2)}, u32[]{:S(2)}) collective-permute-start(bf16[256,1280]{1,0:T(8,128)(2,1)S(1)} %bitcast.12), channel_id=1, source_target_pairs={{0,1},{1,0},{2,3},{3,2},{4,5},{5,4},{6,7},{7,6},{8,9},{9,8},{10,11... | collective-permute-start | bytes 1966088 | tf_op jit(solution)/shard_map/ppermute | solution.py:65
  61.9 2.0 %collective-permute-start.17 = (bf16[128,256]{1,0:T(8,128)(2,1)S(1)}, bf16[128,256]{1,0:T(8,128)(2,1)S(1)}, u32[]{:S(2)}, u32[]{:S(2)}) collective-permute-start(bf16[128,256]{1,0:T(8,128)(2,1)S(1)} %get-tuple-element.64), channel_id=1, source_target_pairs={{0,1},{1,0},{2,3},{3,2},{4,5},{5,4},{6,7},{7,6},{8,9},{9,8},{10,11... | collective-permute-start | bytes 196616 | tf_op jit(solution)/shard_map/ppermute | solution.py:65
  62.5 4.3 %collective-permute-start.18 = (bf16[128,256]{1,0:T(8,128)(2,1)S(1)}, bf16[128,256]{1,0:T(8,128)(2,1)S(1)}, u32[]{:S(2)}, u32[]{:S(2)}) collective-permute-start(bf16[128,256]{1,0:T(8,128)(2,1)S(1)} %get-tuple-element.66), channel_id=1, source_target_pairs={{0,2},{1,3},{2,0},{3,1},{4,6},{5,7},{6,4},{7,5},{8,10},{9,11},{10,... | collective-permute-start | bytes 196616 | tf_op jit(solution)/shard_map/ppermute | solution.py:65
  63.8 4.3 %collective-permute-start.20 = (bf16[128,256]{1,0:T(8,128)(2,1)S(1)}, bf16[128,256]{1,0:T(8,128)(2,1)S(1)}, u32[]{:S(2)}, u32[]{:S(2)}) collective-permute-start(bf16[128,256]{1,0:T(8,128)(2,1)S(1)} %get-tuple-element.69), channel_id=1, source_target_pairs={{0,3},{1,2},{2,1},{3,0},{4,7},{5,6},{6,5},{7,4},{8,11},{9,10},{10,... | collective-permute-start | bytes 196616 | tf_op jit(solution)/shard_map/ppermute | solution.py:65
  63.9 12.8 %collective-permute-start.26 = (bf16[544,384]{1,0:T(8,128)(2,1)S(1)}, bf16[544,384]{1,0:T(8,128)(2,1)S(1)}, u32[]{:S(2)}, u32[]{:S(2)}) collective-permute-start(bf16[544,384]{1,0:T(8,128)(2,1)S(1)} %collective-permute-done.14.refs_0_), channel_id=1, source_target_pairs={{0,16},{16,0},{1,17},{17,1},{2,18},{18,2},{3,19},{19,3},{4,20},{20... | collective-permute-start | bytes 1253384 | tf_op jit(solution)/shard_map/ppermute | solution.py:73
  66.8 12.3 %collective-permute-start.27 = (bf16[544,384]{1,0:T(8,128)(2,1)S(1)}, bf16[544,384]{1,0:T(8,128)(2,1)S(1)}, u32[]{:S(2)}, u32[]{:S(2)}) collective-permute-start(bf16[544,384]{1,0:T(8,128)(2,1)S(1)} %collective-permute-done.15.refs_11_), channel_id=1, source_target_pairs={{0,4},{1,5},{2,6},{3,7},{4,8},{5,9},{6,10},{7,11},{8,12},{9,13},{1... | collective-permute-start | bytes 1253384 | tf_op jit(solution)/shard_map/ppermute | solution.py:65
  69.5 9.6 %collective-permute-start.22 = (bf16[128,1536]{1,0:T(8,128)(2,1)S(1)}, bf16[128,1536]{1,0:T(8,128)(2,1)S(1)}, u32[]{:S(2)}, u32[]{:S(2)}) collective-permute-start(bf16[128,1536]{1,0:T(8,128)(2,1)S(1)} %output.1.act.act_own), channel_id=1, source_target_pairs={{0,1},{1,0},{2,3},{3,2},{4,5},{5,4},{6,7},{7,6},{8,9},{9,8},{10,11... | collective-permute-start | bytes 1179656 | tf_op jit(solution)/shard_map/ppermute | solution.py:65
  70.3 8.9 %copy-start.2 = (f32[3,1536]{1,0:T(4,128)S(1)}, f32[3,1536]{1,0:T(4,128)}, u32[]{:S(2)}) copy-start(f32[3,1536]{1,0:T(4,128)} %depth.1) | copy-start | bytes 55300
  70.3 6.4 %collective-permute-start.24 = (bf16[16,2816]{1,0:T(8,128)(2,1)S(1)}, bf16[16,2816]{1,0:T(8,128)(2,1)S(1)}, u32[]{:S(2)}, u32[]{:S(2)}) collective-permute-start(bf16[16,2816]{1,0:T(8,128)(2,1)S(1)} %give.1), channel_id=1, source_target_pairs={{1,3},{2,0},{3,5},{4,2},{5,7},{6,4},{7,9},{8,6},{9,11},{10,8},{11,... | collective-permute-start | bytes 270344 | tf_op jit(solution)/shard_map/ppermute | solution.py:65
  71.6 5.1 %collective-permute-start.23 = (bf16[16,2816]{1,0:T(8,128)(2,1)S(1)}, bf16[16,2816]{1,0:T(8,128)(2,1)S(1)}, u32[]{:S(2)}, u32[]{:S(2)}) collective-permute-start(bf16[16,2816]{1,0:T(8,128)(2,1)S(1)} %give.1), channel_id=1, source_target_pairs={{1,2},{2,1},{3,4},{4,3},{5,6},{6,5},{7,8},{8,7},{9,10},{10,9},{11,... | collective-permute-start | bytes 270344 | tf_op jit(solution)/shard_map/ppermute | solution.py:65
  82.8 2.4 %collective-permute-start.28 = (bf16[2,128,1536]{2,1,0:T(8,128)(2,1)S(1)}, bf16[2,128,1536]{2,1,0:T(8,128)(2,1)S(1)}, u32[]{:S(2)}, u32[]{:S(2)}) collective-permute-start(bf16[2,128,1536]{2,1,0:T(8,128)(2,1)S(1)} %get-tuple-element.82), channel_id=1, source_target_pairs={{0,1},{1,0},{2,3},{3,2},{4,5},{5,4},{6,7},{7,6},{8,9},{9,8},{10,11... | collective-permute-start | bytes 2359304 | tf_op jit(solution)/shard_map/ppermute | solution.py:65
